TPU v7x, 32 devices: a whole 2x2x4 slice. The times are simulated.
32 devices in a mesh: seq: 4 (over x, core), ctx: 8 (over z, y).
Axes of the slice: x: 2, y: 2, z: 4, core: 2. Of those that a mesh axis runs over, the one named last changes fastest.
Arguments:
- hidden_in: bfloat16 [4, 1024, 2048], P('seq', 'ctx'), may hold values from -6 to 6
- positions: int32 [4, 1024], P('seq', 'ctx'), may hold values from 0 to 1023, as said below
- attn_gain: bfloat16 [2048], P(('seq', 'ctx')), may hold values from 0.25 to 1.75
- w_query: bfloat16 [2048, 2048], P(('seq', 'ctx')), may hold values from -0.125 to 0.125
- w_key: bfloat16 [2048, 2048], P(('seq', 'ctx')), may hold values from -0.125 to 0.125
- w_value: bfloat16 [2048, 2048], P(('seq', 'ctx')), may hold values from -0.125 to 0.125
- w_out: bfloat16 [2048, 2048], P(('seq', 'ctx')), may hold values from -0.75 to 0.75
- mlp_gain: bfloat16 [2048], P(('seq', 'ctx')), may hold values from 0.25 to 1.75
- w_gate: bfloat16 [2048, 8192], P(('seq', 'ctx')), may hold values from -0.125 to 0.125
- w_up: bfloat16 [2048, 8192], P(('seq', 'ctx')), may hold values from -0.125 to 0.125
- w_down: bfloat16 [8192, 2048], P(('seq', 'ctx')), may hold values from -0.0625 to 0.0625
- out_grad: bfloat16 [4, 1024, 2048], P('seq', 'ctx'), may hold values from -6 to 6
Outputs:
- hidden_out: bfloat16 [4, 1024, 2048], P('seq', 'ctx')
- hidden_grad: float32 [4, 1024, 2048], P('seq', 'ctx')
- attn_gain_grad: float32 [2048], P(('seq', 'ctx'))
- w_query_grad: float32 [2048, 2048], P(('seq', 'ctx'))
- w_key_grad: float32 [2048, 2048], P(('seq', 'ctx'))
- w_value_grad: float32 [2048, 2048], P(('seq', 'ctx'))
- w_out_grad: float32 [2048, 2048], P(('seq', 'ctx'))
- mlp_gain_grad: float32 [2048], P(('seq', 'ctx'))
- w_gate_grad: float32 [2048, 8192], P(('seq', 'ctx'))
- w_up_grad: float32 [2048, 8192], P(('seq', 'ctx'))
- w_down_grad: float32 [8192, 2048], P(('seq', 'ctx'))
Inputs may be any that keep to these rules, and one draw needn't show every extreme that they name: In each sequence the positions are a permutation of 0 to 1023 made of 16 runs of 64 stored tokens, each run holding consecutive positions in increasing order; the order of the runs is drawn from the seed.
All inputs are finite; a program needn't handle non-finite values.
Results may differ from a plain program's by a relative error of at most 0.02.
Values may be sent and summed in bfloat16 or wider, within the bound.
No kernel may reach another device: no remote copies, remote signals or barrier semaphores. Data moves between devices by JAX's collectives and lax.ppermute only.
A program may use at most 704 MiB of HBM per device.

v0:
```python
import math

import jax
import jax.numpy as jnp
from jax import lax
from jax.sharding import PartitionSpec as P

HEADS = 32
HEAD_DIM = 64


eps = 1e-05
rope_base = 130000.0
mask_fill = -1e30


def passed_along(block, axis, distance):
    devices = range(lax.axis_size(axis))
    route = [((i - distance) % len(devices), i) for i in devices]
    return lax.ppermute(block, axis, route)


def rms_scale(values):
    return lax.rsqrt(jnp.mean(values * values, axis=-1, keepdims=True) + eps)


def angle_table(positions):
    exponents = jnp.arange(HEAD_DIM // 2, dtype=jnp.float32) * (2.0 / HEAD_DIM)
    inverse = jnp.exp(-math.log(rope_base) * exponents)
    return positions.astype(jnp.float32)[:, None, None] * inverse[None, None, :]


def rotate(values, angles, direction):
    half_dim = values.shape[-1] // 2
    first_half = values[..., :half_dim]
    second_half = values[..., half_dim:]
    cosine = jnp.cos(angles)
    sine_part = jnp.sin(angles) * direction
    return jnp.concatenate(
        [
            first_half * cosine - second_half * sine_part,
            second_half * cosine + first_half * sine_part,
        ],
        axis=-1,
    )


def split_heads(values):
    return values.reshape(values.shape[0], HEADS, HEAD_DIM)


def flatten_heads(values):
    return values.reshape(values.shape[0], HEADS * HEAD_DIM)


def block_length(row_count):
    block_rows = row_count
    while block_rows > 1024 and block_rows % 2 == 0:
        block_rows = block_rows // 2
    return block_rows


def split_blocks(members, block_rows):
    return tuple(
        (
            member.reshape((member.shape[0] // block_rows, block_rows) + member.shape[1:])
            for member in members
        )
    )


def contract_rows(left, right):
    return lax.dot_general(
        left, right, (((0,), (0,)), ((), ())), preferred_element_type=jnp.float32
    )


def contract_cols(left, right):
    return lax.dot_general(
        left, right, (((1,), (1,)), ((), ())), preferred_element_type=jnp.float32
    )


def masked_scores(query_heads, query_pos, key_heads, key_pos):
    head_scale = 1.0 / math.sqrt(HEAD_DIM)
    scores = (
        jnp.einsum("qhd,khd->hqk", query_heads, key_heads, preferred_element_type=jnp.float32)
        * head_scale
    )
    allowed = key_pos[None, None, :] <= query_pos[None, :, None]
    return (jnp.where(allowed, scores, mask_fill), allowed)


def score_grads(
    query_heads, query_pos, grad_heads, log_total, row_delta, key_heads, value_heads, key_pos
):
    scores, allowed = masked_scores(query_heads, query_pos, key_heads, key_pos)
    probabilities = jnp.where(allowed, jnp.exp(scores - jnp.transpose(log_total)[:, :, None]), 0.0)
    prob_grad = jnp.einsum(
        "qhd,khd->hqk", grad_heads, value_heads, preferred_element_type=jnp.float32
    )
    score_grad = (probabilities * (prob_grad - jnp.transpose(row_delta)[:, :, None])).astype(
        jnp.bfloat16
    )
    return (probabilities.astype(jnp.bfloat16), score_grad)


def local(
    hidden_in,
    positions,
    attn_gain,
    w_query,
    w_key,
    w_value,
    w_out,
    mlp_gain,
    w_gate,
    w_up,
    w_down,
    out_grad,
):
    hidden = hidden_in[0].astype(jnp.float32)
    token_pos = positions[0]
    row_count = hidden.shape[0]
    model_width = hidden.shape[1]
    head_scale = 1.0 / math.sqrt(HEAD_DIM)
    attn_set = (
        lax.all_gather(w_query, ("seq", "ctx"), axis=0, tiled=True),
        lax.all_gather(w_key, ("seq", "ctx"), axis=0, tiled=True),
        lax.all_gather(w_value, ("seq", "ctx"), axis=0, tiled=True),
        lax.all_gather(w_out, ("seq", "ctx"), axis=0, tiled=True),
        lax.all_gather(attn_gain, ("seq", "ctx"), axis=0, tiled=True),
    )
    full_query, full_key, full_value, full_out, full_gain = attn_set
    attn_scale = rms_scale(hidden)
    attn_unit = hidden * attn_scale
    normed = (attn_unit * full_gain.astype(jnp.float32)).astype(jnp.bfloat16)
    angles = angle_table(token_pos)
    query_heads = rotate(
        split_heads(jnp.dot(normed, full_query, preferred_element_type=jnp.float32)), angles, 1.0
    ).astype(jnp.bfloat16)
    key_heads = rotate(
        split_heads(jnp.dot(normed, full_key, preferred_element_type=jnp.float32)), angles, 1.0
    ).astype(jnp.bfloat16)
    value_rows = jnp.dot(normed, full_value, preferred_element_type=jnp.float32).astype(
        jnp.bfloat16
    )
    key_rows = flatten_heads(key_heads)
    start_state = (
        jnp.full((HEADS, row_count), mask_fill, jnp.float32),
        jnp.zeros((HEADS, row_count), jnp.float32),
        jnp.zeros((row_count, model_width), jnp.float32),
    )
    key_piece = lax.all_gather(key_rows, "ctx", axis=0, tiled=True)
    value_piece = lax.all_gather(value_rows, "ctx", axis=0, tiled=True)
    pos_piece = lax.all_gather(token_pos, "ctx", axis=0, tiled=True)
    block_rows = block_length(key_piece.shape[0])

    def one_block(state_now, block_members):
        run_max, run_total, run_acc = state_now
        key_block, value_block, key_pos = block_members
        scores, allowed = masked_scores(query_heads, token_pos, split_heads(key_block), key_pos)
        new_max = jnp.maximum(run_max, jnp.max(scores, axis=-1))
        weights = jnp.where(allowed, jnp.exp(scores - new_max[:, :, None]), 0.0)
        factor = jnp.exp(run_max - new_max)
        run_total = run_total * factor + jnp.sum(weights, axis=-1)
        update = jnp.einsum(
            "hqk,khd->qhd",
            weights.astype(jnp.bfloat16),
            split_heads(value_block),
            preferred_element_type=jnp.float32,
        )
        run_acc = flatten_heads(split_heads(run_acc) * jnp.transpose(factor)[:, :, None] + update)
        return ((new_max, run_total, run_acc), None)

    run_max, run_total, run_acc = lax.scan(
        one_block, start_state, split_blocks((key_piece, value_piece, pos_piece), block_rows)
    )[0]
    attended = split_heads(run_acc) / jnp.transpose(run_total)[:, :, None]
    log_total = jnp.transpose(run_max + jnp.log(run_total))
    attended_low = flatten_heads(attended).astype(jnp.bfloat16)
    middle = hidden + jnp.dot(attended_low, full_out, preferred_element_type=jnp.float32)
    mlp_set = (
        lax.all_gather(w_gate, ("seq", "ctx"), axis=0, tiled=True),
        lax.all_gather(w_up, ("seq", "ctx"), axis=0, tiled=True),
        lax.all_gather(w_down, ("seq", "ctx"), axis=0, tiled=True),
        lax.all_gather(mlp_gain, ("seq", "ctx"), axis=0, tiled=True),
    )
    full_gate, full_up, full_down, full_mlp_gain = mlp_set
    mlp_scale = rms_scale(middle)
    mlp_unit = middle * mlp_scale
    normed_mid = (mlp_unit * full_mlp_gain.astype(jnp.float32)).astype(jnp.bfloat16)
    gate_act = jnp.dot(normed_mid, full_gate, preferred_element_type=jnp.float32)
    up_act = jnp.dot(normed_mid, full_up, preferred_element_type=jnp.float32)
    inner_act = (jax.nn.silu(gate_act) * up_act).astype(jnp.bfloat16)
    result = middle + jnp.dot(inner_act, full_down, preferred_element_type=jnp.float32)
    hidden_out = result.astype(jnp.bfloat16)[None]
    back_attn = (
        lax.all_gather(w_query, ("seq", "ctx"), axis=0, tiled=True),
        lax.all_gather(w_key, ("seq", "ctx"), axis=0, tiled=True),
        lax.all_gather(w_value, ("seq", "ctx"), axis=0, tiled=True),
        lax.all_gather(w_out, ("seq", "ctx"), axis=0, tiled=True),
        lax.all_gather(attn_gain, ("seq", "ctx"), axis=0, tiled=True),
    )
    back_mlp = (
        lax.all_gather(w_gate, ("seq", "ctx"), axis=0, tiled=True),
        lax.all_gather(w_up, ("seq", "ctx"), axis=0, tiled=True),
        lax.all_gather(w_down, ("seq", "ctx"), axis=0, tiled=True),
        lax.all_gather(mlp_gain, ("seq", "ctx"), axis=0, tiled=True),
    )
    back_query, back_key, back_value, back_out, back_gain = back_attn
    back_gate, back_up, back_down, back_mlp_gain = back_mlp
    grad_low = out_grad[0]
    grad_out = grad_low.astype(jnp.float32)
    inner_grad = contract_cols(grad_low, back_down)
    sigmoid_gate = jax.nn.sigmoid(gate_act)
    gate_grad = (
        inner_grad * up_act * sigmoid_gate * (1.0 + gate_act * (1.0 - sigmoid_gate))
    ).astype(jnp.bfloat16)
    up_grad = (inner_grad * gate_act * sigmoid_gate).astype(jnp.bfloat16)
    columns = normed_mid
    gate_up_sum = lax.psum_scatter(
        jnp.concatenate(
            [contract_rows(columns, gate_grad), contract_rows(columns, up_grad)], axis=1
        ),
        ("seq", "ctx"),
        scatter_dimension=0,
        tiled=True,
    )
    hidden_units = w_gate.shape[1]
    w_gate_grad = gate_up_sum[:, :hidden_units]
    w_up_grad = gate_up_sum[:, hidden_units:]
    columns = inner_act
    w_down_grad = lax.psum_scatter(
        contract_rows(columns, grad_low), ("seq", "ctx"), scatter_dimension=0, tiled=True
    )
    mid_grad_in = contract_cols(gate_grad, back_gate) + contract_cols(up_grad, back_up)
    mid_gain_term = mid_grad_in * back_mlp_gain.astype(jnp.float32)
    middle_grad = grad_out + mlp_scale * (
        mid_gain_term - mlp_unit * jnp.mean(mlp_unit * mid_gain_term, axis=-1, keepdims=True)
    )
    mlp_gain_part = jnp.sum(mid_grad_in * mlp_unit, axis=0)
    middle_low = middle_grad.astype(jnp.bfloat16)
    attended_grad = contract_cols(middle_low, back_out).astype(jnp.bfloat16)
    grad_heads = split_heads(attended_grad)
    row_delta = jnp.sum(grad_heads.astype(jnp.float32) * attended, axis=-1)
    zero_rows = jnp.zeros((row_count, model_width), jnp.float32)

    def pass_turn(turn_index, pass_state):
        key_block, value_block, key_pos, key_acc, value_acc, query_acc = pass_state
        prob_low, score_grad = score_grads(
            query_heads,
            token_pos,
            grad_heads,
            log_total,
            row_delta,
            split_heads(key_block),
            split_heads(value_block),
            key_pos,
        )
        query_acc = query_acc + flatten_heads(
            jnp.einsum(
                "hqk,khd->qhd",
                score_grad,
                split_heads(key_block),
                preferred_element_type=jnp.float32,
            )
            * head_scale
        )
        key_acc = key_acc + flatten_heads(
            jnp.einsum("hqk,qhd->khd", score_grad, query_heads, preferred_element_type=jnp.float32)
            * head_scale
        )
        value_acc = value_acc + flatten_heads(
            jnp.einsum("hqk,qhd->khd", prob_low, grad_heads, preferred_element_type=jnp.float32)
        )
        key_block, value_block, key_pos = passed_along((key_block, value_block, key_pos), "ctx", 1)
        key_acc, value_acc = (
            passed_along(key_acc.astype(jnp.bfloat16), "ctx", 1).astype(key_acc.dtype),
            passed_along(value_acc.astype(jnp.bfloat16), "ctx", 1).astype(value_acc.dtype),
        )
        return (key_block, value_block, key_pos, key_acc, value_acc, query_acc)

    final_state = lax.fori_loop(
        0,
        lax.axis_size("ctx"),
        pass_turn,
        (key_rows, value_rows, token_pos, zero_rows, zero_rows, zero_rows),
    )
    key_acc = final_state[3]
    value_acc = final_state[4]
    query_acc = final_state[5]
    query_grad = flatten_heads(rotate(split_heads(query_acc), angles, -1.0)).astype(jnp.bfloat16)
    key_grad = flatten_heads(rotate(split_heads(key_acc), angles, -1.0)).astype(jnp.bfloat16)
    value_grad = value_acc.astype(jnp.bfloat16)
    normed_grad = (
        contract_cols(query_grad, back_query)
        + contract_cols(key_grad, back_key)
        + contract_cols(value_grad, back_value)
    )
    attn_gain_term = normed_grad * back_gain.astype(jnp.float32)
    hidden_grad = middle_grad + attn_scale * (
        attn_gain_term - attn_unit * jnp.mean(attn_unit * attn_gain_term, axis=-1, keepdims=True)
    )
    attn_gain_part = jnp.sum(normed_grad * attn_unit, axis=0)
    grad_sums = (
        lax.psum_scatter(
            contract_rows(normed, query_grad), ("seq", "ctx"), scatter_dimension=0, tiled=True
        ),
        lax.psum_scatter(
            contract_rows(normed, key_grad), ("seq", "ctx"), scatter_dimension=0, tiled=True
        ),
        lax.psum_scatter(
            contract_rows(normed, value_grad), ("seq", "ctx"), scatter_dimension=0, tiled=True
        ),
        lax.psum_scatter(
            contract_rows(attended_low, middle_low), ("seq", "ctx"), scatter_dimension=0, tiled=True
        ),
        lax.psum_scatter(attn_gain_part, ("seq", "ctx"), scatter_dimension=0, tiled=True),
        lax.psum_scatter(mlp_gain_part, ("seq", "ctx"), scatter_dimension=0, tiled=True),
    )
    return (
        hidden_out,
        hidden_grad[None],
        grad_sums[4],
        grad_sums[0],
        grad_sums[1],
        grad_sums[2],
        grad_sums[3],
        grad_sums[5],
        w_gate_grad,
        w_up_grad,
        w_down_grad,
    )


def solution(mesh):
    return jax.shard_map(
        local,
        mesh=mesh,
        in_specs=(
            P("seq", "ctx", None),
            P("seq", "ctx"),
            P(("seq", "ctx")),
            P(("seq", "ctx"), None),
            P(("seq", "ctx"), None),
            P(("seq", "ctx"), None),
            P(("seq", "ctx"), None),
            P(("seq", "ctx")),
            P(("seq", "ctx"), None),
            P(("seq", "ctx"), None),
            P(("seq", "ctx"), None),
            P("seq", "ctx", None),
        ),
        out_specs=(
            P("seq", "ctx", None),
            P("seq", "ctx", None),
            P(("seq", "ctx")),
            P(("seq", "ctx"), None),
            P(("seq", "ctx"), None),
            P(("seq", "ctx"), None),
            P(("seq", "ctx"), None),
            P(("seq", "ctx")),
            P(("seq", "ctx"), None),
            P(("seq", "ctx"), None),
            P(("seq", "ctx"), None),
        ),
        check_vma=False,
    )
```

profile of v0, /device:TPU:0, one launch (start us, length us, event | category | flops | bytes accessed | tf_op | source)
XLA Modules:
  0.0 6308.0 jit_solution(5481369506368127535)
XLA Ops:
  11.2 43.3 all-reduce.6
  97.9 72.5 %all-gather.11.cloned.1.call-done = bf16[2048,2048]{1,0:T(8,128)(2,1)} async-done(((bf16[64,2048]{1,0:T(8,128)(2,1)}), bf16[2048,2048]{1,0:T(8,128)(2,1)}) %all-gather.11.cloned.1.call-update) | async-done | bytes 8388624 | tf_op jit(solution)/shard_map/all_gather | solution.py:128
  182.7 66.7 %all-gather.13.cloned.1.call-done = bf16[2048,2048]{1,0:T(8,128)(2,1)} async-done(((bf16[64,2048]{1,0:T(8,128)(2,1)}), bf16[2048,2048]{1,0:T(8,128)(2,1)}) %all-gather.13.cloned.1.call-update) | async-done | bytes 8388624 | tf_op jit(solution)/shard_map/all_gather | solution.py:129
  330.4 68.8 %all-gather.15.cloned.1.call-done = bf16[1024,2048]{0,1:T(8,128)(2,1)} async-done(((bf16[128,2048]{0,1:T(8,128)(2,1)}), bf16[1024,2048]{0,1:T(8,128)(2,1)}) %all-gather.15.cloned.1.call-update) | async-done | bytes 4194320 | tf_op jit(solution)/shard_map/all_gather | solution.py:154
  421.3 56.3 all-gather.21.cloned.1.call-done
  483.5 190.5 %all-gather.23.cloned.1.call-done = bf16[2048,8192]{1,0:T(8,128)(2,1)} async-done(((bf16[64,8192]{1,0:T(8,128)(2,1)}), bf16[2048,8192]{1,0:T(8,128)(2,1)}) %all-gather.23.cloned.1.call-update) | async-done | bytes 33554448 | tf_op jit(solution)/shard_map/all_gather | solution.py:184
  691.8 178.2 %all-gather.25.cloned.1.call-done = bf16[2048,8192]{1,0:T(8,128)(2,1)} async-done(((bf16[64,8192]{1,0:T(8,128)(2,1)}), bf16[2048,8192]{1,0:T(8,128)(2,1)}) %all-gather.25.cloned.1.call-update) | async-done | bytes 33554448 | tf_op jit(solution)/shard_map/all_gather | solution.py:185
  887.8 178.2 %all-gather.27.cloned.1.call-done = bf16[8192,2048]{1,0:T(8,128)(2,1)} async-done(((bf16[256,2048]{1,0:T(8,128)(2,1)}), bf16[8192,2048]{1,0:T(8,128)(2,1)}) %all-gather.27.cloned.1.call-update) | async-done | bytes 33554448 | tf_op jit(solution)/shard_map/all_gather | solution.py:186
  1132.3 86.9 %pad_maximum_fusion = f32[2048,16384]{1,0:T(8,128)} fusion(f32[2048,8192]{1,0:T(8,128)} %fusion.73, f32[2048,8192]{1,0:T(8,128)} %fusion.72), kind=kLoop, calls=%fused_computation.12 | loop fusion | flops 33554432 | bytes 268435456 | tf_op jit(solution)/shard_map/concatenate | solution.py:223
  1269.6 780.5 %while.6 = (s32[]{:T(128)}, bf16[128,2048]{0,1:T(8,128)(2,1)}, bf16[128,2048]{0,1:T(8,128)(2,1)}, s32[128]{0:T(128)S(1)}, f32[128,2048]{0,1:T(8,128)}, /*index=5...) while((s32[]{:T(128)}, bf16[128,2048]{0,1:T(8,128)(2,1)}, ...), condition=%wide.region_7.8_spmd.clone, body=%wide.region_6.7_spmd.clone.sunk | while | flops 342900736 | bytes 38343000 | solution.py:284
  1293.9 51.6 collective-permute-done.3
  1392.5 52.2 collective-permute-done.3
  1489.6 54.1 collective-permute-done.3
  1586.8 55.7 collective-permute-done.3
  1685.2 54.9 collective-permute-done.3
  1782.5 54.6 collective-permute-done.3
  1879.0 54.4 collective-permute-done.3
  1974.9 54.4 collective-permute-done.3
  2198.9 1257.0 %all-reduce.9.cloned.1.call-done = f32[2048,16384]{1,0:T(8,128)} async-done(((f32[2048,16384]{1,0:T(8,128)}), f32[2048,16384]{1,0:T(8,128)}) %all-reduce.9.cloned.1.call-update) | async-done | bytes 134217744
  3460.8 355.4 %reduce-scatter.6.cloned.1.call-done = f32[64,2048]{1,0:T(8,128)} async-done(((f32[2048,2048]{1,0:T(8,128)}), f32[64,2048]{1,0:T(8,128)}) %reduce-scatter.6.cloned.1.call-update) | async-done | bytes 524304 | tf_op jit(solution)/shard_map/reduce_scatter | solution.py:307
  3816.3 360.1 %reduce-scatter.8.cloned.1.call-done = f32[64,2048]{1,0:T(8,128)} async-done(((f32[2048,2048]{1,0:T(8,128)}), f32[64,2048]{1,0:T(8,128)}) %reduce-scatter.8.cloned.1.call-update) | async-done | bytes 524304 | tf_op jit(solution)/shard_map/reduce_scatter | solution.py:310
  4176.3 360.2 %reduce-scatter.10.cloned.1.call-done = f32[64,2048]{1,0:T(8,128)} async-done(((f32[2048,2048]{1,0:T(8,128)}), f32[64,2048]{1,0:T(8,128)}) %reduce-scatter.10.cloned.1.call-update) | async-done | bytes 524304 | tf_op jit(solution)/shard_map/reduce_scatter | solution.py:313
  4536.6 360.1 %reduce-scatter.12.cloned.1.call-done = f32[64,2048]{1,0:T(8,128)} async-done(((f32[2048,2048]{1,0:T(8,128)}), f32[64,2048]{1,0:T(8,128)}) %reduce-scatter.12.cloned.1.call-update) | async-done | bytes 524304 | tf_op jit(solution)/shard_map/reduce_scatter | solution.py:316
  4896.6 1404.6 %reduce-scatter.14.cloned.1.call-done = f32[256,2048]{1,0:T(8,128)} async-done(((f32[8192,2048]{1,0:T(8,128)}), f32[256,2048]{1,0:T(8,128)}) %reduce-scatter.14.cloned.1.call-update) | async-done | bytes 2097168 | tf_op jit(solution)/shard_map/reduce_scatter | solution.py:234
  (362 shorter events, 821.7 us)
Async XLA Ops:
  7.9 162.5 %all-gather.11.cloned.1.call-start = ((), (), s32[]{:S(2)}) async-start(), calls=%async_computation.5 | async-start | bytes 8650752 | tf_op jit(solution)/shard_map/all_gather | solution.py:128
  8.7 240.7 %all-gather.13.cloned.1.call-start = ((), (), s32[]{:S(2)}) async-start(), calls=%async_computation.6 | async-start | bytes 8650752 | tf_op jit(solution)/shard_map/all_gather | solution.py:129
  9.4 314.6 %all-gather.19.cloned.1.call-start = ((), (), s32[]{:S(2)}) async-start(), calls=%async_computation.9 | async-start | bytes 4718592 | tf_op jit(solution)/shard_map/all_gather | solution.py:155
  97.0 302.1 %all-gather.15.cloned.1.call-start = ((), (), s32[]{:S(2)}) async-start(), calls=%async_computation.7 | async-start | bytes 4718592 | tf_op jit(solution)/shard_map/all_gather | solution.py:154
  271.6 206.0 %all-gather.21.cloned.1.call-start = ((), (), s32[]{:S(2)}) async-start(), calls=%async_computation.10 | async-start | bytes 8650752 | tf_op jit(solution)/shard_map/all_gather | solution.py:131
  272.2 401.9 %all-gather.23.cloned.1.call-start = ((), (), s32[]{:S(2)}) async-start(), calls=%async_computation.11 | async-start | bytes 34603008 | tf_op jit(solution)/shard_map/all_gather | solution.py:184
  272.9 597.1 %all-gather.25.cloned.1.call-start = ((), (), s32[]{:S(2)}) async-start(), calls=%async_computation.12 | async-start | bytes 34603008 | tf_op jit(solution)/shard_map/all_gather | solution.py:185
  273.7 792.3 %all-gather.27.cloned.1.call-start = ((), (), s32[]{:S(2)}) async-start(), calls=%async_computation.13 | async-start | bytes 34603008 | tf_op jit(solution)/shard_map/all_gather | solution.py:186
  274.4 3181.5 %all-reduce.9.cloned.1.call-start = ((), (), s32[]{:S(2)}) async-start(), calls=%async_computation.19 | async-start | bytes 268435456
  1219.2 2597.0 %reduce-scatter.6.cloned.1.call-start = ((), (), s32[]{:S(2)}) async-start(), calls=%async_computation.14 | async-start | bytes 17301504 | tf_op jit(solution)/shard_map/reduce_scatter | solution.py:307
  1271.6 97.2 %collective-permute-start = (bf16[128,2048]{0,1:T(8,128)(2,1)}, bf16[128,2048]{0,1:T(8,128)(2,1)}, u32[]{:S(2)}, u32[]{:S(2)}) collective-permute-start(bf16[128,2048]{0,1:T(8,128)(2,1)} %copy.48), channel_id=1, source_target_pairs={{7,0},{0,1},{1,2},{2,3},{3,4},{4,5},{5,6},{6,7},{15,8},{8,9},{9,10... | collective-permute-start | bytes 1572872 | tf_op jit(solution)/shard_map/while/body/eval_jaxpr/ppermute | solution.py:20
  1370.7 96.9 %collective-permute-start = (bf16[128,2048]{0,1:T(8,128)(2,1)}, bf16[128,2048]{0,1:T(8,128)(2,1)}, u32[]{:S(2)}, u32[]{:S(2)}) collective-permute-start(bf16[128,2048]{0,1:T(8,128)(2,1)} %copy.48), channel_id=1, source_target_pairs={{7,0},{0,1},{1,2},{2,3},{3,4},{4,5},{5,6},{6,7},{15,8},{8,9},{9,10... | collective-permute-start | bytes 1572872 | tf_op jit(solution)/shard_map/while/body/eval_jaxpr/ppermute | solution.py:20
  1372.6 95.0 %collective-permute-start.1 = (bf16[128,2048]{0,1:T(8,128)(2,1)}, bf16[128,2048]{0,1:T(8,128)(2,1)}, u32[]{:S(2)}, u32[]{:S(2)}) collective-permute-start(bf16[128,2048]{0,1:T(8,128)(2,1)} %copy.49), channel_id=1, source_target_pairs={{7,0},{0,1},{1,2},{2,3},{3,4},{4,5},{5,6},{6,7},{15,8},{8,9},{9,10... | collective-permute-start | bytes 1572872 | tf_op jit(solution)/shard_map/while/body/eval_jaxpr/ppermute | solution.py:20
  1372.6 95.0 %collective-permute-start.2 = (s32[128]{0:T(128)S(1)}, s32[128]{0:T(128)S(1)}, u32[]{:S(2)}, u32[]{:S(2)}) collective-permute-start(s32[128]{0:T(128)S(1)} %copy.50), channel_id=1, source_target_pairs={{7,0},{0,1},{1,2},{2,3},{3,4},{4,5},{5,6},{6,7},{15,8},{8,9},{9,10... | collective-permute-start | bytes 1544 | tf_op jit(solution)/shard_map/while/body/eval_jaxpr/ppermute | solution.py:20
  1469.5 96.8 %collective-permute-start = (bf16[128,2048]{0,1:T(8,128)(2,1)}, bf16[128,2048]{0,1:T(8,128)(2,1)}, u32[]{:S(2)}, u32[]{:S(2)}) collective-permute-start(bf16[128,2048]{0,1:T(8,128)(2,1)} %copy.48), channel_id=1, source_target_pairs={{7,0},{0,1},{1,2},{2,3},{3,4},{4,5},{5,6},{6,7},{15,8},{8,9},{9,10... | collective-permute-start | bytes 1572872 | tf_op jit(solution)/shard_map/while/body/eval_jaxpr/ppermute | solution.py:20
  1471.4 95.0 %collective-permute-start.1 = (bf16[128,2048]{0,1:T(8,128)(2,1)}, bf16[128,2048]{0,1:T(8,128)(2,1)}, u32[]{:S(2)}, u32[]{:S(2)}) collective-permute-start(bf16[128,2048]{0,1:T(8,128)(2,1)} %copy.49), channel_id=1, source_target_pairs={{7,0},{0,1},{1,2},{2,3},{3,4},{4,5},{5,6},{6,7},{15,8},{8,9},{9,10... | collective-permute-start | bytes 1572872 | tf_op jit(solution)/shard_map/while/body/eval_jaxpr/ppermute | solution.py:20
  1471.4 95.0 %collective-permute-start.2 = (s32[128]{0:T(128)S(1)}, s32[128]{0:T(128)S(1)}, u32[]{:S(2)}, u32[]{:S(2)}) collective-permute-start(s32[128]{0:T(128)S(1)} %copy.50), channel_id=1, source_target_pairs={{7,0},{0,1},{1,2},{2,3},{3,4},{4,5},{5,6},{6,7},{15,8},{8,9},{9,10... | collective-permute-start | bytes 1544 | tf_op jit(solution)/shard_map/while/body/eval_jaxpr/ppermute | solution.py:20
  1568.2 96.5 %collective-permute-start = (bf16[128,2048]{0,1:T(8,128)(2,1)}, bf16[128,2048]{0,1:T(8,128)(2,1)}, u32[]{:S(2)}, u32[]{:S(2)}) collective-permute-start(bf16[128,2048]{0,1:T(8,128)(2,1)} %copy.48), channel_id=1, source_target_pairs={{7,0},{0,1},{1,2},{2,3},{3,4},{4,5},{5,6},{6,7},{15,8},{8,9},{9,10... | collective-permute-start | bytes 1572872 | tf_op jit(solution)/shard_map/while/body/eval_jaxpr/ppermute | solution.py:20
  1570.2 94.6 %collective-permute-start.1 = (bf16[128,2048]{0,1:T(8,128)(2,1)}, bf16[128,2048]{0,1:T(8,128)(2,1)}, u32[]{:S(2)}, u32[]{:S(2)}) collective-permute-start(bf16[128,2048]{0,1:T(8,128)(2,1)} %copy.49), channel_id=1, source_target_pairs={{7,0},{0,1},{1,2},{2,3},{3,4},{4,5},{5,6},{6,7},{15,8},{8,9},{9,10... | collective-permute-start | bytes 1572872 | tf_op jit(solution)/shard_map/while/body/eval_jaxpr/ppermute | solution.py:20
  1666.7 95.5 %collective-permute-start = (bf16[128,2048]{0,1:T(8,128)(2,1)}, bf16[128,2048]{0,1:T(8,128)(2,1)}, u32[]{:S(2)}, u32[]{:S(2)}) collective-permute-start(bf16[128,2048]{0,1:T(8,128)(2,1)} %copy.48), channel_id=1, source_target_pairs={{7,0},{0,1},{1,2},{2,3},{3,4},{4,5},{5,6},{6,7},{15,8},{8,9},{9,10... | collective-permute-start | bytes 1572872 | tf_op jit(solution)/shard_map/while/body/eval_jaxpr/ppermute | solution.py:20
  2063.0 2113.4 %reduce-scatter.8.cloned.1.call-start = ((), (), s32[]{:S(2)}) async-start(), calls=%async_computation.15 | async-start | bytes 17301504 | tf_op jit(solution)/shard_map/reduce_scatter | solution.py:310
  2072.2 2464.4 %reduce-scatter.10.cloned.1.call-start = ((), (), s32[]{:S(2)}) async-start(), calls=%async_computation.16 | async-start | bytes 17301504 | tf_op jit(solution)/shard_map/reduce_scatter | solution.py:313
  2081.8 2814.8 %reduce-scatter.12.cloned.1.call-start = ((), (), s32[]{:S(2)}) async-start(), calls=%async_computation.17 | async-start | bytes 17301504 | tf_op jit(solution)/shard_map/reduce_scatter | solution.py:316
  2092.5 4208.7 %reduce-scatter.14.cloned.1.call-start = ((), (), s32[]{:S(2)}) async-start(), calls=%async_computation.18 | async-start | bytes 69206016 | tf_op jit(solution)/shard_map/reduce_scatter | solution.py:234
  (71 other events, 7653.5 us)
Sparse Core Ops, SparseCore 0:
  11.0 80.3 all-gather.16
  94.3 75.9 all-gather.10
  173.3 75.9 all-gather.12
  251.9 71.9 all-gather.18
  325.9 73.2 all-gather.14
  402.0 75.5 all-gather.20
  480.6 193.3 all-gather.22
  677.0 192.9 all-gather.24
  873.0 192.9 all-gather.26
  1219.4 2236.5 all-reduce.8
  3458.8 357.4 reduce-scatter.5
  3819.0 357.2 reduce-scatter.7
  4179.2 357.3 reduce-scatter.9
  4539.3 357.3 reduce-scatter.11
  4899.4 1401.7 reduce-scatter.13
where the time goes:
time: 6320 us; the launch traced here: 6310 us
  waiting for transfers between devices  5560 us (88%)
  matrix products  356 us (6%)
  other arithmetic  180 us (3%)
  blocking collectives  102 us (2%)
  local copies, waits for them, and re-layouts  80.4 us (1%)
    reduce_scatter x1, waiting for transfers between devices, local(): lax.psum_scatter(contract_rows(columns, grad_low), ('seq', 'ctx'), scatte...  1400 us
    unnamed x16, waiting for transfers between devices  1260 us
    ppermute x40, waiting for transfers between devices, passed_along(): return lax.ppermute(block, axis, route)  583 us
    reduce_scatter x1, waiting for transfers between devices, local(): lax.psum_scatter(contract_rows(normed, value_grad), ('seq', 'ctx'), scatt...  360 us
    reduce_scatter x1, waiting for transfers between devices, local(): lax.psum_scatter(contract_rows(attended_low, middle_low), ('seq', 'ctx'),...  360 us
    reduce_scatter x1, waiting for transfers between devices, local(): lax.psum_scatter(contract_rows(normed, key_grad), ('seq', 'ctx'), scatter...  360 us
    reduce_scatter x1, waiting for transfers between devices, local(): lax.psum_scatter(contract_rows(normed, query_grad), ('seq', 'ctx'), scatt...  355 us
    all_gather x1, waiting for transfers between devices, local(): lax.all_gather(w_gate, ('seq', 'ctx'), axis=0, tiled=True)  191 us
  transfers between devices with their start and end apart: 55, of which 31 were waited for; matrix products, arithmetic and copies ran while one was open for 7% of the time, Pallas kernels for 0%

commit v1 on v0

v1 whole, which is shorter than its diff:
```python
import math

import jax
import jax.numpy as jnp
from jax import lax
from jax.sharding import PartitionSpec as P

HEADS = 32
HEAD_DIM = 64

eps = 1e-05
rope_base = 130000.0
mask_fill = -1e30
bf16 = jnp.bfloat16
f32 = jnp.float32


def gather_ctx(block):
    return lax.all_gather(block, "ctx", axis=0, tiled=True)


def gather_seq(block):
    return lax.all_gather(block, "seq", axis=0, tiled=True)


def scatter_ctx(total):
    return lax.psum_scatter(total.astype(bf16), "ctx", scatter_dimension=0, tiled=True).astype(f32)


def scatter_seq(total):
    return lax.psum_scatter(total.astype(bf16), "seq", scatter_dimension=0, tiled=True)


def swap_ctx(blocks):
    return lax.all_to_all(blocks, "ctx", 0, 0, tiled=True)


def rms_scale(values):
    return lax.rsqrt(jnp.mean(values * values, axis=-1, keepdims=True) + eps)


def angle_table(positions):
    exponents = jnp.arange(HEAD_DIM // 2, dtype=f32) * (2.0 / HEAD_DIM)
    inverse = jnp.exp(-math.log(rope_base) * exponents)
    return positions.astype(f32)[:, None, None] * inverse[None, None, :]


def rotate(values, cosine, sine_part):
    half_dim = HEAD_DIM // 2
    heads = values.reshape(values.shape[0], -1, HEAD_DIM)
    first_half = heads[..., :half_dim]
    second_half = heads[..., half_dim:]
    return jnp.concatenate(
        [
            first_half * cosine - second_half * sine_part,
            second_half * cosine + first_half * sine_part,
        ],
        axis=-1,
    ).reshape(values.shape)


def dot(left, right):
    return jnp.dot(left, right, preferred_element_type=f32)


def dot_rows(left, right):
    return lax.dot_general(left, right, (((0,), (0,)), ((), ())), preferred_element_type=f32)


def dot_cols(left, right):
    return lax.dot_general(left, right, (((1,), (1,)), ((), ())), preferred_element_type=f32)


def columns_to_owners(weight, groups):
    n = lax.axis_size("ctx")
    rows = weight.shape[0]
    width = weight.shape[1] // (n * groups)
    blocks = weight.reshape(rows, groups, n, width).transpose(2, 0, 1, 3)
    mine = swap_ctx(blocks.reshape(n, rows, groups * width))
    return gather_seq(mine.reshape(n * rows, groups * width))


def columns_from_owners(total, groups):
    n = lax.axis_size("ctx")
    part = scatter_seq(total)
    rows = part.shape[0] // n
    width = part.shape[1] // groups
    back = swap_ctx(part.reshape(n, rows, groups * width))
    back = back.reshape(n, rows, groups, width).transpose(1, 2, 0, 3)
    return back.reshape(rows, groups * n * width)


def attention(query, key, value, positions):
    heads = query.shape[1] // HEAD_DIM
    scale = 1.0 / math.sqrt(HEAD_DIM)
    allowed = positions[None, None, :] <= positions[None, :, None]
    qh, kh, vh = (m.reshape(-1, heads, HEAD_DIM) for m in (query, key, value))
    scores = jnp.einsum("qhd,khd->hqk", qh, kh, preferred_element_type=f32) * scale
    scores = jnp.where(allowed, scores, mask_fill)
    row_max = jnp.max(scores, axis=-1)
    weights = jnp.exp(scores - row_max[:, :, None])
    row_total = jnp.sum(weights, axis=-1)
    mixed = jnp.einsum("hqk,khd->qhd", weights.astype(bf16), vh, preferred_element_type=f32)
    attended = mixed / row_total.T[:, :, None]
    return attended.reshape(query.shape), row_max + jnp.log(row_total)


def attention_back(query, key, value, positions, attended, lse, grad):
    heads = query.shape[1] // HEAD_DIM
    scale = 1.0 / math.sqrt(HEAD_DIM)
    allowed = positions[None, None, :] <= positions[None, :, None]
    qh, kh, vh, gh = (m.reshape(-1, heads, HEAD_DIM) for m in (query, key, value, grad))
    row_delta = jnp.sum(gh.astype(f32) * attended.reshape(-1, heads, HEAD_DIM), axis=-1)
    scores = jnp.einsum("qhd,khd->hqk", qh, kh, preferred_element_type=f32) * scale
    prob = jnp.where(allowed, jnp.exp(scores - lse[:, :, None]), 0.0)
    prob_grad = jnp.einsum("qhd,khd->hqk", gh, vh, preferred_element_type=f32)
    score_grad = (prob * (prob_grad - row_delta.T[:, :, None])).astype(bf16)
    prob_low = prob.astype(bf16)
    value_acc = jnp.einsum("hqk,qhd->khd", prob_low, gh, preferred_element_type=f32)
    query_acc = jnp.einsum("hqk,khd->qhd", score_grad, kh, preferred_element_type=f32) * scale
    key_acc = jnp.einsum("hqk,qhd->khd", score_grad, qh, preferred_element_type=f32) * scale
    return tuple(m.reshape(query.shape) for m in (query_acc, key_acc, value_acc))


def local(
    hidden_in,
    positions,
    attn_gain,
    w_query,
    w_key,
    w_value,
    w_out,
    mlp_gain,
    w_gate,
    w_up,
    w_down,
    out_grad,
):
    n = lax.axis_size("ctx")
    seqs = lax.axis_size("seq")
    here = lax.axis_index("ctx")
    rows = hidden_in.shape[1]

    def own_rows(whole):
        return lax.dynamic_slice_in_dim(whole, here * rows, rows, 0)

    qkv_sub = columns_to_owners(jnp.concatenate([w_query, w_key, w_value], axis=1), 3)
    x_low = gather_ctx(hidden_in[0])
    pos_all = gather_ctx(positions[0])
    gains = lax.all_gather(jnp.stack([attn_gain, mlp_gain]), ("seq", "ctx"), axis=1, tiled=True)
    full_out = lax.all_gather(w_out, ("seq", "ctx"), axis=0, tiled=True)
    gate_up = columns_to_owners(jnp.concatenate([w_gate, w_up], axis=1), 2 * seqs)
    down_sub = gather_seq(w_down)
    grad_all = gather_ctx(out_grad[0])

    x = x_low.astype(f32)
    attn_scale = rms_scale(x)
    gain1 = gains[0].astype(f32)
    gain2 = gains[1].astype(f32)
    normed = (x * attn_scale * gain1).astype(bf16)
    angles = angle_table(pos_all)
    cosine, sine = jnp.cos(angles), jnp.sin(angles)
    qkv = dot(normed, qkv_sub)
    width = qkv.shape[1] // 3
    query = rotate(qkv[:, :width], cosine, sine).astype(bf16)
    key = rotate(qkv[:, width : 2 * width], cosine, sine).astype(bf16)
    value = qkv[:, 2 * width :].astype(bf16)
    attended, lse = attention(query, key, value, pos_all)
    att_low = lax.all_gather(attended.astype(bf16), "ctx", axis=1, tiled=True)

    middle = x + dot(att_low, full_out)
    mlp_scale = rms_scale(middle)
    normed_mid = (middle * mlp_scale * gain2).astype(bf16)
    gate_up_act = dot(normed_mid, gate_up)
    units = gate_up.shape[1] // 2
    gate_act, up_act = gate_up_act[:, :units], gate_up_act[:, units:]
    sig = jax.nn.sigmoid(gate_act)
    inner = (gate_act * sig * up_act).astype(bf16)
    middle_own = own_rows(middle)
    hidden_out = (middle_own + scatter_ctx(dot(inner, down_sub))).astype(bf16)

    inner_grad = dot_cols(grad_all, down_sub)
    gate_grad = (inner_grad * up_act * sig * (1.0 + gate_act * (1.0 - sig))).astype(bf16)
    up_grad = (inner_grad * gate_act * sig).astype(bf16)
    gate_up_grad = jnp.concatenate([gate_grad, up_grad], axis=1)
    mid_grad_in = scatter_ctx(dot_cols(gate_up_grad, gate_up))
    w_gate_up_grad = columns_from_owners(dot_rows(normed_mid, gate_up_grad), 2 * seqs).astype(f32)
    hidden_units = w_gate.shape[1]
    w_down_grad = scatter_seq(dot_rows(inner, grad_all)).astype(f32)

    mid_scale = own_rows(mlp_scale)
    mid_unit = middle_own * mid_scale
    mid_term = mid_grad_in * gain2
    middle_grad = out_grad[0].astype(f32) + mid_scale * (
        mid_term - mid_unit * jnp.mean(mid_unit * mid_term, axis=-1, keepdims=True)
    )
    mlp_gain_part = jnp.sum(mid_grad_in * mid_unit, axis=0)
    middle_low = middle_grad.astype(bf16)
    att_grad = dot_cols(middle_low, full_out).astype(bf16)
    att_grad = swap_ctx(att_grad.reshape(rows, n, -1).transpose(1, 0, 2)).reshape(n * rows, -1)
    middle_low_all = gather_ctx(middle_low)
    out_rows = w_out.shape[0]
    att_cols = att_low.reshape(n * rows, seqs, n, out_rows)
    att_sub = lax.dynamic_slice_in_dim(att_cols, here, 1, 2).reshape(n * rows, seqs * out_rows)
    w_out_grad = scatter_seq(dot_rows(att_sub, middle_low_all)).astype(f32)

    query_acc, key_acc, value_acc = attention_back(
        query, key, value, pos_all, attended, lse, att_grad
    )
    qkv_grad = jnp.concatenate(
        [rotate(query_acc, cosine, -sine), rotate(key_acc, cosine, -sine), value_acc], axis=1
    ).astype(bf16)
    normed_grad = scatter_ctx(dot_cols(qkv_grad, qkv_sub))
    own_scale = own_rows(attn_scale)
    own_unit = hidden_in[0].astype(f32) * own_scale
    attn_term = normed_grad * gain1
    hidden_grad = middle_grad + own_scale * (
        attn_term - own_unit * jnp.mean(own_unit * attn_term, axis=-1, keepdims=True)
    )
    attn_gain_part = jnp.sum(normed_grad * own_unit, axis=0)
    w_qkv_grad = columns_from_owners(dot_rows(normed, qkv_grad), 3).astype(f32)
    model_width = x.shape[1]
    gain_grads = lax.psum_scatter(
        jnp.stack([attn_gain_part, mlp_gain_part], axis=1),
        ("seq", "ctx"),
        scatter_dimension=0,
        tiled=True,
    )
    return (
        hidden_out[None],
        hidden_grad[None],
        gain_grads[:, 0],
        w_qkv_grad[:, :model_width],
        w_qkv_grad[:, model_width : 2 * model_width],
        w_qkv_grad[:, 2 * model_width :],
        w_out_grad,
        gain_grads[:, 1],
        w_gate_up_grad[:, :hidden_units],
        w_gate_up_grad[:, hidden_units:],
        w_down_grad,
    )


def solution(mesh):
    tokens = P("seq", "ctx", None)
    whole = P(("seq", "ctx"), None)
    gain = P(("seq", "ctx"))
    return jax.shard_map(
        local,
        mesh=mesh,
        in_specs=(
            tokens,
            P("seq", "ctx"),
            gain,
            whole,
            whole,
            whole,
            whole,
            gain,
            whole,
            whole,
            whole,
            tokens,
        ),
        out_specs=(tokens, tokens, gain, whole, whole, whole, whole, gain, whole, whole, whole),
        check_vma=False,
    )
```

time: 6320 us -> 1340 us (0.21)
  waiting for transfers between devices: 5560 us -> 866 us
  matrix products: 356 us -> 150 us
  other arithmetic: 180 us -> 25.9 us
  blocking collectives: 102 us -> 222 us
    reduce_scatter x5 -> x7, waiting for transfers between devices: 2840 us -> 421 us  [the longest x3 293 us: scatter_ctx(): lax.psum_scatter(total.astype(bf16), 'ctx', scatter_dimension=0, tiled=True)]
    unnamed x16 -> x17, waiting for transfers between devices: 1260 us -> 137 us
    all_gather x9 -> x8, waiting for transfers between devices: 877 us -> 293 us  [the longest x3 148 us: gather_ctx(): return lax.all_gather(block, 'ctx', axis=0, tiled=True)]
    ppermute x40 -> x0, waiting for transfers between devices: 583 us -> none  [passed_along(): return lax.ppermute(block, axis, route)]
    dot_general x63 -> x18, matrix products: 356 us -> 150 us  [the longest x4 46.7 us: dot(): return jnp.dot(left, right, preferred_element_type=f32)]
    all_to_all x0 -> x2, blocking collectives: none -> 139 us  [swap_ctx(): return lax.all_to_all(blocks, 'ctx', 0, 0, tiled=True)]
    concatenate x1 -> x2, other arithmetic: 86.9 us -> 1.3 us  [the longest x1 1.16 us: local(): jnp.concatenate([w_query, w_key, w_value], axis=1)]
    unnamed x2 -> x0, blocking collectives: 82.5 us -> none
  transfers between devices with their start and end apart: 55 -> 19, of which waited for: 31 -> 14; matrix products, arithmetic and copies ran while one was open for 7% -> 8% of each run, Pallas kernels for 0% -> 0%
where the time goes in v1:
time: 1340 us; the launch traced here: 1330 us
  waiting for transfers between devices  866 us (65%)
  blocking collectives  222 us (17%)
  matrix products  150 us (11%)
  local copies, waits for them, and re-layouts  33.7 us (3%)
  other arithmetic  25.9 us (2%)
  starting transfers between devices  15.1 us (1%)
  between operations  15.1 us (1%)
    reduce_scatter x3, waiting for transfers between devices, scatter_ctx(): lax.psum_scatter(total.astype(bf16), 'ctx', scatter_dimension=0, tiled=True)  293 us
    all_gather x3, waiting for transfers between devices, gather_ctx(): return lax.all_gather(block, 'ctx', axis=0, tiled=True)  148 us
    all_to_all x2, blocking collectives, swap_ctx(): return lax.all_to_all(blocks, 'ctx', 0, 0, tiled=True)  139 us
    unnamed x17, waiting for transfers between devices  137 us
    reduce_scatter x4, waiting for transfers between devices, scatter_seq(): lax.psum_scatter(total.astype(bf16), 'seq', scatter_dimension=0, tiled=True)  128 us
    all_gather x1, waiting for transfers between devices, local(): full_out = lax.all_gather(w_out, ('seq', 'ctx'), axis=0, tiled=True)  78.3 us
    all_gather x1, blocking collectives, local(): lax.all_gather(jnp.stack([attn_gain, mlp_gain]), ('seq', 'ctx'), axis=1,...  63.2 us
    all_gather x3, waiting for transfers between devices, gather_seq(): return lax.all_gather(block, 'seq', axis=0, tiled=True)  62.4 us
  transfers between devices with their start and end apart: 19, of which 14 were waited for; matrix products, arithmetic and copies ran while one was open for 8% of the time, Pallas kernels for 0%

profile of v1, /device:TPU:0, one launch (start us, length us, event | category | flops | bytes accessed | tf_op | source)
XLA Modules:
  0.0 1327.3 jit_solution(11851029687330130680)
XLA Ops:
  10.7 43.3 %all_to_all.25 = bf16[8,64,768]{2,1,0:T(8,128)(2,1)} all-to-all(bf16[8,64,768]{2,1,0:T(8,128)(2,1)S(1)} %reshape.275), channel_id=1, replica_groups=mesh['seq'=4,'ctx'=8] {'ctx'}, dimensions={0} | all-to-all | bytes 1572864 | tf_op jit(solution)/shard_map/all_to_all | solution.py:35
  54.1 18.9 %all-gather.1 = s32[1,1024]{1,0:T(1,128)S(1)} all-gather(s32[1,128]{1,0:T(1,128)S(1)} %copy-done.30), channel_id=3, replica_groups=mesh['seq'=4,'ctx'=8] {'ctx'}, dimensions={1}, use_global_device_ids=true | all-gather | bytes 4608 | tf_op jit(solution)/shard_map/all_gather | solution.py:19
  73.0 63.2 %all-gather.3 = bf16[32,64,2]{1,2,0:T(2,128)(2,1)S(1)} all-gather(bf16[1,64,2]{1,2,0:T(2,128)(2,1)S(1)} %maximum_bitcast_fusion), channel_id=1, replica_groups=mesh['seq'=4,'ctx'=8] {'seq','ctx'}, dimensions={0}, use_global_device_ids=true | all-gather | bytes 8448 | tf_op jit(solution)/shard_map/all_gather | solution.py:150
  167.7 96.2 %all_to_all.26 = bf16[8,64,2048]{2,1,0:T(8,128)(2,1)} all-to-all(bf16[8,64,2048]{2,1,0:T(8,128)(2,1)} %reshape.281), channel_id=1, replica_groups=mesh['seq'=4,'ctx'=8] {'ctx'}, dimensions={0} | all-to-all | bytes 4194304 | tf_op jit(solution)/shard_map/all_to_all | solution.py:35
  269.7 78.3 %all-gather.17.cloned.1.call-done = bf16[2048,2048]{1,0:T(8,128)(2,1)} async-done(((bf16[64,2048]{1,0:T(8,128)(2,1)}), bf16[2048,2048]{1,0:T(8,128)(2,1)}) %all-gather.17.cloned.1.call-update) | async-done | bytes 8388624 | tf_op jit(solution)/shard_map/all_gather | solution.py:151
  348.0 15.7 %multiply_reduce_fusion = (f32[1024]{0:T(1024)S(1)}, f32[1024,2048]{1,0:T(8,128)}) fusion(bf16[1024,2048]{0,1:T(8,128)(2,1)} %all-gather.15.cloned.1.call-done, bf16[2048,2048]{1,0:T(8,128)(2,1)} %all-gather.17.cloned.1.call-done, bf16[1,1024,2048]{2,1,0:T(8,128)(2,1)} %all-gather.25.cloned.1.call-done), kind=kOutput, calls=%fused_computation.14 | convolution fusion | flops 8598322176 | bytes 25169920 | tf_op jit(solution)/shard_map/dot_general | solution.py:63
  363.7 42.6 %all-gather.19.cloned.1.call-done = bf16[2048,2048]{1,0:T(8,128)(2,1)} async-done(((bf16[512,2048]{1,0:T(8,128)(2,1)}), bf16[2048,2048]{1,0:T(8,128)(2,1)}) %all-gather.19.cloned.1.call-update) | async-done | bytes 8388624 | tf_op jit(solution)/shard_map/all_gather | solution.py:23
  406.3 16.2 %fusion.62 = f32[1024,2048]{1,0:T(8,128)} fusion(bf16[2048,2048]{1,0:T(8,128)(2,1)} %all-gather.19.cloned.1.call-done, f32[1024,2048]{1,0:T(8,128)} %get-tuple-element.51, f32[2048]{0:T(1024)S(1)} %bitcast.153, f32[1024]{0:T(1024)S(1)} %add_rsqrt_fusion), kind=kOutput, calls=%fused_computation.113 | convolution fusion | flops 8596226048 | bytes 25178112 | tf_op jit(solution)/shard_map/dot_general | solution.py:63
  422.5 19.8 %all-gather.21.cloned.1.call-done = bf16[1024,2048]{1,0:T(8,128)(2,1)} async-done(((bf16[256,2048]{1,0:T(8,128)(2,1)}), bf16[1024,2048]{1,0:T(8,128)(2,1)}) %all-gather.21.cloned.1.call-update) | async-done | bytes 4194320 | tf_op jit(solution)/shard_map/all_gather | solution.py:23
  442.2 75.6 %all-gather.27.cloned.1.call-done = bf16[1,1024,2048]{2,1,0:T(8,128)(2,1)} async-done(((bf16[1,128,2048]{2,1,0:T(8,128)(2,1)}), bf16[1,1024,2048]{2,1,0:T(8,128)(2,1)}) %all-gather.27.cloned.1.call-update) | async-done | bytes 4194320 | tf_op jit(solution)/shard_map/all_gather | solution.py:19
  517.8 13.2 multiply_convert_fusion.3
  533.0 12.7 convolution_convert_fusion.1
  545.8 86.2 %reduce-scatter.13.cloned.1.call-done = bf16[128,2048]{1,0:T(8,128)(2,1)} async-done(((bf16[1024,2048]{1,0:T(8,128)(2,1)}), bf16[128,2048]{1,0:T(8,128)(2,1)}) %reduce-scatter.13.cloned.1.call-update) | async-done | bytes 524304 | tf_op jit(solution)/shard_map/reduce_scatter | solution.py:27
  648.3 14.4 %all-to-all-done.2 = bf16[8,128,256]{1,2,0:T(8,128)(2,1)S(1)} async-done(((bf16[8,128,256]{1,2,0:T(8,128)(2,1)}), bf16[8,128,256]{1,2,0:T(8,128)(2,1)S(1)}, u32[]{:S(2)}, u32[]{:S(2)}) %all-to-all-start.2) | async-done | bytes 524320 | tf_op jit(solution)/shard_map/all_to_all | solution.py:35
  672.6 9.4 multiply_convert_fusion
  694.3 15.3 %convolution_convert_fusion = bf16[2048,2048]{1,0:T(8,128)(2,1)} fusion(bf16[1024,1024]{1,0:T(8,128)(2,1)} %copy-done.38, bf16[1024,1024]{1,0:T(8,128)(2,1)S(1)} %copy-done.37, f32[1024,2048]{1,0:T(8,128)} %get-tuple-element.51, f32[2048]{0:T(1024)S(1)} %bitcast.156, f32[1024]{0:T(1024)S(1)} %add_rsqrt_fusion), kind=kOutput, calls=%fused_computation.19 | convolution fusion | flops 8608808960 | bytes 20983808 | tf_op jit(solution)/shard_map/dot_general | solution.py:67
  719.6 8.3 fusion.16
  740.0 65.3 %reduce-scatter.21.cloned.1.call-done = bf16[512,2048]{1,0:T(8,128)(2,1)} async-done(((bf16[2048,2048]{1,0:T(8,128)(2,1)}), bf16[512,2048]{1,0:T(8,128)(2,1)}) %reduce-scatter.21.cloned.1.call-update) | async-done | bytes 2097168 | tf_op jit(solution)/shard_map/reduce_scatter | solution.py:31
  813.1 123.5 %reduce-scatter.15.cloned.1.call-done = bf16[128,2048]{1,0:T(8,128)(2,1)} async-done(((bf16[1024,2048]{1,0:T(8,128)(2,1)}), bf16[128,2048]{1,0:T(8,128)(2,1)}) %reduce-scatter.15.cloned.1.call-update) | async-done | bytes 524304 | tf_op jit(solution)/shard_map/reduce_scatter | solution.py:27
  939.6 72.8 %all-gather.23.cloned.1.call-done = bf16[1024,2048]{1,0:T(8,128)(2,1)} async-done(((bf16[128,2048]{1,0:T(8,128)(2,1)}), bf16[1024,2048]{1,0:T(8,128)(2,1)}) %all-gather.23.cloned.1.call-update) | async-done | bytes 4194320 | tf_op jit(solution)/shard_map/all_gather | solution.py:19
  1017.0 40.7 %reduce-scatter.23.cloned.1.call-done = bf16[256,2048]{1,0:T(8,128)(2,1)} async-done(((bf16[1024,2048]{1,0:T(8,128)(2,1)}), bf16[256,2048]{1,0:T(8,128)(2,1)}) %reduce-scatter.23.cloned.1.call-update) | async-done | bytes 1048592 | tf_op jit(solution)/shard_map/reduce_scatter | solution.py:31
  1066.6 83.0 %reduce-scatter.11.cloned.1.call-done = bf16[128,2048]{1,0:T(8,128)(2,1)} async-done(((bf16[1024,2048]{1,0:T(8,128)(2,1)}), bf16[128,2048]{1,0:T(8,128)(2,1)}) %reduce-scatter.11.cloned.1.call-update) | async-done | bytes 524304 | tf_op jit(solution)/shard_map/reduce_scatter | solution.py:27
  1152.9 134.2 %reduce-scatter.25.cloned.1.call-done = f32[64,2]{1,0:T(8,128)} async-done(((f32[2048,2]{1,0:T(8,128)}), f32[64,2]{1,0:T(8,128)}) %reduce-scatter.25.cloned.1.call-update) | async-done | bytes 528
  1289.2 21.6 %reduce-scatter.19.cloned.1.call-done = bf16[64,2048]{1,0:T(8,128)(2,1)} async-done(((bf16[256,2048]{1,0:T(8,128)(2,1)}), bf16[64,2048]{1,0:T(8,128)(2,1)}) %reduce-scatter.19.cloned.1.call-update) | async-done | bytes 262160 | tf_op jit(solution)/shard_map/reduce_scatter | solution.py:31
  (184 shorter events, 141.6 us)
Async XLA Ops:
  7.2 131.1 %all-gather.25.cloned.1.call-start = ((), (), s32[]{:S(2)}) async-start(), calls=%async_computation.26 | async-start | bytes 4718592 | tf_op jit(solution)/shard_map/all_gather | solution.py:19
  7.9 133.8 %all-gather.13.cloned.1.call-start = ((), (), s32[]{:S(2)}) async-start(), calls=%async_computation.13 | async-start | bytes 3932160 | tf_op jit(solution)/shard_map/all_gather | solution.py:23
  54.0 215.7 %all-gather.15.cloned.1.call-start = ((), (), s32[]{:S(2)}) async-start(), calls=%async_computation.14 | async-start | bytes 4718592 | tf_op jit(solution)/shard_map/all_gather | solution.py:169
  163.4 184.6 %all-gather.17.cloned.1.call-start = ((), (), s32[]{:S(2)}) async-start(), calls=%async_computation.15 | async-start | bytes 8650752 | tf_op jit(solution)/shard_map/all_gather | solution.py:151
  164.0 242.3 %all-gather.19.cloned.1.call-start = ((), (), s32[]{:S(2)}) async-start(), calls=%async_computation.16 | async-start | bytes 10485760 | tf_op jit(solution)/shard_map/all_gather | solution.py:23
  263.9 178.3 %all-gather.21.cloned.1.call-start = ((), (), s32[]{:S(2)}) async-start(), calls=%async_computation.17 | async-start | bytes 5242880 | tf_op jit(solution)/shard_map/all_gather | solution.py:23
  264.5 253.3 %all-gather.27.cloned.1.call-start = ((), (), s32[]{:S(2)}) async-start(), calls=%async_computation.27 | async-start | bytes 4718592 | tf_op jit(solution)/shard_map/all_gather | solution.py:19
  265.2 366.8 %reduce-scatter.13.cloned.1.call-start = ((), (), s32[]{:S(2)}) async-start(), calls=%async_computation.19 | async-start | bytes 4718592 | tf_op jit(solution)/shard_map/reduce_scatter | solution.py:27
  545.7 88.7 %copy-start.3 = (bf16[1,128,2048]{2,1,0:T(8,128)(2,1)S(1)}, bf16[1,128,2048]{2,1,0:T(8,128)(2,1)}, u32[]{:S(2)}) copy-start(bf16[1,128,2048]{2,1,0:T(8,128)(2,1)} %param.23) | copy-start | bytes 1572868
  545.8 90.3 %copy-start.24 = (f32[128]{0:T(128)}, f32[128]{0:T(128)S(1)}, u32[]{:S(2)}) copy-start(f32[128]{0:T(128)S(1)} %dynamic-slice.6) | copy-start | bytes 1540
  643.7 19.1 %all-to-all-start.2 = ((bf16[8,128,256]{1,2,0:T(8,128)(2,1)}), bf16[8,128,256]{1,2,0:T(8,128)(2,1)S(1)}, u32[]{:S(2)}, u32[]{:S(2)}) async-start(bf16[8,128,256]{1,2,0:T(8,128)(2,1)} %bitcast.24), calls=%async_computation.4 | async-start | bytes 1048576 | tf_op jit(solution)/shard_map/all_to_all | solution.py:35
  648.0 88.2 %reduce-scatter.17.cloned.1.call-start = ((), (), s32[]{:S(2)}) async-start(), calls=%async_computation.21 | async-start | bytes 3932160 | tf_op jit(solution)/shard_map/reduce_scatter | solution.py:31
  694.0 111.4 %reduce-scatter.21.cloned.1.call-start = ((), (), s32[]{:S(2)}) async-start(), calls=%async_computation.24 | async-start | bytes 10485760 | tf_op jit(solution)/shard_map/reduce_scatter | solution.py:31
  709.6 227.0 %reduce-scatter.15.cloned.1.call-start = ((), (), s32[]{:S(2)}) async-start(), calls=%async_computation.20 | async-start | bytes 4718592 | tf_op jit(solution)/shard_map/reduce_scatter | solution.py:27
  717.9 294.5 %all-gather.23.cloned.1.call-start = ((), (), s32[]{:S(2)}) async-start(), calls=%async_computation.22 | async-start | bytes 4718592 | tf_op jit(solution)/shard_map/all_gather | solution.py:19
  718.5 339.2 %reduce-scatter.23.cloned.1.call-start = ((), (), s32[]{:S(2)}) async-start(), calls=%async_computation.25 | async-start | bytes 5242880 | tf_op jit(solution)/shard_map/reduce_scatter | solution.py:31
  727.9 421.6 %reduce-scatter.11.cloned.1.call-start = ((), (), s32[]{:S(2)}) async-start(), calls=%async_computation.18 | async-start | bytes 4718592 | tf_op jit(solution)/shard_map/reduce_scatter | solution.py:27
  736.2 200.5 %copy-start.1 = (bf16[1,128,2048]{2,1,0:T(8,128)(2,1)S(1)}, bf16[1,128,2048]{2,1,0:T(8,128)(2,1)}, u32[]{:S(2)}) copy-start(bf16[1,128,2048]{2,1,0:T(8,128)(2,1)} %param.12) | copy-start | bytes 1572868
  736.2 201.9 %copy-start.23 = (f32[2048]{0:T(1024)S(1)}, f32[2048]{0:T(1024)}, u32[]{:S(2)}) copy-start(f32[2048]{0:T(1024)} %get-tuple-element.11) | copy-start | bytes 24580
  736.3 69.1 %all-to-all-start.3 = ((bf16[8,64,768]{2,1,0:T(8,128)(2,1)}), bf16[8,64,768]{2,1,0:T(8,128)(2,1)S(1)}, u32[]{:S(2)}, u32[]{:S(2)}) async-start(bf16[8,64,768]{2,1,0:T(8,128)(2,1)} %bitcast.144), calls=%async_computation.7 | async-start | bytes 1572864 | tf_op jit(solution)/shard_map/all_to_all | solution.py:35
  805.4 507.3 %all-to-all-start.4 = ((bf16[8,64,2048]{2,1,0:T(8,128)(2,1)}), bf16[8,64,2048]{2,1,0:T(8,128)(2,1)S(1)}, u32[]{:S(2)}, u32[]{:S(2)}) async-start(bf16[8,64,2048]{2,1,0:T(8,128)(2,1)} %bitcast.143), calls=%async_computation.10 | async-start | bytes 4194304 | tf_op jit(solution)/shard_map/all_to_all | solution.py:35
  810.9 476.3 %reduce-scatter.25.cloned.1.call-start = ((), (), s32[]{:S(2)}) async-start(), calls=%async_computation.28 | async-start | bytes 1081344
  939.5 371.3 %reduce-scatter.19.cloned.1.call-start = ((), (), s32[]{:S(2)}) async-start(), calls=%async_computation.23 | async-start | bytes 1310720 | tf_op jit(solution)/shard_map/reduce_scatter | solution.py:31
  1062.3 87.2 %copy-start.29 = (f32[128]{0:T(128)S(1)}, f32[128]{0:T(128)}, u32[]{:S(2)}) copy-start(f32[128]{0:T(128)} %copy-done.28) | copy-start | bytes 1540
  (34 other events, 535.7 us)
Sparse Core Ops, SparseCore 0:
  10.1 89.2 all-gather.24
  100.9 26.7 all-gather.12
  163.5 106.1 all-gather.14
  272.5 75.4 all-gather.16
  349.4 56.8 all-gather.18
  407.7 34.4 all-gather.20
  444.4 73.3 all-gather.26
  545.9 86.1 reduce-scatter.12
  694.1 36.9 reduce-scatter.16
  733.6 71.7 reduce-scatter.20
  809.4 127.1 reduce-scatter.14
  939.2 73.1 all-gather.22
  1014.9 42.7 reduce-scatter.22
  1061.7 87.8 reduce-scatter.10
  1152.2 134.8 reduce-scatter.24
  1289.7 21.1 reduce-scatter.18

commit v2 on v1

--- a/solution.py
+++ b/solution.py
@@ -15,24 +15,94 @@
 f32 = jnp.float32
 
 
+def swap(block, axis, mask):
+    n = lax.axis_size(axis)
+    return lax.ppermute(block, axis, [(i, i ^ mask) for i in range(n)])
+
+
+def ctx_masks():
+    masks = []
+    bit = lax.axis_size("ctx") // 2
+    while bit:
+        masks.append(bit ^ (bit >> 1) if bit > 2 else bit)
+        bit //= 2
+    return masks
+
+
 def gather_ctx(block):
-    return lax.all_gather(block, "ctx", axis=0, tiled=True)
+    held = [(0, block)]
+    for mask in ctx_masks():
+        held += [(offset ^ mask, swap(part, "ctx", mask)) for offset, part in held]
+    return held
 
 
 def gather_seq(block):
-    return lax.all_gather(block, "seq", axis=0, tiled=True)
+    held = [(0, block)]
+    mask = lax.axis_size("seq") // 2
+    while mask:
+        held += [(offset ^ mask, swap(part, "seq", mask)) for offset, part in held]
+        mask //= 2
+    return held
+
+
+def ordered(held, axis):
+    here = lax.axis_index(axis)
+    block = held[0][1]
+    whole = jnp.zeros((len(held),) + block.shape, block.dtype)
+    for offset, part in held:
+        whole = lax.dynamic_update_index_in_dim(whole, part, here ^ offset, 0)
+    return whole
+
+
+def rows_of(held, axis):
+    whole = ordered(held, axis)
+    return whole.reshape((whole.shape[0] * whole.shape[1],) + whole.shape[2:])
+
+
+def sum_over(parts, axis, masks):
+    levels = [[0]]
+    for mask in masks:
+        levels.append([offset ^ mask for level in levels for offset in level])
+    for mask, level in reversed(list(zip(masks, levels[1:]))):
+        for offset in reversed(level):
+            got = swap(parts.pop(offset).astype(bf16), axis, mask)
+            parts[offset ^ mask] = parts[offset ^ mask].astype(f32) + got.astype(f32)
+    return parts[0]
 
 
 def scatter_ctx(total):
-    return lax.psum_scatter(total.astype(bf16), "ctx", scatter_dimension=0, tiled=True).astype(f32)
+    n = lax.axis_size("ctx")
+    here = lax.axis_index("ctx")
+    rows = total.shape[0] // n
+    parts = {
+        o: lax.dynamic_slice_in_dim(total, (here ^ o) * rows, rows, 0) for o in range(n)
+    }
+    return sum_over(parts, "ctx", ctx_masks())
 
 
 def scatter_seq(total):
-    return lax.psum_scatter(total.astype(bf16), "seq", scatter_dimension=0, tiled=True)
-
-
-def swap_ctx(blocks):
-    return lax.all_to_all(blocks, "ctx", 0, 0, tiled=True)
+    n = lax.axis_size("seq")
+    here = lax.axis_index("seq")
+    rows = total.shape[0] // n
+    piece = lambda o: lax.dynamic_slice_in_dim(total, (here ^ o) * rows, rows, 0)
+    got = swap(jnp.concatenate([piece(3), piece(1)], axis=0).astype(bf16), "seq", 1).astype(f32)
+    far = swap((piece(2) + got[:rows]).astype(bf16), "seq", 2).astype(f32)
+    return piece(0) + got[rows:] + far
+
+
+def swap_ctx(block_of):
+    n = lax.axis_size("ctx")
+    here = lax.axis_index("ctx")
+    return [(o, swap(block_of(here ^ o), "ctx", o) if o else block_of(here)) for o in range(n)]
+
+
+def total_over_all(values):
+    for axis in ("ctx", "seq"):
+        mask = 1
+        while mask < lax.axis_size(axis):
+            values = values + swap(values, axis, mask)
+            mask *= 2
+    return values
 
 
 def rms_scale(values):
@@ -71,23 +141,34 @@
     return lax.dot_general(left, right, (((1,), (1,)), ((), ())), preferred_element_type=f32)
 
 
-def columns_to_owners(weight, groups):
-    n = lax.axis_size("ctx")
-    rows = weight.shape[0]
-    width = weight.shape[1] // (n * groups)
-    blocks = weight.reshape(rows, groups, n, width).transpose(2, 0, 1, 3)
-    mine = swap_ctx(blocks.reshape(n, rows, groups * width))
-    return gather_seq(mine.reshape(n * rows, groups * width))
-
-
-def columns_from_owners(total, groups):
-    n = lax.axis_size("ctx")
-    part = scatter_seq(total)
+def columns_to_owners(weights, groups):
+    n = lax.axis_size("ctx")
+    rows = weights[0].shape[0]
+    width = weights[0].shape[1] // (n * groups)
+
+    def block_of(device):
+        cuts = [
+            lax.dynamic_slice_in_dim(weight, (g * n + device) * width, width, 1)
+            for weight in weights
+            for g in range(groups)
+        ]
+        return jnp.concatenate(cuts, axis=1)
+
+    mine = rows_of(swap_ctx(block_of), "ctx")
+    return rows_of(gather_seq(mine), "seq")
+
+
+def columns_from_owners(total, count, groups):
+    n = lax.axis_size("ctx")
+    part = scatter_seq(total).astype(bf16)
     rows = part.shape[0] // n
-    width = part.shape[1] // groups
-    back = swap_ctx(part.reshape(n, rows, groups * width))
-    back = back.reshape(n, rows, groups, width).transpose(1, 2, 0, 3)
-    return back.reshape(rows, groups * n * width)
+    width = part.shape[1] // (count * groups)
+    back = swap_ctx(lambda device: lax.dynamic_slice_in_dim(part, device * rows, rows, 0))
+    back = ordered(back, "ctx").reshape(n, rows, count, groups, width)
+    return [
+        back[:, :, i].transpose(1, 2, 0, 3).reshape(rows, groups * n * width).astype(f32)
+        for i in range(count)
+    ]
 
 
 def attention(query, key, value, positions):
@@ -144,19 +225,25 @@
     def own_rows(whole):
         return lax.dynamic_slice_in_dim(whole, here * rows, rows, 0)
 
-    qkv_sub = columns_to_owners(jnp.concatenate([w_query, w_key, w_value], axis=1), 3)
-    x_low = gather_ctx(hidden_in[0])
-    pos_all = gather_ctx(positions[0])
-    gains = lax.all_gather(jnp.stack([attn_gain, mlp_gain]), ("seq", "ctx"), axis=1, tiled=True)
+    pos_high, pos_low = positions[0] // 64, positions[0] % 64
+    small = jnp.concatenate(
+        [pos_high.astype(bf16), pos_low.astype(bf16), attn_gain, mlp_gain]
+    ).reshape(1, -1)
+    small = rows_of(gather_ctx(small), "ctx")
+    pos_all = (small[:, :rows].astype(jnp.int32) * 64 + small[:, rows : 2 * rows].astype(jnp.int32)).reshape(-1)
+    gains = ordered(gather_seq(small[:, 2 * rows :]), "seq").reshape(seqs, n, 2, -1)
+    gain1 = gains[:, :, 0].reshape(-1).astype(f32)
+    gain2 = gains[:, :, 1].reshape(-1).astype(f32)
+    x_low = rows_of(gather_ctx(hidden_in[0]), "ctx")
+    qkv_sub = columns_to_owners((w_query, w_key, w_value), 1)
+    down_sub = rows_of(gather_seq(w_down), "seq")
+    grad_all = rows_of(gather_ctx(out_grad[0]), "ctx")
     full_out = lax.all_gather(w_out, ("seq", "ctx"), axis=0, tiled=True)
-    gate_up = columns_to_owners(jnp.concatenate([w_gate, w_up], axis=1), 2 * seqs)
-    down_sub = gather_seq(w_down)
-    grad_all = gather_ctx(out_grad[0])
+    gate_sub = columns_to_owners((w_gate,), seqs)
+    up_sub = columns_to_owners((w_up,), seqs)
 
     x = x_low.astype(f32)
     attn_scale = rms_scale(x)
-    gain1 = gains[0].astype(f32)
-    gain2 = gains[1].astype(f32)
     normed = (x * attn_scale * gain1).astype(bf16)
     angles = angle_table(pos_all)
     cosine, sine = jnp.cos(angles), jnp.sin(angles)
@@ -166,14 +253,14 @@
     key = rotate(qkv[:, width : 2 * width], cosine, sine).astype(bf16)
     value = qkv[:, 2 * width :].astype(bf16)
     attended, lse = attention(query, key, value, pos_all)
-    att_low = lax.all_gather(attended.astype(bf16), "ctx", axis=1, tiled=True)
+    att_low = ordered(gather_ctx(attended.astype(bf16)), "ctx")
+    att_low = att_low.transpose(1, 0, 2).reshape(n * rows, -1)
 
     middle = x + dot(att_low, full_out)
     mlp_scale = rms_scale(middle)
     normed_mid = (middle * mlp_scale * gain2).astype(bf16)
-    gate_up_act = dot(normed_mid, gate_up)
-    units = gate_up.shape[1] // 2
-    gate_act, up_act = gate_up_act[:, :units], gate_up_act[:, units:]
+    gate_act = dot(normed_mid, gate_sub)
+    up_act = dot(normed_mid, up_sub)
     sig = jax.nn.sigmoid(gate_act)
     inner = (gate_act * sig * up_act).astype(bf16)
     middle_own = own_rows(middle)
@@ -182,11 +269,10 @@
     inner_grad = dot_cols(grad_all, down_sub)
     gate_grad = (inner_grad * up_act * sig * (1.0 + gate_act * (1.0 - sig))).astype(bf16)
     up_grad = (inner_grad * gate_act * sig).astype(bf16)
-    gate_up_grad = jnp.concatenate([gate_grad, up_grad], axis=1)
-    mid_grad_in = scatter_ctx(dot_cols(gate_up_grad, gate_up))
-    w_gate_up_grad = columns_from_owners(dot_rows(normed_mid, gate_up_grad), 2 * seqs).astype(f32)
-    hidden_units = w_gate.shape[1]
-    w_down_grad = scatter_seq(dot_rows(inner, grad_all)).astype(f32)
+    mid_grad_in = scatter_ctx(dot_cols(gate_grad, gate_sub) + dot_cols(up_grad, up_sub))
+    (w_gate_grad,) = columns_from_owners(dot_rows(normed_mid, gate_grad), 1, seqs)
+    (w_up_grad,) = columns_from_owners(dot_rows(normed_mid, up_grad), 1, seqs)
+    w_down_grad = scatter_seq(dot_rows(inner, grad_all))
 
     mid_scale = own_rows(mlp_scale)
     mid_unit = middle_own * mid_scale
@@ -196,13 +282,16 @@
     )
     mlp_gain_part = jnp.sum(mid_grad_in * mid_unit, axis=0)
     middle_low = middle_grad.astype(bf16)
-    att_grad = dot_cols(middle_low, full_out).astype(bf16)
-    att_grad = swap_ctx(att_grad.reshape(rows, n, -1).transpose(1, 0, 2)).reshape(n * rows, -1)
-    middle_low_all = gather_ctx(middle_low)
+    att_grad_own = dot_cols(middle_low, full_out).astype(bf16)
+    head_cols = att_grad_own.shape[1] // n
+    att_grad = rows_of(
+        swap_ctx(lambda d: lax.dynamic_slice_in_dim(att_grad_own, d * head_cols, head_cols, 1)), "ctx"
+    )
+    middle_low_all = rows_of(gather_ctx(middle_low), "ctx")
     out_rows = w_out.shape[0]
     att_cols = att_low.reshape(n * rows, seqs, n, out_rows)
     att_sub = lax.dynamic_slice_in_dim(att_cols, here, 1, 2).reshape(n * rows, seqs * out_rows)
-    w_out_grad = scatter_seq(dot_rows(att_sub, middle_low_all)).astype(f32)
+    w_out_grad = scatter_seq(dot_rows(att_sub, middle_low_all))
 
     query_acc, key_acc, value_acc = attention_back(
         query, key, value, pos_all, attended, lse, att_grad
@@ -210,33 +299,31 @@
     qkv_grad = jnp.concatenate(
         [rotate(query_acc, cosine, -sine), rotate(key_acc, cosine, -sine), value_acc], axis=1
     ).astype(bf16)
-    normed_grad = scatter_ctx(dot_cols(qkv_grad, qkv_sub))
+    normed_grad_part = dot_cols(qkv_grad, qkv_sub)
+    attn_gain_part = jnp.sum(normed_grad_part * (x * attn_scale), axis=0)
+    gain_grads = total_over_all(jnp.stack([attn_gain_part, mlp_gain_part]))
+    gain_rows = attn_gain.shape[0]
+    place = (lax.axis_index("seq") * n + here) * gain_rows
+    gain_grads = lax.dynamic_slice_in_dim(gain_grads, place, gain_rows, 1)
+    normed_grad = scatter_ctx(normed_grad_part)
     own_scale = own_rows(attn_scale)
     own_unit = hidden_in[0].astype(f32) * own_scale
     attn_term = normed_grad * gain1
     hidden_grad = middle_grad + own_scale * (
         attn_term - own_unit * jnp.mean(own_unit * attn_term, axis=-1, keepdims=True)
     )
-    attn_gain_part = jnp.sum(normed_grad * own_unit, axis=0)
-    w_qkv_grad = columns_from_owners(dot_rows(normed, qkv_grad), 3).astype(f32)
-    model_width = x.shape[1]
-    gain_grads = lax.psum_scatter(
-        jnp.stack([attn_gain_part, mlp_gain_part], axis=1),
-        ("seq", "ctx"),
-        scatter_dimension=0,
-        tiled=True,
-    )
+    w_query_grad, w_key_grad, w_value_grad = columns_from_owners(dot_rows(normed, qkv_grad), 3, 1)
     return (
         hidden_out[None],
         hidden_grad[None],
-        gain_grads[:, 0],
-        w_qkv_grad[:, :model_width],
-        w_qkv_grad[:, model_width : 2 * model_width],
-        w_qkv_grad[:, 2 * model_width :],
+        gain_grads[0],
+        w_query_grad,
+        w_key_grad,
+        w_value_grad,
         w_out_grad,
-        gain_grads[:, 1],
-        w_gate_up_grad[:, :hidden_units],
-        w_gate_up_grad[:, hidden_units:],
+        gain_grads[1],
+        w_gate_grad,
+        w_up_grad,
         w_down_grad,
     )
 

time: 1340 us -> 957 us (0.71)
  waiting for transfers between devices: 866 us -> 364 us
  blocking collectives: 222 us -> 0 us
  starting transfers between devices: 15.1 us -> 192 us
  local copies, waits for them, and re-layouts: 33.7 us -> 145 us
  other arithmetic: 25.9 us -> 84.2 us
    reduce_scatter x7 -> x0, waiting for transfers between devices: 421 us -> none  [the longest x3 293 us: scatter_ctx(): lax.psum_scatter(total.astype(bf16), 'ctx', scatter_dimension=0, tiled=True)]
    ppermute x0 -> x135, waiting for transfers between devices: none -> 364 us  [swap(): return lax.ppermute(block, axis, [(i, i ^ mask) for i in range(n)])]
    all_gather x7 -> x0, waiting for transfers between devices: 215 us -> none  [the longest x3 148 us: gather_ctx(): return lax.all_gather(block, 'ctx', axis=0, tiled=True)]
    ppermute x0 -> x135, starting transfers between devices: none -> 192 us  [swap(): return lax.ppermute(block, axis, [(i, i ^ mask) for i in range(n)])]
    all_to_all x2 -> x0, blocking collectives: 139 us -> none  [swap_ctx(): return lax.all_to_all(blocks, 'ctx', 0, 0, tiled=True)]
    unnamed x17 -> x1, waiting for transfers between devices: 137 us -> 0.02 us
    all_gather x2 -> x0, blocking collectives: 82.2 us -> none  [the longest x1 63.2 us: local(): lax.all_gather(jnp.stack([attn_gain, mlp_gain]), ('seq', 'ctx'), axis=1,...]
    all_gather x1, waiting for transfers between devices: 78.3 us -> 0.01 us  [local(): full_out = lax.all_gather(w_out, ('seq', 'ctx'), axis=0, tiled=True)]
  transfers between devices with their start and end apart: 19 -> 136, of which waited for: 14 -> 63; matrix products, arithmetic and copies ran while one was open for 8% -> 28% of each run, Pallas kernels for 0% -> 0%
where the time goes in v2:
time: 957 us; the launch traced here: 945 us
  waiting for transfers between devices  364 us (38%)
  starting transfers between devices  192 us (20%)
  local copies, waits for them, and re-layouts  145 us (15%)
  matrix products  142 us (15%)
  other arithmetic  84.2 us (9%)
  between operations  17.2 us (2%)
    ppermute x135, waiting for transfers between devices, swap(): return lax.ppermute(block, axis, [(i, i ^ mask) for i in range(n)])  364 us
    ppermute x135, starting transfers between devices, swap(): return lax.ppermute(block, axis, [(i, i ^ mask) for i in range(n)])  192 us
    dynamic_update_slice x111, local copies, waits for them, and re-layouts, ordered(): whole = lax.dynamic_update_index_in_dim(whole, part, here ^ offset, 0)  76.6 us
    dot_general x5, matrix products, dot_cols(): lax.dot_general(left, right, (((1,), (1,)), ((), ())), preferred_element_...  43.2 us
    dot_general x5, matrix products, dot(): return jnp.dot(left, right, preferred_element_type=f32)  41.7 us
    dot_general x5, matrix products, dot_rows(): lax.dot_general(left, right, (((0,), (0,)), ((), ())), preferred_element_...  26 us
  transfers between devices with their start and end apart: 136, of which 63 were waited for; matrix products, arithmetic and copies ran while one was open for 28% of the time, Pallas kernels for 0%

profile of v2, /device:TPU:0, one launch (start us, length us, event | category | flops | bytes accessed | tf_op | source)
XLA Modules:
  0.0 945.2 jit_solution(17931817819434238935)
XLA Ops:
  75.8 9.8 %collective-permute-done.18 = bf16[64,768]{1,0:T(8,128)(2,1)S(1)} collective-permute-done((bf16[64,768]{1,0:T(8,128)(2,1)}, bf16[64,768]{1,0:T(8,128)(2,1)S(1)}, u32[]{:S(2)}, u32[]{:S(2)}) %collective-permute-start.18) | collective-permute-done | bytes 98336 | tf_op jit(solution)/shard_map/ppermute | solution.py:20
  168.0 11.3 %collective-permute-done.37 = bf16[64,1024]{1,0:T(8,128)(2,1)S(1)} collective-permute-done((bf16[64,1024]{1,0:T(8,128)(2,1)}, bf16[64,1024]{1,0:T(8,128)(2,1)S(1)}, u32[]{:S(2)}, u32[]{:S(2)}) %collective-permute-start.37) | collective-permute-done | bytes 131104 | tf_op jit(solution)/shard_map/ppermute | solution.py:20
  202.9 29.7 %collective-permute-done.24 = bf16[512,768]{1,0:T(8,128)(2,1)S(1)} collective-permute-done((bf16[512,768]{1,0:T(8,128)(2,1)S(1)}, bf16[512,768]{1,0:T(8,128)(2,1)S(1)}, u32[]{:S(2)}, u32[]{:S(2)}) %collective-permute-start.24) | collective-permute-done | bytes 786464 | tf_op jit(solution)/shard_map/ppermute | solution.py:20
  249.2 10.3 %collective-permute-done.4 = bf16[128,2048]{1,0:T(8,128)(2,1)S(1)} collective-permute-done((bf16[128,2048]{1,0:T(8,128)(2,1)}, bf16[128,2048]{1,0:T(8,128)(2,1)S(1)}, u32[]{:S(2)}, u32[]{:S(2)}) %collective-permute-start.4) | collective-permute-done | bytes 524320 | tf_op jit(solution)/shard_map/ppermute | solution.py:20
  270.8 11.3 %collective-permute-done.68 = bf16[128,2048]{1,0:T(8,128)(2,1)S(1)} collective-permute-done((bf16[128,2048]{1,0:T(8,128)(2,1)S(1)}, bf16[128,2048]{1,0:T(8,128)(2,1)S(1)}, u32[]{:S(2)}, u32[]{:S(2)}) %collective-permute-start.68) | collective-permute-done | bytes 524320 | tf_op jit(solution)/shard_map/ppermute | solution.py:20
  293.1 9.5 %collective-permute-done.6 = bf16[128,2048]{1,0:T(8,128)(2,1)S(1)} collective-permute-done((bf16[128,2048]{1,0:T(8,128)(2,1)S(1)}, bf16[128,2048]{1,0:T(8,128)(2,1)S(1)}, u32[]{:S(2)}, u32[]{:S(2)}) %collective-permute-start.6) | collective-permute-done | bytes 524320 | tf_op jit(solution)/shard_map/ppermute | solution.py:20
  347.9 8.8 collective-permute-done.27
  356.7 10.2 %collective-permute-start.29 = (bf16[1024,256]{0,1:T(8,128)(2,1)S(1)}, bf16[1024,256]{0,1:T(8,128)(2,1)S(1)}, u32[]{:S(2)}, u32[]{:S(2)}) collective-permute-start(bf16[1024,256]{0,1:T(8,128)(2,1)S(1)} %collective-permute-done.27), channel_id=1, source_target_pairs={{0,2},{1,3},{2,0},{3,1},{4,6},{5,7},{6,4},{7,5},{8,10},{9,11},{10,... | collective-permute-start | bytes 1572872 | tf_op jit(solution)/shard_map/ppermute | solution.py:20
  381.9 11.2 %collective-permute-done.32 = bf16[1024,256]{0,1:T(8,128)(2,1)S(1)} collective-permute-done((bf16[1024,256]{0,1:T(8,128)(2,1)S(1)}, bf16[1024,256]{0,1:T(8,128)(2,1)S(1)}, u32[]{:S(2)}, u32[]{:S(2)}) %collective-permute-start.32) | collective-permute-done | bytes 524320 | tf_op jit(solution)/shard_map/ppermute | solution.py:20
  393.1 9.9 %collective-permute-done.33 = bf16[1024,256]{0,1:T(8,128)(2,1)S(1)} collective-permute-done((bf16[1024,256]{0,1:T(8,128)(2,1)S(1)}, bf16[1024,256]{0,1:T(8,128)(2,1)S(1)}, u32[]{:S(2)}, u32[]{:S(2)}) %collective-permute-start.33) | collective-permute-done | bytes 524320 | tf_op jit(solution)/shard_map/ppermute | solution.py:20
  405.9 14.3 %multiply_reduce_fusion = (f32[1024]{0:T(1024)S(1)}, f32[1024,2048]{1,0:T(8,128)S(1)}) fusion(bf16[1024,2048]{0,1:T(8,128)(2,1)} %bitcast.394, bf16[2048,2048]{1,0:T(8,128)(2,1)} %all-gather.2.cloned.1.call-done, bf16[8,128,2048]{2,1,0:T(8,128)(2,1)} %bitcast_dynamic-update-slice_fusion.38), kind=kOutput, calls=%fused_computation.19 | convolution fusion | flops 8598322176 | bytes 25169920 | tf_op jit(solution)/shard_map/dot_general | solution.py:133
  421.0 11.5 %fusion.79 = f32[1024,1024]{1,0:T(8,128)} fusion(bf16[1024,2048]{1,0:T(8,128)(2,1)S(1)} %multiply_convert_fusion.1, bf16[2048,1024]{1,0:T(8,128)(2,1)} %bitcast.419), kind=kOutput, calls=%fused_computation.426 | convolution fusion | flops 4294967296 | bytes 12582912 | tf_op jit(solution)/shard_map/dot_general | solution.py:133
  438.8 14.6 %multiply_convert_fusion.3 = (bf16[1024,1024]{1,0:T(8,128)(2,1)}, bf16[1024,1024]{1,0:T(8,128)(2,1)}, bf16[1024,1024]{1,0:T(8,128)(2,1)}) fusion(f32[1024,1024]{1,0:T(8,128)} %fusion.78, f32[1024,1024]{1,0:T(8,128)} %fusion.79, bf16[1024,2048]{1,0:T(8,128)(2,1)} %bitcast.415, bf16[1024,2048]{1,0:T(8,128)(2,1)} %bitcast.417), kind=kOutput, calls=%fused_computation.25 | convolution fusion | flops 4311744512 | bytes 23068672 | tf_op jit(solution)/shard_map/dot_general | solution.py:141
  481.8 10.1 %convolution_add_fusion = f32[1024,2048]{1,0:T(8,128)} fusion(f32[1024,2048]{1,0:T(8,128)} %fusion.81, bf16[1024,1024]{1,0:T(8,128)(2,1)} %get-tuple-element.38, bf16[2048,1024]{1,0:T(8,128)(2,1)S(1)} %bitcast.414), kind=kOutput, calls=%fused_computation.28 | convolution fusion | flops 4297064448 | bytes 23068672 | tf_op jit(solution)/shard_map/dot_general | solution.py:141
  510.3 11.2 %collective-permute-done.75 = bf16[128,2048]{1,0:T(8,128)(2,1)S(1)} collective-permute-done((bf16[128,2048]{1,0:T(8,128)(2,1)S(1)}, bf16[128,2048]{1,0:T(8,128)(2,1)S(1)}, u32[]{:S(2)}, u32[]{:S(2)}) %collective-permute-start.75) | collective-permute-done | bytes 524320 | tf_op jit(solution)/shard_map/ppermute | solution.py:20
  544.1 11.4 %collective-permute-done.73 = bf16[128,2048]{1,0:T(8,128)(2,1)S(1)} collective-permute-done((bf16[128,2048]{1,0:T(8,128)(2,1)S(1)}, bf16[128,2048]{1,0:T(8,128)(2,1)S(1)}, u32[]{:S(2)}, u32[]{:S(2)}) %collective-permute-start.73) | collective-permute-done | bytes 524320 | tf_op jit(solution)/shard_map/ppermute | solution.py:20
  614.1 9.3 multiply_convert_fusion
  649.3 9.6 %collective-permute-done.92 = f32[2,2048]{1,0:T(2,128)S(1)} collective-permute-done((f32[2,2048]{1,0:T(2,128)S(1)}, f32[2,2048]{1,0:T(2,128)S(1)}, u32[]{:S(2)}, u32[]{:S(2)}) %collective-permute-start.92) | collective-permute-done | bytes 16416 | tf_op jit(solution)/shard_map/ppermute | solution.py:20
  706.2 10.1 %collective-permute-done.89 = bf16[128,2048]{1,0:T(8,128)(2,1)S(1)} collective-permute-done((bf16[128,2048]{1,0:T(8,128)(2,1)S(1)}, bf16[128,2048]{1,0:T(8,128)(2,1)S(1)}, u32[]{:S(2)}, u32[]{:S(2)}) %collective-permute-start.89) | collective-permute-done | bytes 524320 | tf_op jit(solution)/shard_map/ppermute | solution.py:20
  721.7 17.0 %collective-permute-done.110 = bf16[128,2048]{1,0:T(8,128)(2,1)S(1)} collective-permute-done((bf16[128,2048]{1,0:T(8,128)(2,1)S(1)}, bf16[128,2048]{1,0:T(8,128)(2,1)S(1)}, u32[]{:S(2)}, u32[]{:S(2)}) %collective-permute-start.110) | collective-permute-done | bytes 524320 | tf_op jit(solution)/shard_map/ppermute | solution.py:20
  755.2 18.9 %collective-permute-done.125 = bf16[512,1024]{1,0:T(8,128)(2,1)} collective-permute-done((bf16[512,1024]{1,0:T(8,128)(2,1)}, bf16[512,1024]{1,0:T(8,128)(2,1)}, u32[]{:S(2)}, u32[]{:S(2)}) %collective-permute-start.125) | collective-permute-done | bytes 1048608 | tf_op jit(solution)/shard_map/ppermute | solution.py:20
  779.6 13.7 %collective-permute-done.134 = bf16[256,2048]{1,0:T(8,128)(2,1)} collective-permute-done((bf16[256,2048]{1,0:T(8,128)(2,1)}, bf16[256,2048]{1,0:T(8,128)(2,1)}, u32[]{:S(2)}, u32[]{:S(2)}) %collective-permute-start.134) | collective-permute-done | bytes 1048608 | tf_op jit(solution)/shard_map/ppermute | solution.py:20
  820.7 13.3 %collective-permute-start.118 = (bf16[64,1024]{1,0:T(8,128)(2,1)S(1)}, bf16[64,1024]{1,0:T(8,128)(2,1)S(1)}, u32[]{:S(2)}, u32[]{:S(2)}) collective-permute-start(bf16[64,1024]{1,0:T(8,128)(2,1)S(1)} %get-tuple-element.75), channel_id=1, source_target_pairs={{0,2},{1,3},{2,0},{3,1},{4,6},{5,7},{6,4},{7,5},{8,10},{9,11},{10,... | collective-permute-start | bytes 393224 | tf_op jit(solution)/shard_map/ppermute | solution.py:20
  842.5 11.2 %collective-permute-start.121 = (bf16[64,1024]{1,0:T(8,128)(2,1)S(1)}, bf16[64,1024]{1,0:T(8,128)(2,1)S(1)}, u32[]{:S(2)}, u32[]{:S(2)}) collective-permute-start(bf16[64,1024]{1,0:T(8,128)(2,1)S(1)} %get-tuple-element.72), channel_id=1, source_target_pairs={{0,5},{1,4},{2,7},{3,6},{4,1},{5,0},{6,3},{7,2},{8,13},{9,12},{10,... | collective-permute-start | bytes 393224 | tf_op jit(solution)/shard_map/ppermute | solution.py:20
  (746 shorter events, 630.0 us)
Async XLA Ops:
  7.2 398.7 %all-gather.2.cloned.1.call-start = ((), (), s32[]{:S(2)}) async-start(), calls=%async_computation | async-start | bytes 8650752 | tf_op jit(solution)/shard_map/all_gather | solution.py:241
  15.8 175.2 %collective-permute-start = (bf16[128,2048]{1,0:T(8,128)(2,1)}, bf16[128,2048]{1,0:T(8,128)(2,1)}, u32[]{:S(2)}, u32[]{:S(2)}) collective-permute-start(bf16[128,2048]{1,0:T(8,128)(2,1)} %bitcast.399), channel_id=1, source_target_pairs={{0,6},{1,7},{2,4},{3,5},{4,2},{5,3},{6,0},{7,1},{8,14},{9,15},{10,... | collective-permute-start | bytes 1572872 | tf_op jit(solution)/shard_map/ppermute | solution.py:20
  51.7 144.8 %collective-permute-start.1 = (bf16[128,2048]{1,0:T(8,128)(2,1)S(1)}, bf16[128,2048]{1,0:T(8,128)(2,1)}, u32[]{:S(2)}, u32[]{:S(2)}) collective-permute-start(bf16[128,2048]{1,0:T(8,128)(2,1)S(1)} %bitcast.400), channel_id=1, source_target_pairs={{0,2},{1,3},{2,0},{3,1},{4,6},{5,7},{6,4},{7,5},{8,10},{9,11},{10,... | collective-permute-start | bytes 1572872 | tf_op jit(solution)/shard_map/ppermute | solution.py:20
  54.1 193.2 %collective-permute-start.3 = (bf16[128,2048]{1,0:T(8,128)(2,1)S(1)}, bf16[128,2048]{1,0:T(8,128)(2,1)}, u32[]{:S(2)}, u32[]{:S(2)}) collective-permute-start(bf16[128,2048]{1,0:T(8,128)(2,1)S(1)} %bitcast.401), channel_id=1, source_target_pairs={{0,1},{1,0},{2,3},{3,2},{4,5},{5,4},{6,7},{7,6},{8,9},{9,8},{10,11... | collective-permute-start | bytes 1572872 | tf_op jit(solution)/shard_map/ppermute | solution.py:20
  56.9 71.7 %collective-permute-start.44 = (bf16[64,1024]{1,0:T(8,128)(2,1)}, bf16[64,1024]{1,0:T(8,128)(2,1)}, u32[]{:S(2)}, u32[]{:S(2)}) collective-permute-start(bf16[64,1024]{1,0:T(8,128)(2,1)} %pad_maximum_fusion.23), channel_id=1, source_target_pairs={{0,1},{1,0},{2,3},{3,2},{4,5},{5,4},{6,7},{7,6},{8,9},{9,8},{10,11... | collective-permute-start | bytes 393224 | tf_op jit(solution)/shard_map/ppermute | solution.py:20
  191.0 43.9 %collective-permute-start.54 = (bf16[256,2048]{1,0:T(8,128)(2,1)S(1)}, bf16[256,2048]{1,0:T(8,128)(2,1)S(1)}, u32[]{:S(2)}, u32[]{:S(2)}) collective-permute-start(bf16[256,2048]{1,0:T(8,128)(2,1)S(1)} %copy-done.41), channel_id=1, source_target_pairs={{0,16},{8,24},{16,0},{24,8},{1,17},{9,25},{17,1},{25,9},{2,18},{10... | collective-permute-start | bytes 3145736 | tf_op jit(solution)/shard_map/ppermute | solution.py:20
  232.7 55.0 %collective-permute-start.51 = (bf16[512,1024]{1,0:T(8,128)(2,1)S(1)}, bf16[512,1024]{1,0:T(8,128)(2,1)S(1)}, u32[]{:S(2)}, u32[]{:S(2)}) collective-permute-start(bf16[512,1024]{1,0:T(8,128)(2,1)S(1)} %bitcast.406), channel_id=1, source_target_pairs={{0,16},{8,24},{16,0},{24,8},{1,17},{9,25},{17,1},{25,9},{2,18},{10... | collective-permute-start | bytes 3145736 | tf_op jit(solution)/shard_map/ppermute | solution.py:20
  238.0 51.6 %collective-permute-start.52 = (bf16[512,1024]{1,0:T(8,128)(2,1)S(1)}, bf16[512,1024]{1,0:T(8,128)(2,1)S(1)}, u32[]{:S(2)}, u32[]{:S(2)}) collective-permute-start(bf16[512,1024]{1,0:T(8,128)(2,1)S(1)} %bitcast.407), channel_id=1, source_target_pairs={{0,8},{8,0},{16,24},{24,16},{1,9},{9,1},{17,25},{25,17},{2,10},{10... | collective-permute-start | bytes 3145736 | tf_op jit(solution)/shard_map/ppermute | solution.py:20
  290.2 53.9 %collective-permute-start.56 = (bf16[256,2048]{1,0:T(8,128)(2,1)S(1)}, bf16[256,2048]{1,0:T(8,128)(2,1)}, u32[]{:S(2)}, u32[]{:S(2)}) collective-permute-start(bf16[256,2048]{1,0:T(8,128)(2,1)S(1)} %collective-permute-done.54), channel_id=1, source_target_pairs={{0,8},{8,0},{16,24},{24,16},{1,9},{9,1},{17,25},{25,17},{2,10},{10... | collective-permute-start | bytes 3145736 | tf_op jit(solution)/shard_map/ppermute | solution.py:20
  292.4 75.8 %collective-permute-start.53 = (bf16[512,1024]{1,0:T(8,128)(2,1)S(1)}, bf16[512,1024]{1,0:T(8,128)(2,1)S(1)}, u32[]{:S(2)}, u32[]{:S(2)}) collective-permute-start(bf16[512,1024]{1,0:T(8,128)(2,1)S(1)} %collective-permute-done.51), channel_id=1, source_target_pairs={{0,8},{8,0},{16,24},{24,16},{1,9},{9,1},{17,25},{25,17},{2,10},{10... | collective-permute-start | bytes 3145736 | tf_op jit(solution)/shard_map/ppermute | solution.py:20
  302.5 67.7 %collective-permute-start.43 = (bf16[512,1024]{1,0:T(8,128)(2,1)}, bf16[512,1024]{1,0:T(8,128)(2,1)S(1)}, u32[]{:S(2)}, u32[]{:S(2)}) collective-permute-start(bf16[512,1024]{1,0:T(8,128)(2,1)} %collective-permute-done.41), channel_id=1, source_target_pairs={{0,8},{8,0},{16,24},{24,16},{1,9},{9,1},{17,25},{25,17},{2,10},{10... | collective-permute-start | bytes 3145736 | tf_op jit(solution)/shard_map/ppermute | solution.py:20
  498.2 45.9 %collective-permute-start.71 = (bf16[128,2048]{1,0:T(8,128)(2,1)}, bf16[128,2048]{1,0:T(8,128)(2,1)}, u32[]{:S(2)}, u32[]{:S(2)}) collective-permute-start(bf16[128,2048]{1,0:T(8,128)(2,1)} %get-tuple-element.32), channel_id=1, source_target_pairs={{0,1},{1,0},{2,3},{3,2},{4,5},{5,4},{6,7},{7,6},{8,9},{9,8},{10,11... | collective-permute-start | bytes 1572872 | tf_op jit(solution)/shard_map/ppermute | solution.py:20
  524.9 44.5 %collective-permute-start.58 = (bf16[128,2048]{1,0:T(8,128)(2,1)}, bf16[128,2048]{1,0:T(8,128)(2,1)}, u32[]{:S(2)}, u32[]{:S(2)}) collective-permute-start(bf16[128,2048]{1,0:T(8,128)(2,1)} %get-tuple-element.44), channel_id=1, source_target_pairs={{0,1},{1,0},{2,3},{3,2},{4,5},{5,4},{6,7},{7,6},{8,9},{9,8},{10,11... | collective-permute-start | bytes 1572872 | tf_op jit(solution)/shard_map/ppermute | solution.py:20
  525.6 44.6 %collective-permute-start.61 = (bf16[128,2048]{1,0:T(8,128)(2,1)}, bf16[128,2048]{1,0:T(8,128)(2,1)}, u32[]{:S(2)}, u32[]{:S(2)}) collective-permute-start(bf16[128,2048]{1,0:T(8,128)(2,1)} %get-tuple-element.42), channel_id=1, source_target_pairs={{0,1},{1,0},{2,3},{3,2},{4,5},{5,4},{6,7},{7,6},{8,9},{9,8},{10,11... | collective-permute-start | bytes 1572872 | tf_op jit(solution)/shard_map/ppermute | solution.py:20
  584.4 91.9 %collective-permute-start.133 = (bf16[512,2048]{1,0:T(8,128)(2,1)}, bf16[512,2048]{1,0:T(8,128)(2,1)}, u32[]{:S(2)}, u32[]{:S(2)}) collective-permute-start(bf16[512,2048]{1,0:T(8,128)(2,1)} %pad_maximum_fusion.2), channel_id=1, source_target_pairs={{0,8},{8,0},{16,24},{24,16},{1,9},{9,1},{17,25},{25,17},{2,10},{10... | collective-permute-start | bytes 6291464 | tf_op jit(solution)/shard_map/ppermute | solution.py:20
  584.6 94.0 %collective-permute-start.115 = (bf16[1024,1024]{1,0:T(8,128)(2,1)}, bf16[1024,1024]{1,0:T(8,128)(2,1)}, u32[]{:S(2)}, u32[]{:S(2)}) collective-permute-start(bf16[1024,1024]{1,0:T(8,128)(2,1)} %pad_maximum_fusion), channel_id=1, source_target_pairs={{0,8},{8,0},{16,24},{24,16},{1,9},{9,1},{17,25},{25,17},{2,10},{10... | collective-permute-start | bytes 6291464 | tf_op jit(solution)/shard_map/ppermute | solution.py:20
  586.2 98.7 %collective-permute-start.124 = (bf16[1024,1024]{1,0:T(8,128)(2,1)}, bf16[1024,1024]{1,0:T(8,128)(2,1)}, u32[]{:S(2)}, u32[]{:S(2)}) collective-permute-start(bf16[1024,1024]{1,0:T(8,128)(2,1)} %pad_maximum_fusion.1), channel_id=1, source_target_pairs={{0,8},{8,0},{16,24},{24,16},{1,9},{9,1},{17,25},{25,17},{2,10},{10... | collective-permute-start | bytes 6291464 | tf_op jit(solution)/shard_map/ppermute | solution.py:20
  587.8 56.9 %collective-permute-start.60 = (bf16[128,2048]{1,0:T(8,128)(2,1)}, bf16[128,2048]{1,0:T(8,128)(2,1)}, u32[]{:S(2)}, u32[]{:S(2)}) collective-permute-start(bf16[128,2048]{1,0:T(8,128)(2,1)} %get-tuple-element.43), channel_id=1, source_target_pairs={{0,1},{1,0},{2,3},{3,2},{4,5},{5,4},{6,7},{7,6},{8,9},{9,8},{10,11... | collective-permute-start | bytes 1572872 | tf_op jit(solution)/shard_map/ppermute | solution.py:20
  590.8 54.6 %collective-permute-start.62 = (bf16[128,2048]{1,0:T(8,128)(2,1)}, bf16[128,2048]{1,0:T(8,128)(2,1)}, u32[]{:S(2)}, u32[]{:S(2)}) collective-permute-start(bf16[128,2048]{1,0:T(8,128)(2,1)} %get-tuple-element.46), channel_id=1, source_target_pairs={{0,2},{1,3},{2,0},{3,1},{4,6},{5,7},{6,4},{7,5},{8,10},{9,11},{10,... | collective-permute-start | bytes 1572872 | tf_op jit(solution)/shard_map/ppermute | solution.py:20
  644.6 189.8 %collective-permute-start.57 = (bf16[128,2048]{1,0:T(8,128)(2,1)}, bf16[128,2048]{1,0:T(8,128)(2,1)}, u32[]{:S(2)}, u32[]{:S(2)}) collective-permute-start(bf16[128,2048]{1,0:T(8,128)(2,1)} %get-tuple-element.41), channel_id=1, source_target_pairs={{0,1},{1,0},{2,3},{3,2},{4,5},{5,4},{6,7},{7,6},{8,9},{9,8},{10,11... | collective-permute-start | bytes 1572872 | tf_op jit(solution)/shard_map/ppermute | solution.py:20
  705.0 44.2 %collective-permute-start.88 = (bf16[128,2048]{1,0:T(8,128)(2,1)S(1)}, bf16[128,2048]{1,0:T(8,128)(2,1)S(1)}, u32[]{:S(2)}, u32[]{:S(2)}) collective-permute-start(bf16[128,2048]{1,0:T(8,128)(2,1)S(1)} %get-tuple-element.28), channel_id=1, source_target_pairs={{0,1},{1,0},{2,3},{3,2},{4,5},{5,4},{6,7},{7,6},{8,9},{9,8},{10,11... | collective-permute-start | bytes 1572872 | tf_op jit(solution)/shard_map/ppermute | solution.py:20
  749.2 59.1 %collective-permute-start.97 = (bf16[1024,768]{1,0:T(8,128)(2,1)}, bf16[1024,768]{1,0:T(8,128)(2,1)}, u32[]{:S(2)}, u32[]{:S(2)}) collective-permute-start(bf16[1024,768]{1,0:T(8,128)(2,1)} %pad_maximum_fusion.4), channel_id=1, source_target_pairs={{0,8},{8,0},{16,24},{24,16},{1,9},{9,1},{17,25},{25,17},{2,10},{10... | collective-permute-start | bytes 4718600 | tf_op jit(solution)/shard_map/ppermute | solution.py:20
  749.2 58.7 %collective-permute-start.85 = (bf16[128,2048]{1,0:T(8,128)(2,1)}, bf16[128,2048]{1,0:T(8,128)(2,1)S(1)}, u32[]{:S(2)}, u32[]{:S(2)}) collective-permute-start(bf16[128,2048]{1,0:T(8,128)(2,1)} %get-tuple-element.26), channel_id=1, source_target_pairs={{0,1},{1,0},{2,3},{3,2},{4,5},{5,4},{6,7},{7,6},{8,9},{9,8},{10,11... | collective-permute-start | bytes 1572872 | tf_op jit(solution)/shard_map/ppermute | solution.py:20
  811.7 48.6 %collective-permute-start.117 = (bf16[64,1024]{1,0:T(8,128)(2,1)S(1)}, bf16[64,1024]{1,0:T(8,128)(2,1)S(1)}, u32[]{:S(2)}, u32[]{:S(2)}) collective-permute-start(bf16[64,1024]{1,0:T(8,128)(2,1)S(1)} %get-tuple-element.76), channel_id=1, source_target_pairs={{0,1},{1,0},{2,3},{3,2},{4,5},{5,4},{6,7},{7,6},{8,9},{9,8},{10,11... | collective-permute-start | bytes 393224 | tf_op jit(solution)/shard_map/ppermute | solution.py:20
  (218 other events, 4062.2 us)
Sparse Core Ops, SparseCore 0:
  16.8 87.4 all-gather.1

commit v3 on v1

--- a/solution.py
+++ b/solution.py
@@ -3,6 +3,8 @@
 import jax
 import jax.numpy as jnp
 from jax import lax
+from jax.experimental import pallas as pl
+from jax.experimental.pallas import tpu as pltpu
 from jax.sharding import PartitionSpec as P
 
 HEADS = 32
@@ -15,23 +17,23 @@
 f32 = jnp.float32
 
 
-def gather_ctx(block):
+def plain_gather_ctx(block):
     return lax.all_gather(block, "ctx", axis=0, tiled=True)
 
 
-def gather_seq(block):
+def plain_gather_seq(block):
     return lax.all_gather(block, "seq", axis=0, tiled=True)
 
 
-def scatter_ctx(total):
+def plain_scatter_ctx(total):
     return lax.psum_scatter(total.astype(bf16), "ctx", scatter_dimension=0, tiled=True).astype(f32)
 
 
-def scatter_seq(total):
+def plain_scatter_seq(total):
     return lax.psum_scatter(total.astype(bf16), "seq", scatter_dimension=0, tiled=True)
 
 
-def swap_ctx(blocks):
+def plain_swap_ctx(blocks):
     return lax.all_to_all(blocks, "ctx", 0, 0, tiled=True)
 
 
@@ -76,16 +78,16 @@
     rows = weight.shape[0]
     width = weight.shape[1] // (n * groups)
     blocks = weight.reshape(rows, groups, n, width).transpose(2, 0, 1, 3)
-    mine = swap_ctx(blocks.reshape(n, rows, groups * width))
-    return gather_seq(mine.reshape(n * rows, groups * width))
+    mine = plain_swap_ctx(blocks.reshape(n, rows, groups * width))
+    return plain_gather_seq(mine.reshape(n * rows, groups * width))
 
 
 def columns_from_owners(total, groups):
     n = lax.axis_size("ctx")
-    part = scatter_seq(total)
+    part = plain_scatter_seq(total)
     rows = part.shape[0] // n
     width = part.shape[1] // groups
-    back = swap_ctx(part.reshape(n, rows, groups * width))
+    back = plain_swap_ctx(part.reshape(n, rows, groups * width))
     back = back.reshape(n, rows, groups, width).transpose(1, 2, 0, 3)
     return back.reshape(rows, groups * n * width)
 
@@ -122,7 +124,7 @@
     return tuple(m.reshape(query.shape) for m in (query_acc, key_acc, value_acc))
 
 
-def local(
+def plain(
     hidden_in,
     positions,
     attn_gain,
@@ -145,13 +147,13 @@
         return lax.dynamic_slice_in_dim(whole, here * rows, rows, 0)
 
     qkv_sub = columns_to_owners(jnp.concatenate([w_query, w_key, w_value], axis=1), 3)
-    x_low = gather_ctx(hidden_in[0])
-    pos_all = gather_ctx(positions[0])
+    x_low = plain_gather_ctx(hidden_in[0])
+    pos_all = plain_gather_ctx(positions[0])
     gains = lax.all_gather(jnp.stack([attn_gain, mlp_gain]), ("seq", "ctx"), axis=1, tiled=True)
     full_out = lax.all_gather(w_out, ("seq", "ctx"), axis=0, tiled=True)
     gate_up = columns_to_owners(jnp.concatenate([w_gate, w_up], axis=1), 2 * seqs)
-    down_sub = gather_seq(w_down)
-    grad_all = gather_ctx(out_grad[0])
+    down_sub = plain_gather_seq(w_down)
+    grad_all = plain_gather_ctx(out_grad[0])
 
     x = x_low.astype(f32)
     attn_scale = rms_scale(x)
@@ -177,16 +179,16 @@
     sig = jax.nn.sigmoid(gate_act)
     inner = (gate_act * sig * up_act).astype(bf16)
     middle_own = own_rows(middle)
-    hidden_out = (middle_own + scatter_ctx(dot(inner, down_sub))).astype(bf16)
+    hidden_out = (middle_own + plain_scatter_ctx(dot(inner, down_sub))).astype(bf16)
 
     inner_grad = dot_cols(grad_all, down_sub)
     gate_grad = (inner_grad * up_act * sig * (1.0 + gate_act * (1.0 - sig))).astype(bf16)
     up_grad = (inner_grad * gate_act * sig).astype(bf16)
     gate_up_grad = jnp.concatenate([gate_grad, up_grad], axis=1)
-    mid_grad_in = scatter_ctx(dot_cols(gate_up_grad, gate_up))
+    mid_grad_in = plain_scatter_ctx(dot_cols(gate_up_grad, gate_up))
     w_gate_up_grad = columns_from_owners(dot_rows(normed_mid, gate_up_grad), 2 * seqs).astype(f32)
     hidden_units = w_gate.shape[1]
-    w_down_grad = scatter_seq(dot_rows(inner, grad_all)).astype(f32)
+    w_down_grad = plain_scatter_seq(dot_rows(inner, grad_all)).astype(f32)
 
     mid_scale = own_rows(mlp_scale)
     mid_unit = middle_own * mid_scale
@@ -197,12 +199,12 @@
     mlp_gain_part = jnp.sum(mid_grad_in * mid_unit, axis=0)
     middle_low = middle_grad.astype(bf16)
     att_grad = dot_cols(middle_low, full_out).astype(bf16)
-    att_grad = swap_ctx(att_grad.reshape(rows, n, -1).transpose(1, 0, 2)).reshape(n * rows, -1)
-    middle_low_all = gather_ctx(middle_low)
+    att_grad = plain_swap_ctx(att_grad.reshape(rows, n, -1).transpose(1, 0, 2)).reshape(n * rows, -1)
+    middle_low_all = plain_gather_ctx(middle_low)
     out_rows = w_out.shape[0]
     att_cols = att_low.reshape(n * rows, seqs, n, out_rows)
     att_sub = lax.dynamic_slice_in_dim(att_cols, here, 1, 2).reshape(n * rows, seqs * out_rows)
-    w_out_grad = scatter_seq(dot_rows(att_sub, middle_low_all)).astype(f32)
+    w_out_grad = plain_scatter_seq(dot_rows(att_sub, middle_low_all)).astype(f32)
 
     query_acc, key_acc, value_acc = attention_back(
         query, key, value, pos_all, attended, lse, att_grad
@@ -210,7 +212,7 @@
     qkv_grad = jnp.concatenate(
         [rotate(query_acc, cosine, -sine), rotate(key_acc, cosine, -sine), value_acc], axis=1
     ).astype(bf16)
-    normed_grad = scatter_ctx(dot_cols(qkv_grad, qkv_sub))
+    normed_grad = plain_scatter_ctx(dot_cols(qkv_grad, qkv_sub))
     own_scale = own_rows(attn_scale)
     own_unit = hidden_in[0].astype(f32) * own_scale
     attn_term = normed_grad * gain1
@@ -241,10 +243,400 @@
     )
 
 
+class Box:
+    def __init__(self, value):
+        self.value = value
+
+
+def value_of(block):
+    return block.value if isinstance(block, Box) else block
+
+
+def order(block, *boxes):
+    values = lax.optimization_barrier((value_of(block),) + tuple(box.value for box in boxes))
+    for box, value in zip(boxes, values[1:]):
+        box.value = value
+    return values[0]
+
+
+class Link:
+    def __init__(self, axis, depth):
+        self.axis = axis
+        self.depth = depth
+        self.arrived = []
+
+    def swap(self, block, mask):
+        n = lax.axis_size(self.axis)
+        if len(self.arrived) >= self.depth:
+            before = order(block, self.arrived[-self.depth])
+            if isinstance(block, Box):
+                block.value = before
+            block = before
+        got = Box(lax.ppermute(value_of(block), self.axis, [(i, i ^ mask) for i in range(n)]))
+        self.arrived.append(got)
+        return got
+
+
+def place(pieces, places, columns=False):
+    pieces = [value_of(piece) for piece in pieces]
+    rows, width = pieces[0].shape
+    count = len(pieces)
+    shape = (rows, count * width) if columns else (count * rows, width)
+
+    def kernel(places_ref, *refs):
+        parts, whole, sems = refs[:count], refs[count], refs[count + 1]
+        copies = []
+        for i in range(count):
+            if columns:
+                there = whole.at[:, pl.ds(pl.multiple_of(places_ref[i] * width, width), width)]
+            else:
+                there = whole.at[pl.ds(pl.multiple_of(places_ref[i] * rows, rows), rows), :]
+            copies.append(pltpu.make_async_copy(parts[i], there, sems.at[i]))
+        for copy in copies:
+            copy.start()
+        for copy in copies:
+            copy.wait()
+
+    return pl.pallas_call(
+        kernel,
+        out_shape=jax.ShapeDtypeStruct(shape, pieces[0].dtype),
+        in_specs=[pl.BlockSpec(memory_space=pltpu.SMEM)]
+        + [pl.BlockSpec(memory_space=pl.ANY)] * count,
+        out_specs=pl.BlockSpec(memory_space=pltpu.VMEM),
+        scratch_shapes=[pltpu.SemaphoreType.DMA((count,))],
+        compiler_params=pltpu.CompilerParams(vmem_limit_bytes=32 * 1024 * 1024),
+        cost_estimate=pl.CostEstimate(flops=0, bytes_accessed=4 * rows * width * count, transcendentals=0),
+    )(jnp.stack(places).astype(jnp.int32), *pieces)
+
+
+def cut_columns(weights, groups, beside):
+    n = lax.axis_size("ctx")
+    rows = weights[0].shape[0]
+    width = weights[0].shape[1] // (n * groups)
+    arrays = list(weights) + ([] if beside is None else [beside])
+    total = len(weights) * groups * width + (0 if beside is None else beside.shape[1])
+
+    def kernel(*refs):
+        out = refs[-1]
+        for device in range(n):
+            at = 0
+            for weight in refs[: len(weights)]:
+                for group in range(groups):
+                    start = (group * n + device) * width
+                    out[device, :, at : at + width] = weight[:, start : start + width]
+                    at += width
+            if beside is not None:
+                out[device, :, at:] = refs[len(weights)][...]
+
+    vmem = pl.BlockSpec(memory_space=pltpu.VMEM)
+    return pl.pallas_call(
+        kernel,
+        out_shape=jax.ShapeDtypeStruct((n, rows, total), bf16),
+        in_specs=[vmem] * len(arrays),
+        out_specs=vmem,
+        compiler_params=pltpu.CompilerParams(vmem_limit_bytes=32 * 1024 * 1024),
+    )(*arrays)
+
+
+def paste_columns(blocks, count, groups, beside=0):
+    n, rows, total = blocks.shape
+    width = (total - beside) // (count * groups)
+    shapes = [jax.ShapeDtypeStruct((rows, groups * n * width), f32)] * count
+    if beside:
+        shapes.append(jax.ShapeDtypeStruct((rows, n * beside), f32))
+
+    def kernel(ref, *outs):
+        for device in range(n):
+            at = 0
+            for i in range(count):
+                for group in range(groups):
+                    start = (group * n + device) * width
+                    outs[i][:, start : start + width] = ref[device, :, at : at + width].astype(f32)
+                    at += width
+            if beside:
+                start = device * beside
+                outs[count][:, start : start + beside] = ref[device, :, at:].astype(f32)
+
+    vmem = pl.BlockSpec(memory_space=pltpu.VMEM)
+    return pl.pallas_call(
+        kernel,
+        out_shape=shapes,
+        in_specs=[vmem],
+        out_specs=[vmem] * len(shapes),
+        compiler_params=pltpu.CompilerParams(vmem_limit_bytes=32 * 1024 * 1024),
+    )(blocks)
+
+
+def gather_ctx(y, z, block):
+    two = z.swap(block, 2)
+    six = z.swap(block, 6)
+    one = y.swap(block, 1)
+    four = z.swap(six, 2)
+    held = [(0, block), (2, two), (6, six), (1, one), (4, four)]
+    for offset, part in ((3, two), (7, six), (5, four)):
+        held.append((offset, y.swap(part, 1)))
+    return held
+
+
+def gather_seq(x, here, block):
+    near = x.swap(block, 1)
+    far = x.swap(block, 2)
+    both = x.swap(far, 1)
+    return [(0, block), (1, near), (2, far), (3, both)]
+
+
+def scatter_ctx(y, z, total, here, beside=()):
+    beside = list(beside)
+
+    def after_next(block):
+        return order(block, *beside.pop(0)()) if beside else block
+
+    n = lax.axis_size("ctx")
+    rows = total.shape[0] // n
+    part = [lax.dynamic_slice_in_dim(total, (here ^ o) * rows, rows, 0) for o in range(n)]
+
+    def add(offset, got):
+        return part[offset].astype(f32) + got.value.astype(f32)
+
+    four = add(4, y.swap(part[5], 1))
+    two = add(2, y.swap(part[3], 1))
+    got_four = z.swap(four.astype(bf16), 2)
+    six = add(6, y.swap(after_next(part[7]), 1))
+    got_two = z.swap(two.astype(bf16), 2)
+    from_y = y.swap(part[1], 1)
+    got_six = z.swap(after_next((six + got_four.value.astype(f32)).astype(bf16)), 6)
+    return add(0, from_y) + got_two.value.astype(f32) + got_six.value.astype(f32)
+
+
+def scatter_ctx_grouped(y, z, total, here):
+    n = lax.axis_size("ctx")
+    rows = total.shape[0] // n
+    offsets = [0, 6, 2, 4, 1, 7, 3, 5]
+    left = [lax.dynamic_slice_in_dim(total, (here ^ o) * rows, rows, 0) for o in offsets]
+    for link, mask in ((y, 1), (z, 2), (z, 6)):
+        half = len(left) // 2
+        got = link.swap(jnp.concatenate(left[half:], axis=0).astype(bf16), mask)
+        left = [
+            part + got.value[i * rows : (i + 1) * rows].astype(f32)
+            for i, part in enumerate(left[:half])
+        ]
+    return left[0]
+
+
+def scatter_seq_near(x, total, here):
+    rows = total.shape[0] // 4
+
+    def piece(offset):
+        return lax.dynamic_slice_in_dim(total, (here ^ offset) * rows, rows, 0)
+
+    got = x.swap(jnp.concatenate([piece(3), piece(1)], axis=0).astype(bf16), 1)
+    return piece(0) + got.value[rows:].astype(f32), (
+        piece(2) + got.value[:rows].astype(f32)
+    ).astype(bf16)
+
+
+def to_owners(part, count, groups, beside=0):
+    n = lax.axis_size("ctx")
+    blocks = lax.all_to_all(part.reshape(n, -1, part.shape[1]), "ctx", 0, 0, tiled=True)
+    return paste_columns(blocks, count, groups, beside)
+
+
+def scatter_halves(y, z, total, here, beside=()):
+    n = lax.axis_size("ctx")
+    parts = total.reshape(n, 2, -1, total.shape[1])
+    first = lax.psum_scatter(
+        parts[:, 0].reshape(-1, total.shape[1]), "ctx", scatter_dimension=0, tiled=True
+    )
+    second = scatter_ctx(y, z, parts[:, 1].reshape(-1, total.shape[1]), here, beside)
+    return jnp.concatenate([first.astype(f32), second], axis=0)
+
+
+def tuned(
+    hidden_in,
+    positions,
+    attn_gain,
+    w_query,
+    w_key,
+    w_value,
+    w_out,
+    mlp_gain,
+    w_gate,
+    w_up,
+    w_down,
+    out_grad,
+):
+    n = lax.axis_size("ctx")
+    seqs = lax.axis_size("seq")
+    here = lax.axis_index("ctx")
+    seq_here = lax.axis_index("seq")
+    rows = hidden_in.shape[1]
+    weight_rows = w_query.shape[0]
+    y, z, x = Link("ctx", 2), Link("ctx", 2), Link("seq", 1)
+
+    def own_rows(whole):
+        return lax.dynamic_slice_in_dim(whole, here * rows, rows, 0)
+
+    def from_devices(held, index=here):
+        return place([part for _, part in held], [index ^ o for o, _ in held])
+
+    own_pos = positions[0].reshape(weight_rows, -1)
+    per_row = own_pos.shape[1]
+    beside = jnp.concatenate(
+        [
+            attn_gain[:, None],
+            mlp_gain[:, None],
+            (own_pos // 64).astype(bf16),
+            (own_pos % 64).astype(bf16),
+        ],
+        axis=1,
+    )
+    beside = jnp.pad(beside, ((0, 0), (0, 128 - beside.shape[1])))
+    x_low = lax.all_gather(hidden_in[0], "ctx", axis=0, tiled=True)
+    blocks = cut_columns((w_query, w_key, w_value), 1, beside)
+    qkv_mine = lax.all_to_all(blocks, "ctx", 0, 0, tiled=True).reshape(n * weight_rows, -1)
+    late_gate, late_up, late_out, late_down, qkv_mine = lax.optimization_barrier(
+        (w_gate, w_up, w_out, w_down, qkv_mine)
+    )
+    full_out = lax.all_gather(late_out, ("seq", "ctx"), axis=0, tiled=True)
+    qkv_steps = gather_seq(x, seq_here, qkv_mine)
+    down_steps = gather_seq(x, seq_here, late_down)
+    blocks = cut_columns((late_gate, late_up), seqs, None)
+    gate_up = lax.all_to_all(blocks, "ctx", 0, 0, tiled=True).reshape(n * weight_rows, -1)
+    gate_up_steps = gather_seq(x, seq_here, gate_up)
+    qkv_sub = from_devices(qkv_steps, seq_here)
+    down_sub = from_devices(down_steps, seq_here)
+    gate_up = from_devices(gate_up_steps, seq_here)
+    pos_cuts = qkv_mine[:, -128:].astype(jnp.int32)
+    pos_all = pos_cuts[:, 2 : 2 + per_row] * 64 + pos_cuts[:, 2 + per_row : 2 + 2 * per_row]
+    pos_all = pos_all.reshape(-1)
+    gain1 = qkv_sub[:, -128].astype(f32)
+    gain2 = qkv_sub[:, -127].astype(f32)
+    qkv_sub = qkv_sub[:, :-128]
+
+    x_all = x_low.astype(f32)
+    attn_scale = rms_scale(x_all)
+    normed = (x_all * attn_scale * gain1).astype(bf16)
+    angles = angle_table(pos_all)
+    cosine, sine = jnp.cos(angles), jnp.sin(angles)
+    qkv = dot(normed, qkv_sub)
+    width = qkv.shape[1] // 3
+    query = rotate(qkv[:, :width], cosine, sine).astype(bf16)
+    key = rotate(qkv[:, width : 2 * width], cosine, sine).astype(bf16)
+    value = qkv[:, 2 * width :].astype(bf16)
+    attended, lse = attention(query, key, value, pos_all)
+    att_held = gather_ctx(y, z, attended.astype(bf16))
+    att_low = place([part for _, part in att_held], [here ^ o for o, _ in att_held], columns=True)
+    late_grad, att_low = lax.optimization_barrier((out_grad[0], att_low))
+    grad_all = lax.all_gather(late_grad, "ctx", axis=0, tiled=True)
+
+    middle = x_all + dot(att_low, full_out)
+    mlp_scale = rms_scale(middle)
+    normed_mid = (middle * mlp_scale * gain2).astype(bf16)
+    gate_up_act = dot(normed_mid, gate_up)
+    units = gate_up.shape[1] // 2
+    gate_act, up_act = gate_up_act[:, :units], gate_up_act[:, units:]
+    sig = jax.nn.sigmoid(gate_act)
+    inner = (gate_act * sig * up_act).astype(bf16)
+    middle_own = own_rows(middle)
+
+    inner_grad = dot_cols(grad_all, down_sub)
+    gate_grad = (inner_grad * up_act * sig * (1.0 + gate_act * (1.0 - sig))).astype(bf16)
+    up_grad = (inner_grad * gate_act * sig).astype(bf16)
+    gate_up_grad = jnp.concatenate([gate_grad, up_grad], axis=1)
+    mid_grad_part = dot_cols(gate_up_grad, gate_up).astype(bf16)
+    gate_up_near, gate_up_far = scatter_seq_near(x, dot_rows(normed_mid, gate_up_grad), seq_here)
+    gate_up_far = Box(gate_up_far)
+    mid_grad_in = scatter_halves(y, z, mid_grad_part, here, [lambda: [gate_up_far]])
+    gate_up_far = x.swap(gate_up_far, 2)
+    down_weight_part = dot_rows(inner, grad_all)
+    down_part = dot(inner, down_sub).astype(bf16)
+    mid_grad_in, down_weight_part, down_part = lax.optimization_barrier(
+        (mid_grad_in, down_weight_part, down_part)
+    )
+    down_own = lax.psum_scatter(down_part, "ctx", scatter_dimension=0, tiled=True)
+
+    mid_scale = own_rows(mlp_scale)
+    mid_unit = middle_own * mid_scale
+    mid_term = mid_grad_in * gain2
+    middle_grad = out_grad[0].astype(f32) + mid_scale * (
+        mid_term - mid_unit * jnp.mean(mid_unit * mid_term, axis=-1, keepdims=True)
+    )
+    mlp_gain_part = jnp.sum(mid_grad_in * mid_unit, axis=0)
+    middle_low = middle_grad.astype(bf16)
+    att_grad = dot_cols(middle_low, full_out).astype(bf16)
+    blocks = cut_columns((att_grad,), 1, None)
+    att_grad = lax.all_to_all(blocks, "ctx", 0, 0, tiled=True).reshape(n * rows, -1)
+    w_out_part = dot_rows(own_rows(att_low), middle_low)
+    down_weight_near, down_weight_far = scatter_seq_near(x, down_weight_part, seq_here)
+    att_grad, w_out_part, gate_up_far.value, down_weight_far = lax.optimization_barrier(
+        (att_grad, w_out_part, gate_up_far.value, down_weight_far)
+    )
+    down_weight_far = x.swap(down_weight_far, 2)
+    w_out_near, w_out_far = scatter_seq_near(x, w_out_part, seq_here)
+    gate_up_sum = (gate_up_near + gate_up_far.value.astype(f32)).astype(bf16)
+    w_gate_grad, w_up_grad = to_owners(gate_up_sum, 2, seqs)
+
+    query_acc, key_acc, value_acc = attention_back(
+        query, key, value, pos_all, attended, lse, att_grad
+    )
+    qkv_grad = jnp.concatenate(
+        [rotate(query_acc, cosine, -sine), rotate(key_acc, cosine, -sine), value_acc], axis=1
+    ).astype(bf16)
+    qkv_grad, down_weight_far.value, w_out_far, down_own = lax.optimization_barrier(
+        (qkv_grad, down_weight_far.value, w_out_far, down_own)
+    )
+    hidden_out = (middle_own + down_own.astype(f32)).astype(bf16)
+    w_down_grad = down_weight_near + down_weight_far.value.astype(f32)
+    w_out_far = x.swap(w_out_far, 2)
+    normed_grad_part = dot_cols(qkv_grad, qkv_sub)
+    attn_gain_part = jnp.sum(normed_grad_part * (x_all * attn_scale), axis=0)
+    beside = jnp.stack([attn_gain_part, mlp_gain_part], axis=1)
+    beside = jnp.pad(beside, ((0, 0), (0, 126)))
+    qkv_part = jnp.concatenate([dot_rows(normed, qkv_grad), beside], axis=1)
+    x_again = Link("seq", 1)
+    qkv_near, qkv_far = scatter_seq_near(x_again, qkv_part, seq_here)
+    qkv_far, qkv_sum = Box(qkv_far), Box(None)
+
+    def add_far():
+        far = x_again.swap(qkv_far, 2)
+        qkv_sum.value = (qkv_near + far.value.astype(f32)).astype(bf16)
+        return [qkv_sum]
+
+    normed_grad = scatter_halves(
+        y, z, normed_grad_part.astype(bf16), here, [lambda: [qkv_far], add_far]
+    )
+    w_query_grad, w_key_grad, w_value_grad, gain_grads = to_owners(qkv_sum.value, 3, 1, 128)
+    gain_grads = gain_grads.astype(f32).reshape(weight_rows, n, 128).sum(axis=1)
+    w_out_far, normed_grad = lax.optimization_barrier((w_out_far.value, normed_grad))
+    w_out_sum = w_out_near + w_out_far.astype(f32)
+    w_out_grad = scatter_ctx_grouped(y, z, w_out_sum, here)
+
+    own_scale = own_rows(attn_scale)
+    own_unit = hidden_in[0].astype(f32) * own_scale
+    attn_term = normed_grad * gain1
+    hidden_grad = middle_grad + own_scale * (
+        attn_term - own_unit * jnp.mean(own_unit * attn_term, axis=-1, keepdims=True)
+    )
+    return (
+        hidden_out[None],
+        hidden_grad[None],
+        gain_grads[:, 0],
+        w_query_grad,
+        w_key_grad,
+        w_value_grad,
+        w_out_grad,
+        gain_grads[:, 1],
+        w_gate_grad,
+        w_up_grad,
+        w_down_grad,
+    )
+
+
 def solution(mesh):
     tokens = P("seq", "ctx", None)
     whole = P(("seq", "ctx"), None)
     gain = P(("seq", "ctx"))
+    local = tuned if mesh.shape["ctx"] == 8 and mesh.shape["seq"] == 4 else plain
     return jax.shard_map(
         local,
         mesh=mesh,

time: 1340 us -> 767 us (0.57)
  waiting for transfers between devices: 866 us -> 313 us
  blocking collectives: 222 us -> 47.2 us
  other arithmetic: 25.9 us -> 86.4 us
  starting transfers between devices: 15.1 us -> 62.1 us
  local copies, waits for them, and re-layouts: 33.7 us -> 59.6 us
  Pallas kernels: 0 us -> 14.6 us
    reduce_scatter x7 -> x3, waiting for transfers between devices: 421 us -> 30.4 us  [the longest x2 30.4 us: scatter_halves(): lax.psum_scatter(parts[:, 0].reshape(-1, total.shape[1]), 'ctx', scatter_...]
    all_gather x8 -> x3, waiting for transfers between devices: 293 us -> 29.7 us  [the longest x1 29.7 us: tuned(): grad_all = lax.all_gather(late_grad, 'ctx', axis=0, tiled=True)]
    ppermute x0 -> x41, waiting for transfers between devices: none -> 222 us  [swap(): lax.ppermute(value_of(block), self.axis, [(i, i ^ mask) for i in range(n)])]
    unnamed x17 -> x6, waiting for transfers between devices: 137 us -> 0.76 us
    all_to_all x2 -> x1, blocking collectives: 139 us -> 47.2 us  [tuned(): lax.all_to_all(blocks, 'ctx', 0, 0, tiled=True).reshape(n * weight_rows, -1)]
    all_gather x2 -> x0, blocking collectives: 82.2 us -> none  [the longest x1 63.2 us: local(): lax.all_gather(jnp.stack([attn_gain, mlp_gain]), ('seq', 'ctx'), axis=1,...]
    ppermute x0 -> x41, starting transfers between devices: none -> 41.8 us  [swap(): lax.ppermute(value_of(block), self.axis, [(i, i ^ mask) for i in range(n)])]
    convert_element_type x3 -> x17, other arithmetic: 6.27 us -> 35.7 us  [the longest x4 16 us: scatter_seq_near(): return (piece(0) + got.value[rows:].astype(f32), (piece(2) + got.value[:r...]
  transfers between devices with their start and end apart: 19 -> 51, of which waited for: 14 -> 27; matrix products, arithmetic and copies ran while one was open for 8% -> 29% of each run, Pallas kernels for 0% -> 2%
where the time goes in v3:
time: 767 us; the launch traced here: 755 us
  waiting for transfers between devices  313 us (41%)
  matrix products  157 us (20%)
  other arithmetic  86.4 us (11%)
  starting transfers between devices  62.1 us (8%)
  local copies, waits for them, and re-layouts  59.6 us (8%)
  blocking collectives  47.2 us (6%)
  between operations  15.5 us (2%)
  Pallas kernels  14.6 us (2%)
    ppermute x41, waiting for transfers between devices, swap(): lax.ppermute(value_of(block), self.axis, [(i, i ^ mask) for i in range(n)])  222 us
    all_to_all x1, blocking collectives, tuned(): lax.all_to_all(blocks, 'ctx', 0, 0, tiled=True).reshape(n * weight_rows, -1)  47.2 us
    dot_general x4, matrix products, dot(): return jnp.dot(left, right, preferred_element_type=f32)  41.9 us
    ppermute x41, starting transfers between devices, swap(): lax.ppermute(value_of(block), self.axis, [(i, i ^ mask) for i in range(n)])  41.8 us
    dot_general x4, matrix products, dot_cols(): lax.dot_general(left, right, (((1,), (1,)), ((), ())), preferred_element_...  38.5 us
    dot_general x4, matrix products, dot_rows(): lax.dot_general(left, right, (((0,), (0,)), ((), ())), preferred_element_...  37.4 us
    unnamed x124, local copies, waits for them, and re-layouts  37.2 us
    reduce_scatter x2, waiting for transfers between devices, scatter_halves(): lax.psum_scatter(parts[:, 0].reshape(-1, total.shape[1]), 'ctx', scatter_...  30.4 us
  transfers between devices with their start and end apart: 51, of which 27 were waited for; matrix products, arithmetic and copies ran while one was open for 29% of the time, Pallas kernels for 2%

profile of v3, /device:TPU:0, one launch (start us, length us, event | category | flops | bytes accessed | tf_op | source)
XLA Modules:
  0.0 755.4 jit_solution(12189551480979397404)
XLA Ops:
  13.9 47.2 %all_to_all.25 = bf16[8,64,896]{2,1,0:T(8,128)(2,1)S(1)} all-to-all(bf16[8,64,896]{2,1,0:T(8,128)(2,1)S(1)} %shard_map.203), channel_id=1, replica_groups=mesh['seq'=4,'ctx'=8] {'ctx'}, dimensions={0} | all-to-all | bytes 1835008 | tf_op jit(solution)/shard_map/all_to_all | solution.py:496
  66.1 20.9 %collective-permute-done.1.refs_2_ = bf16[512,896]{1,0:T(8,128)(2,1)S(1)} collective-permute-done((bf16[512,896]{1,0:T(8,128)(2,1)S(1)}, bf16[512,896]{1,0:T(8,128)(2,1)S(1)}, u32[]{:S(2)}, u32[]{:S(2)}) %collective-permute-start.1) | collective-permute-done | bytes 917536 | tf_op jit(solution)/shard_map/ppermute | solution.py:275
  108.1 13.6 %collective-permute-done.11.refs_2_ = bf16[256,2048]{1,0:T(8,128)(2,1)} collective-permute-done((bf16[256,2048]{1,0:T(8,128)(2,1)}, bf16[256,2048]{1,0:T(8,128)(2,1)}, u32[]{:S(2)}, u32[]{:S(2)}) %collective-permute-start.11) | collective-permute-done | bytes 1048608 | tf_op jit(solution)/shard_map/ppermute | solution.py:275
  140.7 13.5 %all-to-all-done.1 = bf16[8,64,2048]{2,1,0:T(8,128)(2,1)S(1)} async-done(((bf16[8,64,2048]{2,1,0:T(8,128)(2,1)}), bf16[8,64,2048]{2,1,0:T(8,128)(2,1)S(1)}, u32[]{:S(2)}, u32[]{:S(2)}) %all-to-all-start.1) | async-done | bytes 2097184 | tf_op jit(solution)/shard_map/all_to_all | solution.py:504
  176.3 21.8 %collective-permute-done.4.refs_1_ = bf16[1024,256]{1,0:T(8,128)(2,1)S(1)} collective-permute-done((bf16[1024,256]{1,0:T(8,128)(2,1)S(1)}, bf16[1024,256]{1,0:T(8,128)(2,1)S(1)}, u32[]{:S(2)}, u32[]{:S(2)}) %collective-permute-start.4) | collective-permute-done | bytes 524320 | tf_op jit(solution)/shard_map/ppermute | solution.py:275
  198.1 13.6 %collective-permute-done.3.refs_2_ = bf16[1024,256]{1,0:T(8,128)(2,1)} collective-permute-done((bf16[1024,256]{1,0:T(8,128)(2,1)S(1)}, bf16[1024,256]{1,0:T(8,128)(2,1)}, u32[]{:S(2)}, u32[]{:S(2)}) %collective-permute-start.3) | collective-permute-done | bytes 524320 | tf_op jit(solution)/shard_map/ppermute | solution.py:275
  214.5 12.0 %collective-permute-done.7.refs_5_ = bf16[1024,256]{1,0:T(8,128)(2,1)S(1)} collective-permute-done((bf16[1024,256]{1,0:T(8,128)(2,1)S(1)}, bf16[1024,256]{1,0:T(8,128)(2,1)S(1)}, u32[]{:S(2)}, u32[]{:S(2)}) %collective-permute-start.7) | collective-permute-done | bytes 524320 | tf_op jit(solution)/shard_map/ppermute | solution.py:275
  237.1 10.4 %collective-permute-done.9.refs_7_ = bf16[1024,256]{1,0:T(8,128)(2,1)} collective-permute-done((bf16[1024,256]{1,0:T(8,128)(2,1)}, bf16[1024,256]{1,0:T(8,128)(2,1)}, u32[]{:S(2)}, u32[]{:S(2)}) %collective-permute-start.9) | collective-permute-done | bytes 524320 | tf_op jit(solution)/shard_map/ppermute | solution.py:275
  267.2 15.6 %multiply_reduce_fusion = (f32[1024]{0:T(1024)S(1)}, f32[1024,2048]{1,0:T(8,128)}) fusion(bf16[1024,2048]{1,0:T(8,128)(2,1)} %copy-done.5, bf16[2048,2048]{1,0:T(8,128)(2,1)} %all-gather.5.cloned.1.call-done, bf16[1,1024,2048]{2,1,0:T(8,128)(2,1)} %all-gather.9.cloned.1.call-done), kind=kOutput, calls=%fused_computation.20 | convolution fusion | flops 8598322176 | bytes 25169920 | tf_op jit(solution)/shard_map/dot_general | solution.py:65
  282.8 14.0 %fusion.70 = f32[1024,2048]{0,1:T(8,128)} fusion(bf16[2048,2048]{1,0:T(8,128)(2,1)S(1)} %copy-done.1, f32[1024,2048]{1,0:T(8,128)} %get-tuple-element.224, f32[2048]{0:T(1024)S(1)} %get-tuple-element.161, f32[1024]{0:T(1024)S(1)} %add_rsqrt_fusion), kind=kOutput, calls=%fused_computation.179 | convolution fusion | flops 8596226048 | bytes 25178112 | tf_op jit(solution)/shard_map/dot_general | solution.py:65
  296.8 29.7 %all-gather.7.cloned.1.call-done = bf16[1024,2048]{1,0:T(8,128)(2,1)} async-done(((bf16[128,2048]{1,0:T(8,128)(2,1)}), bf16[1024,2048]{1,0:T(8,128)(2,1)}) %all-gather.7.cloned.1.call-update) | async-done | bytes 4194320 | tf_op jit(solution)/shard_map/all_gather | solution.py:530
  326.5 13.3 %multiply_convert_fusion.4 = (bf16[1024,1024]{0,1:T(8,128)(2,1)S(1)}, bf16[1024,1024]{0,1:T(8,128)(2,1)S(1)}, bf16[1024,1024]{0,1:T(8,128)(2,1)}) fusion(f32[1024,2048]{0,1:T(8,128)} %fusion.70, bf16[1024,2048]{1,0:T(8,128)(2,1)} %all-gather.7.cloned.1.call-done, bf16[1024,2048]{1,0:T(8,128)(2,1)} %copy-done.6), kind=kOutput, calls=%fused_computation.42 | convolution fusion | flops 4311744512 | bytes 23068672 | tf_op jit(solution)/shard_map/dot_general | solution.py:73
  339.8 13.9 %fusion.18 = f32[2048,2048]{1,0:T(8,128)} fusion(bf16[1024,1024]{0,1:T(8,128)(2,1)S(1)} %get-tuple-element.170, bf16[1024,1024]{0,1:T(8,128)(2,1)S(1)} %get-tuple-element.169, f32[1024,2048]{1,0:T(8,128)S(1)} %copy-done.42, f32[2048]{0:T(1024)S(1)} %get-tuple-element.161, f32[1024]{0:T(1024)S(1)} %add_rsqrt_fusion), kind=kOutput, calls=%fused_computation.50 | convolution fusion | flops 8604614656 | bytes 29372416 | tf_op jit(solution)/shard_map/dot_general | solution.py:69
  361.7 10.9 %convolution_convert_fusion = bf16[1024,2048]{1,0:T(8,128)(2,1)} fusion(bf16[2048,2048]{1,0:T(8,128)(2,1)S(1)} %bitcast.97, bf16[1024,1024]{0,1:T(8,128)(2,1)S(1)} %get-tuple-element.170, bf16[1024,1024]{0,1:T(8,128)(2,1)S(1)} %get-tuple-element.169), kind=kOutput, calls=%fused_computation.44 | convolution fusion | flops 8600420352 | bytes 16777216 | tf_op jit(solution)/shard_map/dot_general | solution.py:73
  416.4 10.6 %fusion.75 = f32[1024,2048]{1,0:T(8,128)} fusion(bf16[1024,1024]{0,1:T(8,128)(2,1)} %get-tuple-element.175, bf16[1024,2048]{1,0:T(8,128)(2,1)} %all-gather.7.cloned.1.call-done), kind=kOutput, calls=%fused_computation.184 | convolution fusion | flops 4294967296 | bytes 14680064 | tf_op jit(solution)/shard_map/dot_general | solution.py:69
  427.1 21.0 %reduce-scatter.4.cloned.1.call-done = bf16[64,2048]{1,0:T(8,128)(2,1)} async-done(((bf16[512,2048]{1,0:T(8,128)(2,1)}), bf16[64,2048]{1,0:T(8,128)(2,1)}) %reduce-scatter.4.cloned.1.call-update) | async-done | bytes 262160 | tf_op jit(solution)/shard_map/reduce_scatter | solution.py:447
  471.2 9.4 %fusion.52 = f32[2048,2048]{1,0:T(8,128)} fusion(bf16[1024,2048]{1,0:T(8,128)(2,1)} %copy-done.5, s32[]{:T(128)S(6)} %select_n.100, f32[128,2048]{1,0:T(8,128)S(1)} %multiply_add_fusion), kind=kOutput, calls=%fused_computation.123 | convolution fusion | flops 1074003968 | bytes 18350084 | tf_op jit(solution)/shard_map/dot_general | solution.py:69
  483.8 16.3 %all-to-all-done.2 = bf16[8,128,256]{2,1,0:T(8,128)(2,1)S(1)} async-done(((bf16[8,128,256]{2,1,0:T(8,128)(2,1)}), bf16[8,128,256]{2,1,0:T(8,128)(2,1)S(1)}, u32[]{:S(2)}, u32[]{:S(2)}) %all-to-all-start.2) | async-done | bytes 524320 | tf_op jit(solution)/shard_map/all_to_all | solution.py:568
  507.2 17.5 %collective-permute-done.26 = bf16[256,2048]{1,0:T(8,128)(2,1)} collective-permute-done((bf16[256,2048]{1,0:T(8,128)(2,1)}, bf16[256,2048]{1,0:T(8,128)(2,1)}, u32[]{:S(2)}, u32[]{:S(2)}) %collective-permute-start.26) | collective-permute-done | bytes 1048608 | tf_op jit(solution)/shard_map/ppermute | solution.py:275
  524.7 12.3 %multiply_convert_fusion = bf16[4,1024,1024]{1,2,0:T(8,128)(2,1)S(1)} fusion(f32[4,1024,1024]{1,2,0:T(8,128)} %get-tuple-element.220, bf16[1024,4,64]{0,2,1:T(8,128)(2,1)} %bitcast.122, bf16[1024,4,64]{0,2,1:T(8,128)(2,1)} %bitcast.129, f32[4,1024]{1,0:T(4,128)} %bitcast.134, f32[4,1024]{1,0:T(4,128)} %log_add_fusion, pred[1024,1024]{0,1:T(8,128)(4,1)S(1)} %copy-done.34), kind=kOutput, calls=%fused_computation | convolution fusion | flops 562036736 | bytes 27295744 | tf_op jit(solution)/shard_map/qhd,khd->hqk/dot_general | solution.py:118
  616.7 30.0 %collective-permute-done.36 = bf16[512,896]{0,1:T(8,128)(2,1)} collective-permute-done((bf16[512,896]{0,1:T(8,128)(2,1)}, bf16[512,896]{0,1:T(8,128)(2,1)}, u32[]{:S(2)}, u32[]{:S(2)}) %collective-permute-start.36) | collective-permute-done | bytes 917536 | tf_op jit(solution)/shard_map/ppermute | solution.py:275
  651.9 11.4 %collective-permute-done.37 = bf16[64,2048]{1,0:T(8,128)(2,1)S(1)} collective-permute-done((bf16[64,2048]{1,0:T(8,128)(2,1)S(1)}, bf16[64,2048]{1,0:T(8,128)(2,1)S(1)}, u32[]{:S(2)}, u32[]{:S(2)}) %collective-permute-start.37) | collective-permute-done | bytes 262176 | tf_op jit(solution)/shard_map/ppermute | solution.py:275
  665.1 9.4 %reduce-scatter.8.cloned.1.call-done = bf16[64,2048]{1,0:T(8,128)(2,1)} async-done(((bf16[512,2048]{1,0:T(8,128)(2,1)}), bf16[64,2048]{1,0:T(8,128)(2,1)}) %reduce-scatter.8.cloned.1.call-update) | async-done | bytes 262160 | tf_op jit(solution)/shard_map/reduce_scatter | solution.py:447
  701.8 13.7 %collective-permute-done.38 = bf16[256,2048]{1,0:T(8,128)(2,1)} collective-permute-done((bf16[256,2048]{1,0:T(8,128)(2,1)}, bf16[256,2048]{1,0:T(8,128)(2,1)}, u32[]{:S(2)}, u32[]{:S(2)}) %collective-permute-start.38) | collective-permute-done | bytes 1048608 | tf_op jit(solution)/shard_map/ppermute | solution.py:275
  (320 shorter events, 337.9 us)
Async XLA Ops:
  7.2 114.5 %all-gather.9.cloned.1.call-start = ((), (), s32[]{:S(2)}) async-start(), calls=%async_computation.13 | async-start | bytes 4718592 | tf_op jit(solution)/shard_map/all_gather | solution.py:494
  7.9 259.3 %all-gather.5.cloned.1.call-start = ((), (), s32[]{:S(2)}) async-start(), calls=%async_computation.8 | async-start | bytes 8650752 | tf_op jit(solution)/shard_map/all_gather | solution.py:500
  92.2 62.0 %all-to-all-start.1 = ((bf16[8,64,2048]{2,1,0:T(8,128)(2,1)}), bf16[8,64,2048]{2,1,0:T(8,128)(2,1)S(1)}, u32[]{:S(2)}, u32[]{:S(2)}) async-start(bf16[8,64,2048]{2,1,0:T(8,128)(2,1)} %copy-done.2), calls=%async_computation.1 | async-start | bytes 4194304 | tf_op jit(solution)/shard_map/all_to_all | solution.py:504
  95.8 230.7 %all-gather.7.cloned.1.call-start = ((), (), s32[]{:S(2)}) async-start(), calls=%async_computation.9 | async-start | bytes 4718592 | tf_op jit(solution)/shard_map/all_gather | solution.py:530
  121.7 32.5 %collective-permute-start.12 = (bf16[256,2048]{1,0:T(8,128)(2,1)}, bf16[256,2048]{1,0:T(8,128)(2,1)S(1)}, u32[]{:S(2)}, u32[]{:S(2)}) collective-permute-start(bf16[256,2048]{1,0:T(8,128)(2,1)} %collective-permute-done.11.refs_2_), channel_id=1, source_target_pairs={{0,8},{8,0},{16,24},{24,16},{1,9},{9,1},{17,25},{25,17},{2,10},{10... | collective-permute-start | bytes 3145736 | tf_op jit(solution)/shard_map/ppermute | solution.py:275
  172.8 38.9 %collective-permute-start.3 = (bf16[1024,256]{1,0:T(8,128)(2,1)S(1)}, bf16[1024,256]{1,0:T(8,128)(2,1)}, u32[]{:S(2)}, u32[]{:S(2)}) collective-permute-start(bf16[1024,256]{1,0:T(8,128)(2,1)S(1)} %copy.85.refs_0_), channel_id=1, source_target_pairs={{0,6},{1,7},{2,4},{3,5},{4,2},{5,3},{6,0},{7,1},{8,14},{9,15},{10,... | collective-permute-start | bytes 1572872 | tf_op jit(solution)/shard_map/ppermute | solution.py:275
  174.3 80.0 %collective-permute-start.14 = (bf16[512,2048]{1,0:T(8,128)(2,1)S(1)}, bf16[512,2048]{1,0:T(8,128)(2,1)}, u32[]{:S(2)}, u32[]{:S(2)}) collective-permute-start(bf16[512,2048]{1,0:T(8,128)(2,1)S(1)} %bitcast.99), channel_id=1, source_target_pairs={{0,16},{8,24},{16,0},{24,8},{1,17},{9,25},{17,1},{25,9},{2,18},{10... | collective-permute-start | bytes 6291464 | tf_op jit(solution)/shard_map/ppermute | solution.py:275
  175.8 37.4 %collective-permute-start.5 = (bf16[1024,256]{1,0:T(8,128)(2,1)S(1)}, bf16[1024,256]{1,0:T(8,128)(2,1)S(1)}, u32[]{:S(2)}, u32[]{:S(2)}) collective-permute-start(bf16[1024,256]{1,0:T(8,128)(2,1)S(1)} %copy.85.refs_0_), channel_id=1, source_target_pairs={{0,1},{1,0},{2,3},{3,2},{4,5},{5,4},{6,7},{7,6},{8,9},{9,8},{10,11... | collective-permute-start | bytes 1572872 | tf_op jit(solution)/shard_map/ppermute | solution.py:275
  254.1 194.0 %reduce-scatter.4.cloned.1.call-start = ((), (), s32[]{:S(2)}) async-start(), calls=%async_computation.10 | async-start | bytes 2359296 | tf_op jit(solution)/shard_map/reduce_scatter | solution.py:447
  360.7 35.0 %collective-permute-start.19 = (bf16[1024,2048]{1,0:T(8,128)(2,1)}, bf16[1024,2048]{1,0:T(8,128)(2,1)}, u32[]{:S(2)}, u32[]{:S(2)}) collective-permute-start(bf16[1024,2048]{1,0:T(8,128)(2,1)} %pad_maximum_fusion.1), channel_id=1, source_target_pairs={{0,8},{8,0},{16,24},{24,16},{1,9},{9,1},{17,25},{25,17},{2,10},{10... | collective-permute-start | bytes 12582920 | tf_op jit(solution)/shard_map/ppermute | solution.py:275
  376.6 182.3 %reduce-scatter.6.cloned.1.call-start = ((), (), s32[]{:S(2)}) async-start(), calls=%async_computation.11 | async-start | bytes 4718592 | tf_op jit(solution)/shard_map/reduce_scatter | solution.py:556
  408.2 40.9 %collective-permute-start.17 = (bf16[64,2048]{1,0:T(8,128)(2,1)S(1)}, bf16[64,2048]{1,0:T(8,128)(2,1)S(1)}, u32[]{:S(2)}, u32[]{:S(2)}) collective-permute-start(bf16[64,2048]{1,0:T(8,128)(2,1)S(1)} %get-tuple-element.109), channel_id=1, source_target_pairs={{0,1},{1,0},{2,3},{3,2},{4,5},{5,4},{6,7},{7,6},{8,9},{9,8},{10,11... | collective-permute-start | bytes 786440 | tf_op jit(solution)/shard_map/ppermute | solution.py:275
  409.7 39.4 %collective-permute-start.18 = (bf16[64,2048]{1,0:T(8,128)(2,1)S(1)}, bf16[64,2048]{1,0:T(8,128)(2,1)S(1)}, u32[]{:S(2)}, u32[]{:S(2)}) collective-permute-start(bf16[64,2048]{1,0:T(8,128)(2,1)S(1)} %get-tuple-element.110), channel_id=1, source_target_pairs={{0,2},{1,3},{2,0},{3,1},{4,6},{5,7},{6,4},{7,5},{8,10},{9,11},{10,... | collective-permute-start | bytes 786440 | tf_op jit(solution)/shard_map/ppermute | solution.py:275
  411.1 45.1 %collective-permute-start.24 = (bf16[512,2048]{1,0:T(8,128)(2,1)}, bf16[512,2048]{1,0:T(8,128)(2,1)}, u32[]{:S(2)}, u32[]{:S(2)}) collective-permute-start(bf16[512,2048]{1,0:T(8,128)(2,1)} %add_convert_fusion.2), channel_id=1, source_target_pairs={{0,16},{8,24},{16,0},{24,8},{1,17},{9,25},{17,1},{25,9},{2,18},{10... | collective-permute-start | bytes 6291464 | tf_op jit(solution)/shard_map/ppermute | solution.py:275
  414.4 34.8 %collective-permute-start.23 = (bf16[64,2048]{1,0:T(8,128)(2,1)}, bf16[64,2048]{1,0:T(8,128)(2,1)S(1)}, u32[]{:S(2)}, u32[]{:S(2)}) collective-permute-start(bf16[64,2048]{1,0:T(8,128)(2,1)} %add_convert_fusion.13), channel_id=1, source_target_pairs={{0,6},{1,7},{2,4},{3,5},{4,2},{5,3},{6,0},{7,1},{8,14},{9,15},{10,... | collective-permute-start | bytes 786440 | tf_op jit(solution)/shard_map/ppermute | solution.py:275
  466.8 33.2 %all-to-all-start.2 = ((bf16[8,128,256]{2,1,0:T(8,128)(2,1)}), bf16[8,128,256]{2,1,0:T(8,128)(2,1)S(1)}, u32[]{:S(2)}, u32[]{:S(2)}) async-start(bf16[8,128,256]{2,1,0:T(8,128)(2,1)} %shard_map.209), calls=%async_computation.3 | async-start | bytes 1048576 | tf_op jit(solution)/shard_map/all_to_all | solution.py:568
  471.1 203.4 %reduce-scatter.8.cloned.1.call-start = ((), (), s32[]{:S(2)}) async-start(), calls=%async_computation.12 | async-start | bytes 2359296 | tf_op jit(solution)/shard_map/reduce_scatter | solution.py:447
  579.7 97.0 %collective-permute-start.28 = (bf16[512,2048]{1,0:T(8,128)(2,1)}, bf16[512,2048]{1,0:T(8,128)(2,1)}, u32[]{:S(2)}, u32[]{:S(2)}) collective-permute-start(bf16[512,2048]{1,0:T(8,128)(2,1)} %add_convert_fusion.1), channel_id=1, source_target_pairs={{0,16},{8,24},{16,0},{24,8},{1,17},{9,25},{17,1},{25,9},{2,18},{10... | collective-permute-start | bytes 6291464 | tf_op jit(solution)/shard_map/ppermute | solution.py:275
  601.0 45.7 %collective-permute-start.36 = (bf16[512,896]{0,1:T(8,128)(2,1)}, bf16[512,896]{0,1:T(8,128)(2,1)}, u32[]{:S(2)}, u32[]{:S(2)}) collective-permute-start(bf16[512,896]{0,1:T(8,128)(2,1)} %fusion.25), channel_id=1, source_target_pairs={{0,16},{8,24},{16,0},{24,8},{1,17},{9,25},{17,1},{25,9},{2,18},{10... | collective-permute-start | bytes 2752520 | tf_op jit(solution)/shard_map/ppermute | solution.py:275
  608.4 77.3 %all-to-all-start.4 = ((bf16[8,64,2048]{2,1,0:T(8,128)(2,1)}), bf16[8,64,2048]{2,1,0:T(8,128)(2,1)S(1)}, u32[]{:S(2)}, u32[]{:S(2)}) async-start(bf16[8,64,2048]{2,1,0:T(8,128)(2,1)} %bitcast.108), calls=%async_computation.7 | async-start | bytes 4194304 | tf_op jit(solution)/shard_map/all_to_all | solution.py:440
  612.1 38.9 %collective-permute-start.30 = (bf16[64,2048]{1,0:T(8,128)(2,1)S(1)}, bf16[64,2048]{1,0:T(8,128)(2,1)S(1)}, u32[]{:S(2)}, u32[]{:S(2)}) collective-permute-start(bf16[64,2048]{1,0:T(8,128)(2,1)S(1)} %get-tuple-element.135), channel_id=1, source_target_pairs={{0,1},{1,0},{2,3},{3,2},{4,5},{5,4},{6,7},{7,6},{8,9},{9,8},{10,11... | collective-permute-start | bytes 786440 | tf_op jit(solution)/shard_map/ppermute | solution.py:275
  614.0 37.9 %collective-permute-start.31 = (bf16[64,2048]{1,0:T(8,128)(2,1)}, bf16[64,2048]{1,0:T(8,128)(2,1)S(1)}, u32[]{:S(2)}, u32[]{:S(2)}) collective-permute-start(bf16[64,2048]{1,0:T(8,128)(2,1)} %get-tuple-element.136), channel_id=1, source_target_pairs={{0,2},{1,3},{2,0},{3,1},{4,6},{5,7},{6,4},{7,5},{8,10},{9,11},{10,... | collective-permute-start | bytes 786440 | tf_op jit(solution)/shard_map/ppermute | solution.py:275
  684.3 31.1 %collective-permute-start.38 = (bf16[256,2048]{1,0:T(8,128)(2,1)}, bf16[256,2048]{1,0:T(8,128)(2,1)}, u32[]{:S(2)}, u32[]{:S(2)}) collective-permute-start(bf16[256,2048]{1,0:T(8,128)(2,1)} %pad_maximum_fusion.10), channel_id=1, source_target_pairs={{0,1},{1,0},{2,3},{3,2},{4,5},{5,4},{6,7},{7,6},{8,9},{9,8},{10,11... | collective-permute-start | bytes 3145736 | tf_op jit(solution)/shard_map/ppermute | solution.py:275
  693.3 46.5 %all-to-all-start.3 = ((bf16[8,64,896]{2,1,0:T(8,128)(2,1)}), bf16[8,64,896]{2,1,0:T(8,128)(2,1)S(1)}, u32[]{:S(2)}, u32[]{:S(2)}) async-start(bf16[8,64,896]{2,1,0:T(8,128)(2,1)} %bitcast.121), calls=%async_computation.6 | async-start | bytes 1835008 | tf_op jit(solution)/shard_map/all_to_all | solution.py:440
  (88 other events, 993.3 us)
Sparse Core Ops, SparseCore 0:
  10.2 96.0 all-gather.8
  109.2 120.8 all-gather.4
  254.2 72.2 all-gather.6
  376.7 71.3 reduce-scatter.3
  451.6 98.2 reduce-scatter.5
  576.7 97.7 reduce-scatter.7

commit v4 on v3

--- a/solution.py
+++ b/solution.py
@@ -277,20 +277,17 @@
         return got
 
 
-def place(pieces, places, columns=False):
+def place(pieces, places):
     pieces = [value_of(piece) for piece in pieces]
     rows, width = pieces[0].shape
     count = len(pieces)
-    shape = (rows, count * width) if columns else (count * rows, width)
+    shape = (count * rows, width)
 
     def kernel(places_ref, *refs):
         parts, whole, sems = refs[:count], refs[count], refs[count + 1]
         copies = []
         for i in range(count):
-            if columns:
-                there = whole.at[:, pl.ds(pl.multiple_of(places_ref[i] * width, width), width)]
-            else:
-                there = whole.at[pl.ds(pl.multiple_of(places_ref[i] * rows, rows), rows), :]
+            there = whole.at[pl.ds(pl.multiple_of(places_ref[i] * rows, rows), rows), :]
             copies.append(pltpu.make_async_copy(parts[i], there, sems.at[i]))
         for copy in copies:
             copy.start()
@@ -309,7 +306,7 @@
     )(jnp.stack(places).astype(jnp.int32), *pieces)
 
 
-def cut_columns(weights, groups, beside):
+def cut_columns(weights, groups, beside, devices=None):
     n = lax.axis_size("ctx")
     rows = weights[0].shape[0]
     width = weights[0].shape[1] // (n * groups)
@@ -318,15 +315,15 @@
 
     def kernel(*refs):
         out = refs[-1]
-        for device in range(n):
+        for i, device in enumerate(devices or range(n)):
             at = 0
             for weight in refs[: len(weights)]:
                 for group in range(groups):
                     start = (group * n + device) * width
-                    out[device, :, at : at + width] = weight[:, start : start + width]
+                    out[i, :, at : at + width] = weight[:, start : start + width]
                     at += width
             if beside is not None:
-                out[device, :, at:] = refs[len(weights)][...]
+                out[i, :, at:] = refs[len(weights)][...]
 
     vmem = pl.BlockSpec(memory_space=pltpu.VMEM)
     return pl.pallas_call(
@@ -367,69 +364,77 @@
     )(blocks)
 
 
-def gather_ctx(y, z, block):
-    two = z.swap(block, 2)
-    six = z.swap(block, 6)
-    one = y.swap(block, 1)
-    four = z.swap(six, 2)
-    held = [(0, block), (2, two), (6, six), (1, one), (4, four)]
-    for offset, part in ((3, two), (7, six), (5, four)):
-        held.append((offset, y.swap(part, 1)))
-    return held
-
-
-def gather_seq(x, here, block):
-    near = x.swap(block, 1)
+def ring():
+    n = lax.axis_size("ctx")
+    return list(range(0, n, 2)) + list(range(n - 1, 0, -2))
+
+
+def gather_ring(block):
+    return lax.all_gather(block, "ctx", axis=0, tiled=True, axis_index_groups=[ring()])
+
+
+def scatter_ring(total):
+    return lax.psum_scatter(
+        total, "ctx", scatter_dimension=0, tiled=True, axis_index_groups=[ring()]
+    ).astype(f32)
+
+
+def rearranged(stack, places, columns=False):
+    count = len(places)
+    rows, width = stack.shape[0] // count, stack.shape[1]
+
+    def kernel(stack_ref, whole, sems):
+        copies = []
+        for i, to in enumerate(places):
+            if columns:
+                there = whole.at[:, pl.ds(to * width, width)]
+            else:
+                there = whole.at[pl.ds(to * rows, rows), :]
+            block = stack_ref.at[pl.ds(i * rows, rows), :]
+            copies.append(pltpu.make_async_copy(block, there, sems.at[i]))
+        for copy in copies:
+            copy.start()
+        for copy in copies:
+            copy.wait()
+
+    shape = (rows, count * width) if columns else stack.shape
+    return pl.pallas_call(
+        kernel,
+        out_shape=jax.ShapeDtypeStruct(shape, stack.dtype),
+        in_specs=[pl.BlockSpec(memory_space=pl.ANY)],
+        out_specs=pl.BlockSpec(memory_space=pltpu.VMEM),
+        scratch_shapes=[pltpu.SemaphoreType.DMA((count,))],
+        compiler_params=pltpu.CompilerParams(vmem_limit_bytes=32 * 1024 * 1024),
+    )(stack)
+
+
+def whole_ring():
+    n = lax.axis_size("ctx")
+    depth = n // 2
+    chips = []
+    for far, side, upward in ((0, 0, True), (0, 1, False), (1, 1, True), (1, 0, False)):
+        levels = range(depth) if upward else range(depth - 1, -1, -1)
+        chips += [(far, 2 * level + side) for level in levels]
+    return [(2 * far + core) * n + ctx for far, ctx in chips for core in range(2)]
+
+
+def core_swap(block):
+    n = lax.axis_size("seq")
+    return Box(lax.ppermute(value_of(block), "seq", [(i, i ^ 1) for i in range(n)]))
+
+
+def gather_seq(x, block):
     far = x.swap(block, 2)
-    both = x.swap(far, 1)
-    return [(0, block), (1, near), (2, far), (3, both)]
-
-
-def scatter_ctx(y, z, total, here, beside=()):
-    beside = list(beside)
-
-    def after_next(block):
-        return order(block, *beside.pop(0)()) if beside else block
-
-    n = lax.axis_size("ctx")
-    rows = total.shape[0] // n
-    part = [lax.dynamic_slice_in_dim(total, (here ^ o) * rows, rows, 0) for o in range(n)]
-
-    def add(offset, got):
-        return part[offset].astype(f32) + got.value.astype(f32)
-
-    four = add(4, y.swap(part[5], 1))
-    two = add(2, y.swap(part[3], 1))
-    got_four = z.swap(four.astype(bf16), 2)
-    six = add(6, y.swap(after_next(part[7]), 1))
-    got_two = z.swap(two.astype(bf16), 2)
-    from_y = y.swap(part[1], 1)
-    got_six = z.swap(after_next((six + got_four.value.astype(f32)).astype(bf16)), 6)
-    return add(0, from_y) + got_two.value.astype(f32) + got_six.value.astype(f32)
-
-
-def scatter_ctx_grouped(y, z, total, here):
-    n = lax.axis_size("ctx")
-    rows = total.shape[0] // n
-    offsets = [0, 6, 2, 4, 1, 7, 3, 5]
-    left = [lax.dynamic_slice_in_dim(total, (here ^ o) * rows, rows, 0) for o in offsets]
-    for link, mask in ((y, 1), (z, 2), (z, 6)):
-        half = len(left) // 2
-        got = link.swap(jnp.concatenate(left[half:], axis=0).astype(bf16), mask)
-        left = [
-            part + got.value[i * rows : (i + 1) * rows].astype(f32)
-            for i, part in enumerate(left[:half])
-        ]
-    return left[0]
-
-
-def scatter_seq_near(x, total, here):
+    return [(0, block), (1, core_swap(block)), (2, far), (3, core_swap(far))]
+
+
+def scatter_seq_near(total, here):
     rows = total.shape[0] // 4
 
     def piece(offset):
         return lax.dynamic_slice_in_dim(total, (here ^ offset) * rows, rows, 0)
 
-    got = x.swap(jnp.concatenate([piece(3), piece(1)], axis=0).astype(bf16), 1)
+    got = core_swap(jnp.concatenate([piece(3), piece(1)], axis=0).astype(bf16))
     return piece(0) + got.value[rows:].astype(f32), (
         piece(2) + got.value[:rows].astype(f32)
     ).astype(bf16)
@@ -439,16 +444,6 @@
     n = lax.axis_size("ctx")
     blocks = lax.all_to_all(part.reshape(n, -1, part.shape[1]), "ctx", 0, 0, tiled=True)
     return paste_columns(blocks, count, groups, beside)
-
-
-def scatter_halves(y, z, total, here, beside=()):
-    n = lax.axis_size("ctx")
-    parts = total.reshape(n, 2, -1, total.shape[1])
-    first = lax.psum_scatter(
-        parts[:, 0].reshape(-1, total.shape[1]), "ctx", scatter_dimension=0, tiled=True
-    )
-    second = scatter_ctx(y, z, parts[:, 1].reshape(-1, total.shape[1]), here, beside)
-    return jnp.concatenate([first.astype(f32), second], axis=0)
 
 
 def tuned(
@@ -471,13 +466,14 @@
     seq_here = lax.axis_index("seq")
     rows = hidden_in.shape[1]
     weight_rows = w_query.shape[0]
-    y, z, x = Link("ctx", 2), Link("ctx", 2), Link("seq", 1)
+    x = Link("seq", 1)
+    place_here = jnp.where(here % 2 == 0, here // 2, n - 1 - here // 2)
 
     def own_rows(whole):
-        return lax.dynamic_slice_in_dim(whole, here * rows, rows, 0)
-
-    def from_devices(held, index=here):
-        return place([part for _, part in held], [index ^ o for o, _ in held])
+        return lax.dynamic_slice_in_dim(whole, place_here * rows, rows, 0)
+
+    def from_devices(held):
+        return place([part for _, part in held], [seq_here ^ o for o, _ in held])
 
     own_pos = positions[0].reshape(weight_rows, -1)
     per_row = own_pos.shape[1]
@@ -491,24 +487,26 @@
         axis=1,
     )
     beside = jnp.pad(beside, ((0, 0), (0, 128 - beside.shape[1])))
-    x_low = lax.all_gather(hidden_in[0], "ctx", axis=0, tiled=True)
+    x_low = gather_ring(hidden_in[0])
+    down_steps = gather_seq(Link("seq", 1), w_down)
     blocks = cut_columns((w_query, w_key, w_value), 1, beside)
     qkv_mine = lax.all_to_all(blocks, "ctx", 0, 0, tiled=True).reshape(n * weight_rows, -1)
-    late_gate, late_up, late_out, late_down, qkv_mine = lax.optimization_barrier(
-        (w_gate, w_up, w_out, w_down, qkv_mine)
-    )
-    full_out = lax.all_gather(late_out, ("seq", "ctx"), axis=0, tiled=True)
-    qkv_steps = gather_seq(x, seq_here, qkv_mine)
-    down_steps = gather_seq(x, seq_here, late_down)
+    down_far = down_steps[2][1]
+    late_out, qkv_mine, down_far.value = lax.optimization_barrier((w_out, qkv_mine, down_far.value))
+    qkv_steps = gather_seq(x, qkv_mine)
+    far = qkv_steps[2][1]
+    late_gate, late_up, far.value = lax.optimization_barrier((w_gate, w_up, far.value))
+    out_stack = lax.all_gather(
+        late_out, ("seq", "ctx"), axis=0, tiled=True, axis_index_groups=[whole_ring()]
+    )
     blocks = cut_columns((late_gate, late_up), seqs, None)
     gate_up = lax.all_to_all(blocks, "ctx", 0, 0, tiled=True).reshape(n * weight_rows, -1)
-    gate_up_steps = gather_seq(x, seq_here, gate_up)
-    qkv_sub = from_devices(qkv_steps, seq_here)
-    down_sub = from_devices(down_steps, seq_here)
-    gate_up = from_devices(gate_up_steps, seq_here)
+    qkv_sub = from_devices(qkv_steps)
+    down_sub = from_devices(down_steps)
     pos_cuts = qkv_mine[:, -128:].astype(jnp.int32)
     pos_all = pos_cuts[:, 2 : 2 + per_row] * 64 + pos_cuts[:, 2 + per_row : 2 + 2 * per_row]
-    pos_all = pos_all.reshape(-1)
+    pos_all = pos_all.reshape(n, rows)
+    pos_all = jnp.concatenate([pos_all[device] for device in ring()])
     gain1 = qkv_sub[:, -128].astype(f32)
     gain2 = qkv_sub[:, -127].astype(f32)
     qkv_sub = qkv_sub[:, :-128]
@@ -523,11 +521,18 @@
     query = rotate(qkv[:, :width], cosine, sine).astype(bf16)
     key = rotate(qkv[:, width : 2 * width], cosine, sine).astype(bf16)
     value = qkv[:, 2 * width :].astype(bf16)
-    attended, lse = attention(query, key, value, pos_all)
-    att_held = gather_ctx(y, z, attended.astype(bf16))
-    att_low = place([part for _, part in att_held], [here ^ o for o, _ in att_held], columns=True)
+    split = width // 2
+    halves = [slice(0, split), slice(split, width)]
+    att_first, lse_first = attention(*(m[:, halves[0]] for m in (query, key, value)), pos_all)
+    att_second, lse_second = attention(*(m[:, halves[1]] for m in (query, key, value)), pos_all)
+    att_low = jnp.concatenate([att_first, att_second], axis=1).astype(bf16)
+    att_low, out_stack, gate_up = lax.optimization_barrier((att_low, out_stack, gate_up))
+    gate_up = from_devices(gather_seq(x, gate_up))
+    att_stack = gather_ring(att_low)
+    full_out = rearranged(out_stack, whole_ring())
+    att_low = rearranged(att_stack, ring(), columns=True)
     late_grad, att_low = lax.optimization_barrier((out_grad[0], att_low))
-    grad_all = lax.all_gather(late_grad, "ctx", axis=0, tiled=True)
+    grad_all = gather_ring(late_grad)
 
     middle = x_all + dot(att_low, full_out)
     mlp_scale = rms_scale(middle)
@@ -539,21 +544,20 @@
     inner = (gate_act * sig * up_act).astype(bf16)
     middle_own = own_rows(middle)
 
-    inner_grad = dot_cols(grad_all, down_sub)
+    inner_grad = lax.optimization_barrier(dot_cols(grad_all, down_sub))
     gate_grad = (inner_grad * up_act * sig * (1.0 + gate_act * (1.0 - sig))).astype(bf16)
     up_grad = (inner_grad * gate_act * sig).astype(bf16)
-    gate_up_grad = jnp.concatenate([gate_grad, up_grad], axis=1)
+    gate_up_grad = lax.optimization_barrier(jnp.concatenate([gate_grad, up_grad], axis=1))
     mid_grad_part = dot_cols(gate_up_grad, gate_up).astype(bf16)
-    gate_up_near, gate_up_far = scatter_seq_near(x, dot_rows(normed_mid, gate_up_grad), seq_here)
-    gate_up_far = Box(gate_up_far)
-    mid_grad_in = scatter_halves(y, z, mid_grad_part, here, [lambda: [gate_up_far]])
-    gate_up_far = x.swap(gate_up_far, 2)
+    gate_up_near, gate_up_far = scatter_seq_near(dot_rows(normed_mid, gate_up_grad), seq_here)
+    mid_grad_in = scatter_ring(mid_grad_part)
     down_weight_part = dot_rows(inner, grad_all)
     down_part = dot(inner, down_sub).astype(bf16)
-    mid_grad_in, down_weight_part, down_part = lax.optimization_barrier(
-        (mid_grad_in, down_weight_part, down_part)
-    )
-    down_own = lax.psum_scatter(down_part, "ctx", scatter_dimension=0, tiled=True)
+    mid_grad_in, down_weight_part, down_part, gate_up_far = lax.optimization_barrier(
+        (mid_grad_in, down_weight_part, down_part, gate_up_far)
+    )
+    gate_up_far = x.swap(gate_up_far, 2)
+    down_own = scatter_ring(down_part)
 
     mid_scale = own_rows(mlp_scale)
     mid_unit = middle_own * mid_scale
@@ -564,52 +568,63 @@
     mlp_gain_part = jnp.sum(mid_grad_in * mid_unit, axis=0)
     middle_low = middle_grad.astype(bf16)
     att_grad = dot_cols(middle_low, full_out).astype(bf16)
-    blocks = cut_columns((att_grad,), 1, None)
-    att_grad = lax.all_to_all(blocks, "ctx", 0, 0, tiled=True).reshape(n * rows, -1)
-    w_out_part = dot_rows(own_rows(att_low), middle_low)
-    down_weight_near, down_weight_far = scatter_seq_near(x, down_weight_part, seq_here)
-    att_grad, w_out_part, gate_up_far.value, down_weight_far = lax.optimization_barrier(
-        (att_grad, w_out_part, gate_up_far.value, down_weight_far)
+    blocks = cut_columns((att_grad,), 1, None, ring())
+    att_grad = lax.all_to_all(blocks, "ctx", 0, 0, tiled=True, axis_index_groups=[ring()])
+    att_grad = att_grad.reshape(n * rows, -1)
+    middle_low_all = gather_ring(middle_low)
+    gate_up_sum = (gate_up_near + gate_up_far.value.astype(f32)).astype(bf16)
+    att_grad, gate_up_sum, down_own = lax.optimization_barrier((att_grad, gate_up_sum, down_own))
+    w_gate_up = lax.all_to_all(gate_up_sum.reshape(n, weight_rows, -1), "ctx", 0, 0, tiled=True)
+
+    grads = [
+        attention_back(
+            *(m[:, halves[0]] for m in (query, key, value)), pos_all, att_first, lse_first, att_grad[:, halves[0]]
+        )
+    ]
+    down_weight_near, down_weight_far = scatter_seq_near(down_weight_part, seq_here)
+    att_grad, down_weight_far, grads[0] = lax.optimization_barrier(
+        (att_grad, down_weight_far, grads[0])
     )
     down_weight_far = x.swap(down_weight_far, 2)
-    w_out_near, w_out_far = scatter_seq_near(x, w_out_part, seq_here)
-    gate_up_sum = (gate_up_near + gate_up_far.value.astype(f32)).astype(bf16)
-    w_gate_grad, w_up_grad = to_owners(gate_up_sum, 2, seqs)
-
-    query_acc, key_acc, value_acc = attention_back(
-        query, key, value, pos_all, attended, lse, att_grad
-    )
+    grads.append(
+        attention_back(
+            *(m[:, halves[1]] for m in (query, key, value)), pos_all, att_second, lse_second, att_grad[:, halves[1]]
+        )
+    )
+    query_acc, key_acc, value_acc = (jnp.concatenate(pair, axis=1) for pair in zip(*grads))
     qkv_grad = jnp.concatenate(
         [rotate(query_acc, cosine, -sine), rotate(key_acc, cosine, -sine), value_acc], axis=1
     ).astype(bf16)
-    qkv_grad, down_weight_far.value, w_out_far, down_own = lax.optimization_barrier(
-        (qkv_grad, down_weight_far.value, w_out_far, down_own)
-    )
-    hidden_out = (middle_own + down_own.astype(f32)).astype(bf16)
-    w_down_grad = down_weight_near + down_weight_far.value.astype(f32)
-    w_out_far = x.swap(w_out_far, 2)
+    out_rows = w_out.shape[0]
+    att_sub = jnp.concatenate(
+        [
+            lax.dynamic_slice_in_dim(att_low, (i * n + here) * out_rows, out_rows, 1)
+            for i in range(seqs)
+        ],
+        axis=1,
+    )
+    w_out_near, w_out_far = scatter_seq_near(dot_rows(att_sub, middle_low_all), seq_here)
+    hidden_out = (middle_own + down_own).astype(bf16)
+    qkv_grad, w_gate_up, down_weight_far.value = lax.optimization_barrier(
+        (qkv_grad, w_gate_up, down_weight_far.value)
+    )
     normed_grad_part = dot_cols(qkv_grad, qkv_sub)
     attn_gain_part = jnp.sum(normed_grad_part * (x_all * attn_scale), axis=0)
     beside = jnp.stack([attn_gain_part, mlp_gain_part], axis=1)
     beside = jnp.pad(beside, ((0, 0), (0, 126)))
     qkv_part = jnp.concatenate([dot_rows(normed, qkv_grad), beside], axis=1)
-    x_again = Link("seq", 1)
-    qkv_near, qkv_far = scatter_seq_near(x_again, qkv_part, seq_here)
-    qkv_far, qkv_sum = Box(qkv_far), Box(None)
-
-    def add_far():
-        far = x_again.swap(qkv_far, 2)
-        qkv_sum.value = (qkv_near + far.value.astype(f32)).astype(bf16)
-        return [qkv_sum]
-
-    normed_grad = scatter_halves(
-        y, z, normed_grad_part.astype(bf16), here, [lambda: [qkv_far], add_far]
-    )
-    w_query_grad, w_key_grad, w_value_grad, gain_grads = to_owners(qkv_sum.value, 3, 1, 128)
+    qkv_near, qkv_far = scatter_seq_near(qkv_part, seq_here)
+    normed_grad = scatter_ring(normed_grad_part.astype(bf16))
+    qkv_far = Link("seq", 1).swap(qkv_far, 2)
+    qkv_sum = (qkv_near + qkv_far.value.astype(f32)).astype(bf16)
+    w_query_grad, w_key_grad, w_value_grad, gain_grads = to_owners(qkv_sum, 3, 1, 128)
     gain_grads = gain_grads.astype(f32).reshape(weight_rows, n, 128).sum(axis=1)
-    w_out_far, normed_grad = lax.optimization_barrier((w_out_far.value, normed_grad))
-    w_out_sum = w_out_near + w_out_far.astype(f32)
-    w_out_grad = scatter_ctx_grouped(y, z, w_out_sum, here)
+    w_out_grad = w_out_near + Link("seq", 1).swap(w_out_far, 2).value.astype(f32)
+    down_weight_far, w_gate_up, normed_grad = lax.optimization_barrier(
+        (down_weight_far.value, w_gate_up, normed_grad)
+    )
+    w_gate_grad, w_up_grad = paste_columns(w_gate_up, 2, seqs)
+    w_down_grad = down_weight_near + down_weight_far.astype(f32)
 
     own_scale = own_rows(attn_scale)
     own_unit = hidden_in[0].astype(f32) * own_scale

time: 767 us -> 633 us (0.83)
  blocking collectives: 47.2 us -> 0 us
  waiting for transfers between devices: 313 us -> 269 us
  starting transfers between devices: 62.1 us -> 37.8 us
  other arithmetic: 86.4 us -> 66.3 us
  local copies, waits for them, and re-layouts: 59.6 us -> 70.1 us
    ppermute x41 -> x7, waiting for transfers between devices: 222 us -> 94.6 us  [swap(): lax.ppermute(value_of(block), self.axis, [(i, i ^ mask) for i in range(n)])]
    all_to_all x1 -> x0, blocking collectives: 47.2 us -> none  [tuned(): lax.all_to_all(blocks, 'ctx', 0, 0, tiled=True).reshape(n * weight_rows, -1)]
    all_gather x3 -> x5, waiting for transfers between devices: 29.7 us -> 74.1 us  [the longest x4 47.5 us: gather_ring(): lax.all_gather(block, 'ctx', axis=0, tiled=True, axis_index_groups=[ring()])]
    ppermute x41 -> x7, starting transfers between devices: 41.8 us -> 9.92 us  [swap(): lax.ppermute(value_of(block), self.axis, [(i, i ^ mask) for i in range(n)])]
    all_to_all x1 -> x2, waiting for transfers between devices: 13.5 us -> 40.5 us  [tuned(): lax.all_to_all(blocks, 'ctx', 0, 0, tiled=True).reshape(n * weight_rows, -1)]
    reduce_scatter x3, waiting for transfers between devices: 30.4 us -> 4.22 us  [scatter_ring(): lax.psum_scatter(total, 'ctx', scatter_dimension=0, tiled=True, axis_inde...]
    all_to_all x2 -> x1, waiting for transfers between devices: 0.01 us -> 14.7 us  [to_owners(): lax.all_to_all(part.reshape(n, -1, part.shape[1]), 'ctx', 0, 0, tiled=True)]
    unnamed x124 -> x147, local copies, waits for them, and re-layouts: 37.2 us -> 50.9 us
  transfers between devices with their start and end apart: 51 -> 30, of which waited for: 27 -> 17; matrix products, arithmetic and copies ran while one was open for 29% -> 32% of each run, Pallas kernels for 2% -> 2%
where the time goes in v4:
time: 633 us; the launch traced here: 627 us
  waiting for transfers between devices  269 us (42%)
  matrix products  156 us (25%)
  local copies, waits for them, and re-layouts  70.1 us (11%)
  other arithmetic  66.3 us (10%)
  starting transfers between devices  37.8 us (6%)
  between operations  15.6 us (2%)
  Pallas kernels  13 us (2%)
    ppermute x7, waiting for transfers between devices, swap(): lax.ppermute(value_of(block), self.axis, [(i, i ^ mask) for i in range(n)])  94.6 us
    unnamed x147, local copies, waits for them, and re-layouts  50.9 us
    all_gather x4, waiting for transfers between devices, gather_ring(): lax.all_gather(block, 'ctx', axis=0, tiled=True, axis_index_groups=[ring()])  47.5 us
    dot_general x4, matrix products, dot_cols(): lax.dot_general(left, right, (((1,), (1,)), ((), ())), preferred_element_...  44.4 us
    all_to_all x2, waiting for transfers between devices, tuned(): lax.all_to_all(blocks, 'ctx', 0, 0, tiled=True).reshape(n * weight_rows, -1)  40.5 us
    dot_general x4, matrix products, dot(): return jnp.dot(left, right, preferred_element_type=f32)  38.5 us
    dot_general x4, matrix products, dot_rows(): lax.dot_general(left, right, (((0,), (0,)), ((), ())), preferred_element_...  32.3 us
    all_gather x1, waiting for transfers between devices, tuned(): lax.all_gather(late_out, ('seq', 'ctx'), axis=0, tiled=True, axis_index_g...  26.7 us
  transfers between devices with their start and end apart: 30, of which 17 were waited for; matrix products, arithmetic and copies ran while one was open for 32% of the time, Pallas kernels for 2%

profile of v4, /device:TPU:0, one launch (start us, length us, event | category | flops | bytes accessed | tf_op | source)
XLA Modules:
  0.0 627.2 jit_solution(11204046863039527256)
XLA Ops:
  14.8 7.3 %all-to-all-start = ((bf16[8,64,896]{2,1,0:T(8,128)(2,1)}), bf16[8,64,896]{2,1,0:T(8,128)(2,1)S(1)}, u32[]{:S(2)}, u32[]{:S(2)}) async-start(bf16[8,64,896]{2,1,0:T(8,128)(2,1)} %shard_map.203), calls=%async_computation | async-start | bytes 1835008 | tf_op jit(solution)/shard_map/all_to_all | solution.py:493
  23.7 23.1 %collective-permute-done.refs_2_ = bf16[256,2048]{1,0:T(8,128)(2,1)S(1)} collective-permute-done((bf16[256,2048]{1,0:T(8,128)(2,1)S(1)}, bf16[256,2048]{1,0:T(8,128)(2,1)S(1)}, u32[]{:S(2)}, u32[]{:S(2)}) %collective-permute-start) | collective-permute-done | bytes 1048608 | tf_op jit(solution)/shard_map/ppermute | solution.py:275
  46.8 8.4 %all-to-all-done = bf16[8,64,896]{2,1,0:T(8,128)(2,1)S(1)} async-done(((bf16[8,64,896]{2,1,0:T(8,128)(2,1)}), bf16[8,64,896]{2,1,0:T(8,128)(2,1)S(1)}, u32[]{:S(2)}, u32[]{:S(2)}) %all-to-all-start) | async-done | bytes 917536 | tf_op jit(solution)/shard_map/all_to_all | solution.py:493
  58.3 16.7 %collective-permute-done.2.refs_2_ = bf16[512,896]{1,0:T(8,128)(2,1)} collective-permute-done((bf16[512,896]{1,0:T(8,128)(2,1)S(1)}, bf16[512,896]{1,0:T(8,128)(2,1)}, u32[]{:S(2)}, u32[]{:S(2)}) %collective-permute-start.2) | collective-permute-done | bytes 917536 | tf_op jit(solution)/shard_map/ppermute | solution.py:275
  115.6 6.8 %fusion.98 = (bf16[1024,2,64]{0,2,1:T(8,128)(2,1)}, f32[1024,2,64]{0,2,1:T(8,128)}) fusion(f32[1024,2]{0,1:T(2,128)S(1)} %bitcast.173, bf16[1024,2,64]{0,2,1:T(8,128)(2,1)} %bitcast.166, f32[2,1024,1024]{1,2,0:T(8,128)} %copy-done.66, f32[2,1024]{1,0:T(2,128)S(1)} %get-tuple-element.149, pred[1024,1024]{0,1:T(8,128)(4,1)S(1)} %copy-done.34), kind=kOutput, calls=%fused_computation.199 | convolution fusion | flops 277086208 | bytes 10502144 | tf_op jit(solution)/shard_map/hqk,khd->qhd/dot_general | solution.py:105
  124.4 32.1 %all-to-all-done.1 = bf16[8,64,2048]{2,1,0:T(8,128)(2,1)S(1)} async-done(((bf16[8,64,2048]{2,1,0:T(8,128)(2,1)}), bf16[8,64,2048]{2,1,0:T(8,128)(2,1)S(1)}, u32[]{:S(2)}, u32[]{:S(2)}) %all-to-all-start.1) | async-done | bytes 2097184 | tf_op jit(solution)/shard_map/all_to_all | solution.py:503
  156.5 26.7 %all-gather.7.cloned.1.call-done.stack_ref = bf16[2048,2048]{1,0:T(8,128)(2,1)} async-done(((bf16[64,2048]{1,0:T(8,128)(2,1)}), bf16[2048,2048]{1,0:T(8,128)(2,1)}) %all-gather.7.cloned.1.call-update) | async-done | bytes 8388624 | tf_op jit(solution)/shard_map/all_gather | solution.py:499
  184.2 47.4 %all-gather.9.cloned.1.call-done.stack_ref = bf16[8192,256]{1,0:T(8,128)(2,1)} async-done(((bf16[1024,256]{1,0:T(8,128)(2,1)}), bf16[8192,256]{1,0:T(8,128)(2,1)}) %all-gather.9.cloned.1.call-update) | async-done | bytes 4194320 | tf_op jit(solution)/shard_map/all_gather | solution.py:373
  237.7 8.2 %collective-permute-done.4.refs_1_ = bf16[256,2048]{1,0:T(8,128)(2,1)S(1)} collective-permute-done((bf16[256,2048]{1,0:T(8,128)(2,1)S(1)}, bf16[256,2048]{1,0:T(8,128)(2,1)S(1)}, u32[]{:S(2)}, u32[]{:S(2)}) %collective-permute-start.4) | collective-permute-done | bytes 1048608 | tf_op jit(solution)/shard_map/ppermute | solution.py:423
  269.3 10.9 %multiply_reduce_fusion = (f32[1024]{0:T(1024)S(1)}, f32[1024,2048]{1,0:T(8,128)S(1)}) fusion(bf16[1024,2048]{1,0:T(8,128)(2,1)S(1)} %copy-done.6, bf16[2048,2048]{1,0:T(8,128)(2,1)S(1)} %shard_map.207, bf16[1,1024,2048]{2,1,0:T(8,128)(2,1)} %all-gather.15.cloned.1.call-done), kind=kOutput, calls=%fused_computation.17 | convolution fusion | flops 8598322176 | bytes 25169920 | tf_op jit(solution)/shard_map/dot_general | solution.py:65
  283.6 13.5 %fusion.90 = f32[1024,2048]{1,0:T(8,128)} fusion(bf16[2048,2048]{1,0:T(8,128)(2,1)} %copy-done.1, f32[1024,2048]{1,0:T(8,128)S(1)} %get-tuple-element.157, f32[2048]{0:T(1024)S(1)} %get-tuple-element.89, f32[1024]{0:T(1024)S(1)} %add_rsqrt_fusion), kind=kOutput, calls=%fused_computation.191 | convolution fusion | flops 8596226048 | bytes 25178112 | tf_op jit(solution)/shard_map/dot_general | solution.py:65
  297.1 7.7 %fusion.99 = f32[1024,1024]{1,0:T(8,128)S(1)} fusion(bf16[1024,2048]{1,0:T(8,128)(2,1)} %all-gather.11.cloned.1.call-done, bf16[1024,2048]{1,0:T(8,128)(2,1)} %copy-done.9), kind=kOutput, calls=%fused_computation.200 | convolution fusion | flops 4294967296 | bytes 12582912 | tf_op jit(solution)/shard_map/dot_general | solution.py:73
  312.7 20.0 %convolution_convert_fusion = bf16[1024,2048]{1,0:T(8,128)(2,1)} fusion(bf16[1024,2048]{1,0:T(8,128)(2,1)S(1)} %pad_maximum_fusion, bf16[2048,2048]{1,0:T(8,128)(2,1)S(1)} %copy-done.2), kind=kOutput, calls=%fused_computation.50 | convolution fusion | flops 8592031744 | bytes 16777216 | tf_op jit(solution)/shard_map/dot_general | solution.py:73
  332.8 13.2 %fusion.89 = f32[2048,2048]{1,0:T(8,128)S(1)} fusion(bf16[1024,2048]{1,0:T(8,128)(2,1)} %copy-done.39, f32[1024,2048]{1,0:T(8,128)} %copy-done.46, f32[2048]{0:T(1024)S(1)} %get-tuple-element.89, f32[1024]{0:T(1024)S(1)} %add_rsqrt_fusion), kind=kOutput, calls=%fused_computation.190 | convolution fusion | flops 8596226048 | bytes 29372416 | tf_op jit(solution)/shard_map/dot_general | solution.py:69
  355.0 8.3 %convolution_convert_fusion.1 = bf16[1024,2048]{1,0:T(8,128)(2,1)} fusion(bf16[1024,1024]{1,0:T(8,128)(2,1)S(1)} %get-tuple-element.105, bf16[1024,2048]{1,0:T(8,128)(2,1)} %copy-done.9), kind=kOutput, calls=%fused_computation.51 | convolution fusion | flops 4297064448 | bytes 10485760 | tf_op jit(solution)/shard_map/dot_general | solution.py:65
  363.2 9.1 %fusion.100 = f32[1024,2048]{1,0:T(8,128)} fusion(bf16[1024,1024]{1,0:T(8,128)(2,1)S(1)} %get-tuple-element.105, bf16[1024,2048]{1,0:T(8,128)(2,1)} %all-gather.11.cloned.1.call-done), kind=kOutput, calls=%fused_computation.201 | convolution fusion | flops 4294967296 | bytes 14680064 | tf_op jit(solution)/shard_map/dot_general | solution.py:69
  392.2 6.5 %convolution_convert_fusion.2.refs_0_ = bf16[128,2048]{1,0:T(8,128)(2,1)S(1)} fusion(bf16[128,2048]{1,0:T(8,128)(2,1)S(1)} %fusion.88, bf16[2048,2048]{1,0:T(8,128)(2,1)} %copy-done), kind=kOutput, calls=%fused_computation.56 | convolution fusion | flops 1074003968 | bytes 9437184 | tf_op jit(solution)/shard_map/dot_general | solution.py:73
  407.2 28.3 %collective-permute-done.10 = bf16[512,2048]{1,0:T(8,128)(2,1)} collective-permute-done((bf16[512,2048]{1,0:T(8,128)(2,1)}, bf16[512,2048]{1,0:T(8,128)(2,1)}, u32[]{:S(2)}, u32[]{:S(2)}) %collective-permute-start.10) | collective-permute-done | bytes 2097184 | tf_op jit(solution)/shard_map/ppermute | solution.py:275
  461.5 6.4 %fusion.13 = bf16[2,64,1024]{2,1,0:T(8,128)(2,1)} fusion(bf16[1024,2,64]{0,2,1:T(8,128)(2,1)S(1)} %bitcast.155, f32[2,1024,1024]{1,2,0:T(8,128)} %copy-done.66, f32[2,1024]{1,0:T(2,128)S(1)} %log_add_fusion.1, pred[1024,1024]{0,1:T(8,128)(4,1)S(1)} %copy-done.36), kind=kOutput, calls=%fused_computation.43 | convolution fusion | flops 276824064 | bytes 9969664 | tf_op jit(solution)/shard_map/hqk,qhd->khd/dot_general | solution.py:121
  485.7 9.0 %collective-permute-done.12 = bf16[256,2048]{1,0:T(8,128)(2,1)} collective-permute-done((bf16[256,2048]{1,0:T(8,128)(2,1)}, bf16[256,2048]{1,0:T(8,128)(2,1)}, u32[]{:S(2)}, u32[]{:S(2)}) %collective-permute-start.12) | collective-permute-done | bytes 1048608 | tf_op jit(solution)/shard_map/ppermute | solution.py:275
  494.7 26.3 %all-to-all-done.3.ref = bf16[8,64,2048]{2,1,0:T(8,128)(2,1)S(1)} async-done(((bf16[8,64,2048]{2,1,0:T(8,128)(2,1)}), bf16[8,64,2048]{2,1,0:T(8,128)(2,1)S(1)}, u32[]{:S(2)}, u32[]{:S(2)}) %all-to-all-start.3) | async-done | bytes 2097184 | tf_op jit(solution)/shard_map/all_to_all | solution.py:577
  521.0 10.1 %fusion.3 = (f32[2048]{0:T(1024)S(1)}, bf16[1024,2048]{1,0:T(8,128)(2,1)}) fusion(bf16[1,1024,2048]{2,1,0:T(8,128)(2,1)} %all-gather.15.cloned.1.call-done, f32[1024]{0:T(1024)S(1)} %copy-done.62, bf16[1024,768]{0,1:T(8,128)(2,1)} %pad_maximum_fusion.4, bf16[2048,896]{1,0:T(8,128)(2,1)} %copy-done.7), kind=kOutput, calls=%fused_computation.10 | convolution fusion | flops 3231709184 | bytes 13119488 | tf_op jit(solution)/shard_map/dot_general | solution.py:73
  559.0 12.8 %collective-permute-done.14 = bf16[512,896]{0,1:T(8,128)(2,1)} collective-permute-done((bf16[512,896]{0,1:T(8,128)(2,1)}, bf16[512,896]{0,1:T(8,128)(2,1)}, u32[]{:S(2)}, u32[]{:S(2)}) %collective-permute-start.14) | collective-permute-done | bytes 917536 | tf_op jit(solution)/shard_map/ppermute | solution.py:275
  591.6 14.7 %all-to-all-done.4.ref = bf16[8,64,896]{2,1,0:T(8,128)(2,1)S(1)} async-done(((bf16[8,64,896]{2,1,0:T(8,128)(2,1)}), bf16[8,64,896]{2,1,0:T(8,128)(2,1)S(1)}, u32[]{:S(2)}, u32[]{:S(2)}) %all-to-all-start.4) | async-done | bytes 917536 | tf_op jit(solution)/shard_map/all_to_all | solution.py:445
  (314 shorter events, 237.9 us)
Async XLA Ops:
  7.2 84.0 %all-gather.15.cloned.1.call-start = ((), (), s32[]{:S(2)}) async-start(), calls=%async_computation.15 | async-start | bytes 4718592 | tf_op jit(solution)/shard_map/all_gather | solution.py:373
  14.8 40.5 %all-to-all-start = ((bf16[8,64,896]{2,1,0:T(8,128)(2,1)}), bf16[8,64,896]{2,1,0:T(8,128)(2,1)S(1)}, u32[]{:S(2)}, u32[]{:S(2)}) async-start(bf16[8,64,896]{2,1,0:T(8,128)(2,1)} %shard_map.203), calls=%async_computation | async-start | bytes 1835008 | tf_op jit(solution)/shard_map/all_to_all | solution.py:493
  22.1 161.1 %all-gather.7.cloned.1.call-start = ((), (), s32[]{:S(2)}) async-start(), calls=%async_computation.8 | async-start | bytes 8650752 | tf_op jit(solution)/shard_map/all_gather | solution.py:499
  22.1 24.7 %collective-permute-start = (bf16[256,2048]{1,0:T(8,128)(2,1)S(1)}, bf16[256,2048]{1,0:T(8,128)(2,1)S(1)}, u32[]{:S(2)}, u32[]{:S(2)}) collective-permute-start(bf16[256,2048]{1,0:T(8,128)(2,1)S(1)} %copy-done.15), channel_id=1, source_target_pairs={{0,16},{8,24},{16,0},{24,8},{1,17},{9,25},{17,1},{25,9},{2,18},{10... | collective-permute-start | bytes 3145736 | tf_op jit(solution)/shard_map/ppermute | solution.py:275
  55.4 19.7 %collective-permute-start.2 = (bf16[512,896]{1,0:T(8,128)(2,1)S(1)}, bf16[512,896]{1,0:T(8,128)(2,1)}, u32[]{:S(2)}, u32[]{:S(2)}) collective-permute-start(bf16[512,896]{1,0:T(8,128)(2,1)S(1)} %bitcast.128), channel_id=1, source_target_pairs={{0,16},{8,24},{16,0},{24,8},{1,17},{9,25},{17,1},{25,9},{2,18},{10... | collective-permute-start | bytes 2752520 | tf_op jit(solution)/shard_map/ppermute | solution.py:275
  56.9 29.4 %collective-permute-start.1 = (bf16[512,896]{1,0:T(8,128)(2,1)S(1)}, bf16[512,896]{1,0:T(8,128)(2,1)}, u32[]{:S(2)}, u32[]{:S(2)}) collective-permute-start(bf16[512,896]{1,0:T(8,128)(2,1)S(1)} %bitcast.129), channel_id=1, source_target_pairs={{0,8},{8,0},{16,24},{24,16},{1,9},{9,1},{17,25},{25,17},{2,10},{10... | collective-permute-start | bytes 2752520 | tf_op jit(solution)/shard_map/ppermute | solution.py:423
  80.7 75.7 %all-to-all-start.1 = ((bf16[8,64,2048]{2,1,0:T(8,128)(2,1)}), bf16[8,64,2048]{2,1,0:T(8,128)(2,1)S(1)}, u32[]{:S(2)}, u32[]{:S(2)}) async-start(bf16[8,64,2048]{2,1,0:T(8,128)(2,1)} %copy-done.4), calls=%async_computation.1 | async-start | bytes 4194304 | tf_op jit(solution)/shard_map/all_to_all | solution.py:503
  86.2 145.4 %all-gather.9.cloned.1.call-start = ((), (), s32[]{:S(2)}) async-start(), calls=%async_computation.9 | async-start | bytes 4718592 | tf_op jit(solution)/shard_map/all_gather | solution.py:373
  183.2 114.0 %all-gather.11.cloned.1.call-start = ((), (), s32[]{:S(2)}) async-start(), calls=%async_computation.10 | async-start | bytes 4718592 | tf_op jit(solution)/shard_map/all_gather | solution.py:373
  183.2 53.4 %collective-permute-start.7 = (bf16[512,2048]{1,0:T(8,128)(2,1)S(1)}, bf16[512,2048]{1,0:T(8,128)(2,1)}, u32[]{:S(2)}, u32[]{:S(2)}) collective-permute-start(bf16[512,2048]{1,0:T(8,128)(2,1)S(1)} %bitcast.125), channel_id=1, source_target_pairs={{0,16},{8,24},{16,0},{24,8},{1,17},{9,25},{17,1},{25,9},{2,18},{10... | collective-permute-start | bytes 6291464 | tf_op jit(solution)/shard_map/ppermute | solution.py:275
  236.5 144.8 %reduce-scatter.4.cloned.1.call-start = ((), (), s32[]{:S(2)}) async-start(), calls=%async_computation.11 | async-start | bytes 4718592 | tf_op jit(solution)/shard_map/reduce_scatter | solution.py:377
  236.6 18.1 %collective-permute-start.6 = (bf16[512,2048]{1,0:T(8,128)(2,1)S(1)}, bf16[512,2048]{1,0:T(8,128)(2,1)S(1)}, u32[]{:S(2)}, u32[]{:S(2)}) collective-permute-start(bf16[512,2048]{1,0:T(8,128)(2,1)S(1)} %bitcast.126), channel_id=1, source_target_pairs={{0,8},{8,0},{16,24},{24,16},{1,9},{9,1},{17,25},{25,17},{2,10},{10... | collective-permute-start | bytes 6291464 | tf_op jit(solution)/shard_map/ppermute | solution.py:423
  236.7 19.3 %collective-permute-start.8 = (bf16[512,2048]{1,0:T(8,128)(2,1)}, bf16[512,2048]{1,0:T(8,128)(2,1)S(1)}, u32[]{:S(2)}, u32[]{:S(2)}) collective-permute-start(bf16[512,2048]{1,0:T(8,128)(2,1)} %collective-permute-done.7.refs_2_), channel_id=1, source_target_pairs={{0,8},{8,0},{16,24},{24,16},{1,9},{9,1},{17,25},{25,17},{2,10},{10... | collective-permute-start | bytes 6291464 | tf_op jit(solution)/shard_map/ppermute | solution.py:423
  332.7 109.0 %reduce-scatter.6.cloned.1.call-start = ((), (), s32[]{:S(2)}) async-start(), calls=%async_computation.12 | async-start | bytes 4718592 | tf_op jit(solution)/shard_map/reduce_scatter | solution.py:377
  354.9 17.5 %collective-permute-start.9 = (bf16[1024,2048]{1,0:T(8,128)(2,1)}, bf16[1024,2048]{1,0:T(8,128)(2,1)}, u32[]{:S(2)}, u32[]{:S(2)}) collective-permute-start(bf16[1024,2048]{1,0:T(8,128)(2,1)} %pad_maximum_fusion.1), channel_id=1, source_target_pairs={{0,8},{8,0},{16,24},{24,16},{1,9},{9,1},{17,25},{25,17},{2,10},{10... | collective-permute-start | bytes 12582920 | tf_op jit(solution)/shard_map/ppermute | solution.py:423
  382.5 170.4 %all-gather.13.cloned.1.call-start = ((), (), s32[]{:S(2)}) async-start(), calls=%async_computation.14 | async-start | bytes 4718592 | tf_op jit(solution)/shard_map/all_gather | solution.py:373
  387.1 48.4 %collective-permute-start.10 = (bf16[512,2048]{1,0:T(8,128)(2,1)}, bf16[512,2048]{1,0:T(8,128)(2,1)}, u32[]{:S(2)}, u32[]{:S(2)}) collective-permute-start(bf16[512,2048]{1,0:T(8,128)(2,1)} %add_convert_fusion.1), channel_id=1, source_target_pairs={{0,16},{8,24},{16,0},{24,8},{1,17},{9,25},{17,1},{25,9},{2,18},{10... | collective-permute-start | bytes 6291464 | tf_op jit(solution)/shard_map/ppermute | solution.py:275
  399.6 44.4 %all-to-all-start.2 = ((bf16[8,128,256]{2,1,0:T(8,128)(2,1)}), bf16[8,128,256]{2,1,0:T(8,128)(2,1)S(1)}, u32[]{:S(2)}, u32[]{:S(2)}) async-start(bf16[8,128,256]{2,1,0:T(8,128)(2,1)} %shard_map.210), calls=%async_computation.3 | async-start | bytes 1048576 | tf_op jit(solution)/shard_map/all_to_all | solution.py:572
  444.8 76.3 %all-to-all-start.3 = ((bf16[8,64,2048]{2,1,0:T(8,128)(2,1)}), bf16[8,64,2048]{2,1,0:T(8,128)(2,1)S(1)}, u32[]{:S(2)}, u32[]{:S(2)}) async-start(bf16[8,64,2048]{2,1,0:T(8,128)(2,1)} %bitcast.135), calls=%async_computation.5 | async-start | bytes 4194304 | tf_op jit(solution)/shard_map/all_to_all | solution.py:577
  449.8 158.6 %reduce-scatter.8.cloned.1.call-start = ((), (), s32[]{:S(2)}) async-start(), calls=%async_computation.13 | async-start | bytes 4718592 | tf_op jit(solution)/shard_map/reduce_scatter | solution.py:377
  469.7 25.0 %collective-permute-start.12 = (bf16[256,2048]{1,0:T(8,128)(2,1)}, bf16[256,2048]{1,0:T(8,128)(2,1)}, u32[]{:S(2)}, u32[]{:S(2)}) collective-permute-start(bf16[256,2048]{1,0:T(8,128)(2,1)} %add_convert_fusion.2), channel_id=1, source_target_pairs={{0,16},{8,24},{16,0},{24,8},{1,17},{9,25},{17,1},{25,9},{2,18},{10... | collective-permute-start | bytes 3145736 | tf_op jit(solution)/shard_map/ppermute | solution.py:275
  549.1 22.7 %collective-permute-start.14 = (bf16[512,896]{0,1:T(8,128)(2,1)}, bf16[512,896]{0,1:T(8,128)(2,1)}, u32[]{:S(2)}, u32[]{:S(2)}) collective-permute-start(bf16[512,896]{0,1:T(8,128)(2,1)} %fusion.29), channel_id=1, source_target_pairs={{0,16},{8,24},{16,0},{24,8},{1,17},{9,25},{17,1},{25,9},{2,18},{10... | collective-permute-start | bytes 2752520 | tf_op jit(solution)/shard_map/ppermute | solution.py:275
  559.0 22.0 %collective-permute-start.15 = (bf16[128,2048]{1,0:T(8,128)(2,1)}, bf16[128,2048]{1,0:T(8,128)(2,1)}, u32[]{:S(2)}, u32[]{:S(2)}) collective-permute-start(bf16[128,2048]{1,0:T(8,128)(2,1)} %pad_maximum_fusion.12), channel_id=1, source_target_pairs={{0,8},{8,0},{16,24},{24,16},{1,9},{9,1},{17,25},{25,17},{2,10},{10... | collective-permute-start | bytes 1572872 | tf_op jit(solution)/shard_map/ppermute | solution.py:423
  577.2 29.1 %all-to-all-start.4 = ((bf16[8,64,896]{2,1,0:T(8,128)(2,1)}), bf16[8,64,896]{2,1,0:T(8,128)(2,1)S(1)}, u32[]{:S(2)}, u32[]{:S(2)}) async-start(bf16[8,64,896]{2,1,0:T(8,128)(2,1)} %bitcast.140), calls=%async_computation.7 | async-start | bytes 1835008 | tf_op jit(solution)/shard_map/all_to_all | solution.py:445
  (75 other events, 508.3 us)
Sparse Core Ops, SparseCore 0:
  9.6 68.9 all-gather.14
  80.1 102.9 all-gather.6
  185.2 46.3 all-gather.8
  236.6 47.8 all-gather.10
  332.8 48.4 reduce-scatter.3
  383.5 58.1 reduce-scatter.5
  443.8 91.7 all-gather.12
  537.9 52.0 reduce-scatter.7

commit v5 on v4

--- a/solution.py
+++ b/solution.py
@@ -492,10 +492,10 @@
     blocks = cut_columns((w_query, w_key, w_value), 1, beside)
     qkv_mine = lax.all_to_all(blocks, "ctx", 0, 0, tiled=True).reshape(n * weight_rows, -1)
     down_far = down_steps[2][1]
-    late_out, qkv_mine, down_far.value = lax.optimization_barrier((w_out, qkv_mine, down_far.value))
+    late_out, late_gate, late_up, qkv_mine, down_far.value = lax.optimization_barrier(
+        (w_out, w_gate, w_up, qkv_mine, down_far.value)
+    )
     qkv_steps = gather_seq(x, qkv_mine)
-    far = qkv_steps[2][1]
-    late_gate, late_up, far.value = lax.optimization_barrier((w_gate, w_up, far.value))
     out_stack = lax.all_gather(
         late_out, ("seq", "ctx"), axis=0, tiled=True, axis_index_groups=[whole_ring()]
     )
@@ -524,15 +524,28 @@
     split = width // 2
     halves = [slice(0, split), slice(split, width)]
     att_first, lse_first = attention(*(m[:, halves[0]] for m in (query, key, value)), pos_all)
+    value, gate_up = lax.optimization_barrier((value, gate_up))
     att_second, lse_second = attention(*(m[:, halves[1]] for m in (query, key, value)), pos_all)
     att_low = jnp.concatenate([att_first, att_second], axis=1).astype(bf16)
-    att_low, out_stack, gate_up = lax.optimization_barrier((att_low, out_stack, gate_up))
-    gate_up = from_devices(gather_seq(x, gate_up))
+    cut = gate_up.shape[0] // 2
+    parts = [gate_up[:cut], gate_up[cut:]]
+    far = [x.swap(parts[0], 2)]
+    att_low, out_stack, far[0].value = lax.optimization_barrier((att_low, out_stack, far[0].value))
     att_stack = gather_ring(att_low)
+    far.append(x.swap(parts[1], 2))
+    held = []
+    for part, other in zip(parts, far):
+        held += [(0, part), (1, core_swap(part)), (2, other), (3, core_swap(other))]
+    gate_up = place(
+        [part for _, part in held],
+        [(seq_here ^ o) * 2 + i // 4 for i, (o, _) in enumerate(held)],
+    )
     full_out = rearranged(out_stack, whole_ring())
+    late_grad, att_stack, full_out, gate_up, down_sub = lax.optimization_barrier(
+        (out_grad[0], att_stack, full_out, gate_up, down_sub)
+    )
+    grad_all = gather_ring(late_grad)
     att_low = rearranged(att_stack, ring(), columns=True)
-    late_grad, att_low = lax.optimization_barrier((out_grad[0], att_low))
-    grad_all = gather_ring(late_grad)
 
     middle = x_all + dot(att_low, full_out)
     mlp_scale = rms_scale(middle)
@@ -544,6 +557,9 @@
     inner = (gate_act * sig * up_act).astype(bf16)
     middle_own = own_rows(middle)
 
+    down_part = dot(inner, down_sub).astype(bf16)
+    grad_all, down_part = lax.optimization_barrier((grad_all, down_part))
+    down_own = scatter_ring(down_part)
     inner_grad = lax.optimization_barrier(dot_cols(grad_all, down_sub))
     gate_grad = (inner_grad * up_act * sig * (1.0 + gate_act * (1.0 - sig))).astype(bf16)
     up_grad = (inner_grad * gate_act * sig).astype(bf16)
@@ -552,12 +568,10 @@
     gate_up_near, gate_up_far = scatter_seq_near(dot_rows(normed_mid, gate_up_grad), seq_here)
     mid_grad_in = scatter_ring(mid_grad_part)
     down_weight_part = dot_rows(inner, grad_all)
-    down_part = dot(inner, down_sub).astype(bf16)
-    mid_grad_in, down_weight_part, down_part, gate_up_far = lax.optimization_barrier(
-        (mid_grad_in, down_weight_part, down_part, gate_up_far)
-    )
     gate_up_far = x.swap(gate_up_far, 2)
-    down_own = scatter_ring(down_part)
+    mid_grad_in, down_weight_part, down_own, gate_up_far.value = lax.optimization_barrier(
+        (mid_grad_in, down_weight_part, down_own, gate_up_far.value)
+    )
 
     mid_scale = own_rows(mlp_scale)
     mid_unit = middle_own * mid_scale
@@ -572,10 +586,10 @@
     att_grad = lax.all_to_all(blocks, "ctx", 0, 0, tiled=True, axis_index_groups=[ring()])
     att_grad = att_grad.reshape(n * rows, -1)
     middle_low_all = gather_ring(middle_low)
+
     gate_up_sum = (gate_up_near + gate_up_far.value.astype(f32)).astype(bf16)
-    att_grad, gate_up_sum, down_own = lax.optimization_barrier((att_grad, gate_up_sum, down_own))
+    att_grad, gate_up_sum = lax.optimization_barrier((att_grad, gate_up_sum))
     w_gate_up = lax.all_to_all(gate_up_sum.reshape(n, weight_rows, -1), "ctx", 0, 0, tiled=True)
-
     grads = [
         attention_back(
             *(m[:, halves[0]] for m in (query, key, value)), pos_all, att_first, lse_first, att_grad[:, halves[0]]
@@ -605,8 +619,9 @@
     )
     w_out_near, w_out_far = scatter_seq_near(dot_rows(att_sub, middle_low_all), seq_here)
     hidden_out = (middle_own + down_own).astype(bf16)
-    qkv_grad, w_gate_up, down_weight_far.value = lax.optimization_barrier(
-        (qkv_grad, w_gate_up, down_weight_far.value)
+    w_down_grad = down_weight_near + down_weight_far.value.astype(f32)
+    qkv_grad, w_gate_up, w_down_grad, w_out_far = lax.optimization_barrier(
+        (qkv_grad, w_gate_up, w_down_grad, w_out_far)
     )
     normed_grad_part = dot_cols(qkv_grad, qkv_sub)
     attn_gain_part = jnp.sum(normed_grad_part * (x_all * attn_scale), axis=0)
@@ -620,11 +635,8 @@
     w_query_grad, w_key_grad, w_value_grad, gain_grads = to_owners(qkv_sum, 3, 1, 128)
     gain_grads = gain_grads.astype(f32).reshape(weight_rows, n, 128).sum(axis=1)
     w_out_grad = w_out_near + Link("seq", 1).swap(w_out_far, 2).value.astype(f32)
-    down_weight_far, w_gate_up, normed_grad = lax.optimization_barrier(
-        (down_weight_far.value, w_gate_up, normed_grad)
-    )
+    w_out_grad, normed_grad = lax.optimization_barrier((w_out_grad, normed_grad))
     w_gate_grad, w_up_grad = paste_columns(w_gate_up, 2, seqs)
-    w_down_grad = down_weight_near + down_weight_far.astype(f32)
 
     own_scale = own_rows(attn_scale)
     own_unit = hidden_in[0].astype(f32) * own_scale

time: 633 us -> 613 us (0.968)
  waiting for transfers between devices: 269 us -> 258 us
  local copies, waits for them, and re-layouts: 70.1 us -> 61.7 us
    reduce_scatter x3, waiting for transfers between devices: 4.22 us -> 25 us  [scatter_ring(): lax.psum_scatter(total, 'ctx', scatter_dimension=0, tiled=True, axis_inde...]
    all_to_all x1, waiting for transfers between devices: 26.3 us -> 6.05 us  [tuned(): lax.all_to_all(gate_up_sum.reshape(n, weight_rows, -1), 'ctx', 0, 0, tile...]
    all_gather x4, waiting for transfers between devices: 47.5 us -> 28.2 us  [gather_ring(): lax.all_gather(block, 'ctx', axis=0, tiled=True, axis_index_groups=[ring()])]
    unnamed x147 -> x149, local copies, waits for them, and re-layouts: 50.9 us -> 38.1 us
    all_to_all x1, waiting for transfers between devices: 0.01 us -> 12.5 us  [tuned(): lax.all_to_all(blocks, 'ctx', 0, 0, tiled=True, axis_index_groups=[ring()])]
    all_to_all x2, waiting for transfers between devices: 40.5 us -> 28.1 us  [tuned(): lax.all_to_all(blocks, 'ctx', 0, 0, tiled=True).reshape(n * weight_rows, -1)]
    ppermute x7 -> x8, waiting for transfers between devices: 94.6 us -> 107 us  [swap(): lax.ppermute(value_of(block), self.axis, [(i, i ^ mask) for i in range(n)])]
    dot_general x4, matrix products: 44.4 us -> 37.2 us  [dot_cols(): lax.dot_general(left, right, (((1,), (1,)), ((), ())), preferred_element_...]
  transfers between devices with their start and end apart: 30 -> 33, of which waited for: 17 -> 22; matrix products, arithmetic and copies ran while one was open for 32% -> 36% of each run, Pallas kernels for 2% -> 3%
where the time goes in v5:
time: 613 us; the launch traced here: 608 us
  waiting for transfers between devices  258 us (42%)
  matrix products  150 us (24%)
  other arithmetic  64.2 us (10%)
  local copies, waits for them, and re-layouts  61.7 us (10%)
  starting transfers between devices  42.4 us (7%)
  Pallas kernels  16.8 us (3%)
  between operations  15.7 us (3%)
    ppermute x8, waiting for transfers between devices, swap(): lax.ppermute(value_of(block), self.axis, [(i, i ^ mask) for i in range(n)])  107 us
    dot_general x4, matrix products, dot(): return jnp.dot(left, right, preferred_element_type=f32)  39.6 us
    unnamed x149, local copies, waits for them, and re-layouts  38.1 us
    dot_general x4, matrix products, dot_cols(): lax.dot_general(left, right, (((1,), (1,)), ((), ())), preferred_element_...  37.2 us
    dot_general x4, matrix products, dot_rows(): lax.dot_general(left, right, (((0,), (0,)), ((), ())), preferred_element_...  32.8 us
    all_gather x4, waiting for transfers between devices, gather_ring(): lax.all_gather(block, 'ctx', axis=0, tiled=True, axis_index_groups=[ring()])  28.2 us
    all_to_all x2, waiting for transfers between devices, tuned(): lax.all_to_all(blocks, 'ctx', 0, 0, tiled=True).reshape(n * weight_rows, -1)  28.1 us
    reduce_scatter x3, waiting for transfers between devices, scatter_ring(): lax.psum_scatter(total, 'ctx', scatter_dimension=0, tiled=True, axis_inde...  25 us
  transfers between devices with their start and end apart: 33, of which 22 were waited for; matrix products, arithmetic and copies ran while one was open for 36% of the time, Pallas kernels for 3%

profile of v5, /device:TPU:0, one launch (start us, length us, event | category | flops | bytes accessed | tf_op | source)
XLA Modules:
  0.0 608.4 jit_solution(6801337665383137613)
XLA Ops:
  14.8 7.3 %all-to-all-start = ((bf16[8,64,896]{2,1,0:T(8,128)(2,1)}), bf16[8,64,896]{2,1,0:T(8,128)(2,1)S(1)}, u32[]{:S(2)}, u32[]{:S(2)}) async-start(bf16[8,64,896]{2,1,0:T(8,128)(2,1)} %shard_map.203), calls=%async_computation | async-start | bytes 1835008 | tf_op jit(solution)/shard_map/all_to_all | solution.py:493
  23.7 23.1 %collective-permute-done.refs_2_ = bf16[256,2048]{1,0:T(8,128)(2,1)S(1)} collective-permute-done((bf16[256,2048]{1,0:T(8,128)(2,1)S(1)}, bf16[256,2048]{1,0:T(8,128)(2,1)S(1)}, u32[]{:S(2)}, u32[]{:S(2)}) %collective-permute-start) | collective-permute-done | bytes 1048608 | tf_op jit(solution)/shard_map/ppermute | solution.py:275
  46.8 8.5 %all-to-all-done = bf16[8,64,896]{2,1,0:T(8,128)(2,1)S(1)} async-done(((bf16[8,64,896]{2,1,0:T(8,128)(2,1)}), bf16[8,64,896]{2,1,0:T(8,128)(2,1)S(1)}, u32[]{:S(2)}, u32[]{:S(2)}) %all-to-all-start) | async-done | bytes 917536 | tf_op jit(solution)/shard_map/all_to_all | solution.py:493
  66.8 8.3 %collective-permute-done.2.refs_2_ = bf16[512,896]{1,0:T(8,128)(2,1)} collective-permute-done((bf16[512,896]{1,0:T(8,128)(2,1)S(1)}, bf16[512,896]{1,0:T(8,128)(2,1)}, u32[]{:S(2)}, u32[]{:S(2)}) %collective-permute-start.2) | collective-permute-done | bytes 917536 | tf_op jit(solution)/shard_map/ppermute | solution.py:275
  82.9 11.1 %all-gather.15.cloned.1.call-done = bf16[1,1024,2048]{2,1,0:T(8,128)(2,1)} async-done(((bf16[1,128,2048]{2,1,0:T(8,128)(2,1)}), bf16[1,1024,2048]{2,1,0:T(8,128)(2,1)}) %all-gather.15.cloned.1.call-update) | async-done | bytes 4194320 | tf_op jit(solution)/shard_map/all_gather | solution.py:373
  97.3 7.5 %fusion.97 = (bf16[1024,768]{0,1:T(8,128)(2,1)S(1)}, f32[1024,768]{0,1:T(8,128)}) fusion(bf16[2048,896]{1,0:T(8,128)(2,1)S(1)} %copy-done.6, bf16[1,1024,2048]{2,1,0:T(8,128)(2,1)} %all-gather.15.cloned.1.call-done, f32[2048]{0:T(1024)S(1)} %get-tuple-element.104, f32[1024]{0:T(1024)S(1)} %add_rsqrt_fusion.1), kind=kOutput, calls=%fused_computation.198 | convolution fusion | flops 3230400512 | bytes 12070912 | tf_op jit(solution)/shard_map/dot_general | solution.py:65
  106.4 19.6 %all-to-all-done.1 = bf16[8,64,2048]{2,1,0:T(8,128)(2,1)} async-done(((bf16[8,64,2048]{2,1,0:T(8,128)(2,1)}), bf16[8,64,2048]{2,1,0:T(8,128)(2,1)}, u32[]{:S(2)}, u32[]{:S(2)}) %all-to-all-start.1) | async-done | bytes 2097184 | tf_op jit(solution)/shard_map/all_to_all | solution.py:503
  158.3 17.2 %collective-permute-done.4.refs_2_ = bf16[256,2048]{1,0:T(8,128)(2,1)} collective-permute-done((bf16[256,2048]{1,0:T(8,128)(2,1)S(1)}, bf16[256,2048]{1,0:T(8,128)(2,1)}, u32[]{:S(2)}, u32[]{:S(2)}) %collective-permute-start.4) | collective-permute-done | bytes 1048608 | tf_op jit(solution)/shard_map/ppermute | solution.py:275
  175.5 20.1 %all-gather.7.cloned.1.call-done.stack_ref = bf16[2048,2048]{1,0:T(8,128)(2,1)} async-done(((bf16[64,2048]{1,0:T(8,128)(2,1)}), bf16[2048,2048]{1,0:T(8,128)(2,1)}) %all-gather.7.cloned.1.call-update) | async-done | bytes 8388624 | tf_op jit(solution)/shard_map/all_gather | solution.py:499
  199.6 21.8 %collective-permute-done.8.refs_6_ = bf16[256,2048]{1,0:T(8,128)(2,1)} collective-permute-done((bf16[256,2048]{1,0:T(8,128)(2,1)S(1)}, bf16[256,2048]{1,0:T(8,128)(2,1)}, u32[]{:S(2)}, u32[]{:S(2)}) %collective-permute-start.8) | collective-permute-done | bytes 1048608 | tf_op jit(solution)/shard_map/ppermute | solution.py:275
  249.4 14.5 %multiply_reduce_fusion = (f32[1024]{0:T(1024)S(1)}, f32[1024,2048]{1,0:T(8,128)}) fusion(bf16[1024,2048]{1,0:T(8,128)(2,1)S(1)} %shard_map.209, bf16[2048,2048]{1,0:T(8,128)(2,1)S(1)} %copy-done.1, bf16[1,1024,2048]{2,1,0:T(8,128)(2,1)} %all-gather.15.cloned.1.call-done), kind=kOutput, calls=%fused_computation.17 | convolution fusion | flops 8598322176 | bytes 25169920 | tf_op jit(solution)/shard_map/dot_general | solution.py:65
  263.9 11.5 %fusion.90 = f32[1024,2048]{1,0:T(8,128)S(1)} fusion(bf16[2048,2048]{1,0:T(8,128)(2,1)S(1)} %bitcast.135, f32[1024,2048]{1,0:T(8,128)} %get-tuple-element.172, f32[2048]{0:T(1024)S(1)} %get-tuple-element.103, f32[1024]{0:T(1024)S(1)} %add_rsqrt_fusion), kind=kOutput, calls=%fused_computation.191 | convolution fusion | flops 8596226048 | bytes 25178112 | tf_op jit(solution)/shard_map/dot_general | solution.py:65
  293.2 8.0 %fusion.100 = f32[1024,1024]{1,0:T(8,128)S(1)} fusion(bf16[1024,2048]{1,0:T(8,128)(2,1)} %all-gather.11.cloned.1.call-done, bf16[1024,2048]{1,0:T(8,128)(2,1)} %copy-done.8), kind=kOutput, calls=%fused_computation.201 | convolution fusion | flops 4294967296 | bytes 12582912 | tf_op jit(solution)/shard_map/dot_general | solution.py:73
  306.2 12.7 %convolution_convert_fusion = bf16[1024,2048]{1,0:T(8,128)(2,1)} fusion(bf16[1024,2048]{1,0:T(8,128)(2,1)S(1)} %pad_maximum_fusion, bf16[2048,2048]{1,0:T(8,128)(2,1)} %copy-done.2), kind=kOutput, calls=%fused_computation.50 | convolution fusion | flops 8592031744 | bytes 16777216 | tf_op jit(solution)/shard_map/dot_general | solution.py:73
  319.0 13.7 %fusion.89 = f32[2048,2048]{1,0:T(8,128)S(1)} fusion(bf16[1024,2048]{1,0:T(8,128)(2,1)} %copy-done.33, f32[1024,2048]{1,0:T(8,128)} %get-tuple-element.172, f32[2048]{0:T(1024)S(1)} %get-tuple-element.103, f32[1024]{0:T(1024)S(1)} %add_rsqrt_fusion), kind=kOutput, calls=%fused_computation.190 | convolution fusion | flops 8596226048 | bytes 29372416 | tf_op jit(solution)/shard_map/dot_general | solution.py:69
  341.6 7.5 %collective-permute-done.12 = bf16[1024,2048]{1,0:T(8,128)(2,1)} collective-permute-done((bf16[1024,2048]{1,0:T(8,128)(2,1)}, bf16[1024,2048]{1,0:T(8,128)(2,1)}, u32[]{:S(2)}, u32[]{:S(2)}) %collective-permute-start.12) | collective-permute-done | bytes 4194336 | tf_op jit(solution)/shard_map/ppermute | solution.py:423
  358.2 9.0 %fusion.101 = f32[1024,2048]{1,0:T(8,128)} fusion(bf16[1024,1024]{1,0:T(8,128)(2,1)S(1)} %multiply_convert_fusion.5, bf16[1024,2048]{1,0:T(8,128)(2,1)} %all-gather.11.cloned.1.call-done), kind=kOutput, calls=%fused_computation.202 | convolution fusion | flops 4294967296 | bytes 14680064 | tf_op jit(solution)/shard_map/dot_general | solution.py:69
  369.4 25.0 %reduce-scatter.4.cloned.1.call-done = bf16[128,2048]{1,0:T(8,128)(2,1)} async-done(((bf16[1024,2048]{1,0:T(8,128)(2,1)}), bf16[128,2048]{1,0:T(8,128)(2,1)}) %reduce-scatter.4.cloned.1.call-update) | async-done | bytes 524304 | tf_op jit(solution)/shard_map/reduce_scatter | solution.py:377
  428.8 12.5 %all-to-all-done.2 = bf16[8,128,256]{2,1,0:T(8,128)(2,1)S(1)} async-done(((bf16[8,128,256]{2,1,0:T(8,128)(2,1)}), bf16[8,128,256]{2,1,0:T(8,128)(2,1)S(1)}, u32[]{:S(2)}, u32[]{:S(2)}) %all-to-all-start.2) | async-done | bytes 524320 | tf_op jit(solution)/shard_map/all_to_all | solution.py:586
  483.2 6.6 %all-gather.13.cloned.1.call-done = bf16[1024,2048]{1,0:T(8,128)(2,1)} async-done(((bf16[128,2048]{1,0:T(8,128)(2,1)}), bf16[1024,2048]{1,0:T(8,128)(2,1)}) %all-gather.13.cloned.1.call-update) | async-done | bytes 4194320 | tf_op jit(solution)/shard_map/all_gather | solution.py:373
  511.1 10.1 %fusion.3 = (f32[2048]{0:T(1024)S(1)}, bf16[1024,2048]{1,0:T(8,128)(2,1)}) fusion(bf16[1,1024,2048]{2,1,0:T(8,128)(2,1)} %all-gather.15.cloned.1.call-done, f32[1024]{0:T(1024)S(1)} %copy-done.63, bf16[1024,768]{0,1:T(8,128)(2,1)} %pad_maximum_fusion.4, bf16[2048,896]{1,0:T(8,128)(2,1)} %copy-done.5), kind=kOutput, calls=%fused_computation.10 | convolution fusion | flops 3231709184 | bytes 13119488 | tf_op jit(solution)/shard_map/dot_general | solution.py:73
  534.5 20.9 %collective-permute-done.19 = bf16[512,896]{0,1:T(8,128)(2,1)S(1)} collective-permute-done((bf16[512,896]{0,1:T(8,128)(2,1)S(1)}, bf16[512,896]{0,1:T(8,128)(2,1)S(1)}, u32[]{:S(2)}, u32[]{:S(2)}) %collective-permute-start.19) | collective-permute-done | bytes 917536 | tf_op jit(solution)/shard_map/ppermute | solution.py:275
  557.2 9.5 %all-to-all-start.4 = ((bf16[8,64,896]{2,1,0:T(8,128)(2,1)}), bf16[8,64,896]{2,1,0:T(8,128)(2,1)S(1)}, u32[]{:S(2)}, u32[]{:S(2)}) async-start(bf16[8,64,896]{2,1,0:T(8,128)(2,1)} %bitcast.148), calls=%async_computation.7 | async-start | bytes 1835008 | tf_op jit(solution)/shard_map/all_to_all | solution.py:445
  576.4 17.8 %all-to-all-done.4.ref = bf16[8,64,896]{2,1,0:T(8,128)(2,1)S(1)} async-done(((bf16[8,64,896]{2,1,0:T(8,128)(2,1)}), bf16[8,64,896]{2,1,0:T(8,128)(2,1)S(1)}, u32[]{:S(2)}, u32[]{:S(2)}) %all-to-all-start.4) | async-done | bytes 917536 | tf_op jit(solution)/shard_map/all_to_all | solution.py:445
  (328 shorter events, 268.8 us)
Async XLA Ops:
  7.2 86.8 %all-gather.15.cloned.1.call-start = ((), (), s32[]{:S(2)}) async-start(), calls=%async_computation.15 | async-start | bytes 4718592 | tf_op jit(solution)/shard_map/all_gather | solution.py:373
  14.8 40.5 %all-to-all-start = ((bf16[8,64,896]{2,1,0:T(8,128)(2,1)}), bf16[8,64,896]{2,1,0:T(8,128)(2,1)S(1)}, u32[]{:S(2)}, u32[]{:S(2)}) async-start(bf16[8,64,896]{2,1,0:T(8,128)(2,1)} %shard_map.203), calls=%async_computation | async-start | bytes 1835008 | tf_op jit(solution)/shard_map/all_to_all | solution.py:493
  22.1 173.6 %all-gather.7.cloned.1.call-start = ((), (), s32[]{:S(2)}) async-start(), calls=%async_computation.8 | async-start | bytes 8650752 | tf_op jit(solution)/shard_map/all_gather | solution.py:499
  22.1 24.7 %collective-permute-start = (bf16[256,2048]{1,0:T(8,128)(2,1)S(1)}, bf16[256,2048]{1,0:T(8,128)(2,1)S(1)}, u32[]{:S(2)}, u32[]{:S(2)}) collective-permute-start(bf16[256,2048]{1,0:T(8,128)(2,1)S(1)} %copy-done.10), channel_id=1, source_target_pairs={{0,16},{8,24},{16,0},{24,8},{1,17},{9,25},{17,1},{25,9},{2,18},{10... | collective-permute-start | bytes 3145736 | tf_op jit(solution)/shard_map/ppermute | solution.py:275
  60.9 65.1 %all-to-all-start.1 = ((bf16[8,64,2048]{2,1,0:T(8,128)(2,1)}), bf16[8,64,2048]{2,1,0:T(8,128)(2,1)}, u32[]{:S(2)}, u32[]{:S(2)}) async-start(bf16[8,64,2048]{2,1,0:T(8,128)(2,1)} %shard_map.205), calls=%async_computation.1 | async-start | bytes 4194304 | tf_op jit(solution)/shard_map/all_to_all | solution.py:503
  65.3 178.5 %all-gather.9.cloned.1.call-start = ((), (), s32[]{:S(2)}) async-start(), calls=%async_computation.9 | async-start | bytes 4718592 | tf_op jit(solution)/shard_map/all_gather | solution.py:373
  127.9 47.6 %collective-permute-start.4 = (bf16[256,2048]{1,0:T(8,128)(2,1)S(1)}, bf16[256,2048]{1,0:T(8,128)(2,1)}, u32[]{:S(2)}, u32[]{:S(2)}) collective-permute-start(bf16[256,2048]{1,0:T(8,128)(2,1)S(1)} %get-tuple-element.62.refs_0_), channel_id=1, source_target_pairs={{0,16},{8,24},{16,0},{24,8},{1,17},{9,25},{17,1},{25,9},{2,18},{10... | collective-permute-start | bytes 3145736 | tf_op jit(solution)/shard_map/ppermute | solution.py:275
  195.6 97.5 %all-gather.11.cloned.1.call-start = ((), (), s32[]{:S(2)}) async-start(), calls=%async_computation.10 | async-start | bytes 4718592 | tf_op jit(solution)/shard_map/all_gather | solution.py:373
  196.0 25.4 %collective-permute-start.8 = (bf16[256,2048]{1,0:T(8,128)(2,1)S(1)}, bf16[256,2048]{1,0:T(8,128)(2,1)}, u32[]{:S(2)}, u32[]{:S(2)}) collective-permute-start(bf16[256,2048]{1,0:T(8,128)(2,1)S(1)} %get-tuple-element.67.refs_4_), channel_id=1, source_target_pairs={{0,16},{8,24},{16,0},{24,8},{1,17},{9,25},{17,1},{25,9},{2,18},{10... | collective-permute-start | bytes 3145736 | tf_op jit(solution)/shard_map/ppermute | solution.py:275
  196.8 24.8 %collective-permute-start.11 = (bf16[256,2048]{1,0:T(8,128)(2,1)}, bf16[256,2048]{1,0:T(8,128)(2,1)}, u32[]{:S(2)}, u32[]{:S(2)}) collective-permute-start(bf16[256,2048]{1,0:T(8,128)(2,1)} %copy-done.11), channel_id=1, source_target_pairs={{0,8},{8,0},{16,24},{24,16},{1,9},{9,1},{17,25},{25,17},{2,10},{10... | collective-permute-start | bytes 3145736 | tf_op jit(solution)/shard_map/ppermute | solution.py:423
  196.8 35.9 %collective-permute-start.7 = (bf16[256,2048]{1,0:T(8,128)(2,1)S(1)}, bf16[256,2048]{1,0:T(8,128)(2,1)}, u32[]{:S(2)}, u32[]{:S(2)}) collective-permute-start(bf16[256,2048]{1,0:T(8,128)(2,1)S(1)} %get-tuple-element.67.refs_4_), channel_id=1, source_target_pairs={{0,8},{8,0},{16,24},{24,16},{1,9},{9,1},{17,25},{25,17},{2,10},{10... | collective-permute-start | bytes 3145736 | tf_op jit(solution)/shard_map/ppermute | solution.py:423
  197.3 35.4 %collective-permute-start.5 = (bf16[256,2048]{1,0:T(8,128)(2,1)S(1)}, bf16[256,2048]{1,0:T(8,128)(2,1)}, u32[]{:S(2)}, u32[]{:S(2)}) collective-permute-start(bf16[256,2048]{1,0:T(8,128)(2,1)S(1)} %get-tuple-element.62.refs_0_), channel_id=1, source_target_pairs={{0,8},{8,0},{16,24},{24,16},{1,9},{9,1},{17,25},{25,17},{2,10},{10... | collective-permute-start | bytes 3145736 | tf_op jit(solution)/shard_map/ppermute | solution.py:423
  199.4 33.3 %collective-permute-start.6 = (bf16[256,2048]{1,0:T(8,128)(2,1)}, bf16[256,2048]{1,0:T(8,128)(2,1)}, u32[]{:S(2)}, u32[]{:S(2)}) collective-permute-start(bf16[256,2048]{1,0:T(8,128)(2,1)} %collective-permute-done.4.refs_2_), channel_id=1, source_target_pairs={{0,8},{8,0},{16,24},{24,16},{1,9},{9,1},{17,25},{25,17},{2,10},{10... | collective-permute-start | bytes 3145736 | tf_op jit(solution)/shard_map/ppermute | solution.py:423
  243.8 123.4 %reduce-scatter.6.cloned.1.call-start = ((), (), s32[]{:S(2)}) async-start(), calls=%async_computation.12 | async-start | bytes 4718592 | tf_op jit(solution)/shard_map/reduce_scatter | solution.py:377
  293.1 101.3 %reduce-scatter.4.cloned.1.call-start = ((), (), s32[]{:S(2)}) async-start(), calls=%async_computation.11 | async-start | bytes 4718592 | tf_op jit(solution)/shard_map/reduce_scatter | solution.py:377
  318.9 170.8 %all-gather.13.cloned.1.call-start = ((), (), s32[]{:S(2)}) async-start(), calls=%async_computation.13 | async-start | bytes 4718592 | tf_op jit(solution)/shard_map/all_gather | solution.py:373
  354.1 48.0 %collective-permute-start.13 = (bf16[512,2048]{1,0:T(8,128)(2,1)}, bf16[512,2048]{1,0:T(8,128)(2,1)}, u32[]{:S(2)}, u32[]{:S(2)}) collective-permute-start(bf16[512,2048]{1,0:T(8,128)(2,1)} %add_convert_fusion.1), channel_id=1, source_target_pairs={{0,16},{8,24},{16,0},{24,8},{1,17},{9,25},{17,1},{25,9},{2,18},{10... | collective-permute-start | bytes 6291464 | tf_op jit(solution)/shard_map/ppermute | solution.py:275
  413.9 27.4 %all-to-all-start.2 = ((bf16[8,128,256]{2,1,0:T(8,128)(2,1)}), bf16[8,128,256]{2,1,0:T(8,128)(2,1)S(1)}, u32[]{:S(2)}, u32[]{:S(2)}) async-start(bf16[8,128,256]{2,1,0:T(8,128)(2,1)} %shard_map.210), calls=%async_computation.4 | async-start | bytes 1048576 | tf_op jit(solution)/shard_map/all_to_all | solution.py:586
  422.9 40.2 %collective-permute-start.15 = (bf16[512,2048]{1,0:T(8,128)(2,1)}, bf16[512,2048]{1,0:T(8,128)(2,1)}, u32[]{:S(2)}, u32[]{:S(2)}) collective-permute-start(bf16[512,2048]{1,0:T(8,128)(2,1)} %pad_maximum_fusion.2), channel_id=1, source_target_pairs={{0,8},{8,0},{16,24},{24,16},{1,9},{9,1},{17,25},{25,17},{2,10},{10... | collective-permute-start | bytes 6291464 | tf_op jit(solution)/shard_map/ppermute | solution.py:423
  441.3 69.8 %all-to-all-start.3 = ((bf16[8,64,2048]{2,1,0:T(8,128)(2,1)}), bf16[8,64,2048]{2,1,0:T(8,128)(2,1)S(1)}, u32[]{:S(2)}, u32[]{:S(2)}) async-start(bf16[8,64,2048]{2,1,0:T(8,128)(2,1)} %bitcast.143), calls=%async_computation.5 | async-start | bytes 4194304 | tf_op jit(solution)/shard_map/all_to_all | solution.py:592
  444.9 151.3 %reduce-scatter.8.cloned.1.call-start = ((), (), s32[]{:S(2)}) async-start(), calls=%async_computation.14 | async-start | bytes 4718592 | tf_op jit(solution)/shard_map/reduce_scatter | solution.py:377
  476.6 23.6 %collective-permute-start.16 = (bf16[256,2048]{1,0:T(8,128)(2,1)}, bf16[256,2048]{1,0:T(8,128)(2,1)}, u32[]{:S(2)}, u32[]{:S(2)}) collective-permute-start(bf16[256,2048]{1,0:T(8,128)(2,1)} %add_convert_fusion.2), channel_id=1, source_target_pairs={{0,16},{8,24},{16,0},{24,8},{1,17},{9,25},{17,1},{25,9},{2,18},{10... | collective-permute-start | bytes 3145736 | tf_op jit(solution)/shard_map/ppermute | solution.py:275
  533.0 22.5 %collective-permute-start.19 = (bf16[512,896]{0,1:T(8,128)(2,1)S(1)}, bf16[512,896]{0,1:T(8,128)(2,1)S(1)}, u32[]{:S(2)}, u32[]{:S(2)}) collective-permute-start(bf16[512,896]{0,1:T(8,128)(2,1)S(1)} %fusion.29), channel_id=1, source_target_pairs={{0,16},{8,24},{16,0},{24,8},{1,17},{9,25},{17,1},{25,9},{2,18},{10... | collective-permute-start | bytes 2752520 | tf_op jit(solution)/shard_map/ppermute | solution.py:275
  557.2 37.0 %all-to-all-start.4 = ((bf16[8,64,896]{2,1,0:T(8,128)(2,1)}), bf16[8,64,896]{2,1,0:T(8,128)(2,1)S(1)}, u32[]{:S(2)}, u32[]{:S(2)}) async-start(bf16[8,64,896]{2,1,0:T(8,128)(2,1)} %bitcast.148), calls=%async_computation.7 | async-start | bytes 1835008 | tf_op jit(solution)/shard_map/all_to_all | solution.py:445
  (79 other events, 625.3 us)
Sparse Core Ops, SparseCore 0:
  9.6 84.3 all-gather.14
  95.6 99.9 all-gather.6
  197.7 46.0 all-gather.8
  245.2 47.8 all-gather.10
  295.3 48.4 reduce-scatter.5
  345.9 48.4 reduce-scatter.3
  406.7 82.9 all-gather.12
  521.4 59.4 reduce-scatter.7

commit v6 on v5

--- a/solution.py
+++ b/solution.py
@@ -277,7 +277,7 @@
         return got
 
 
-def place(pieces, places):
+def place(pieces, places, inner=(0,)):
     pieces = [value_of(piece) for piece in pieces]
     rows, width = pieces[0].shape
     count = len(pieces)
@@ -287,8 +287,16 @@
         parts, whole, sems = refs[:count], refs[count], refs[count + 1]
         copies = []
         for i in range(count):
-            there = whole.at[pl.ds(pl.multiple_of(places_ref[i] * rows, rows), rows), :]
-            copies.append(pltpu.make_async_copy(parts[i], there, sems.at[i]))
+            for j, to in enumerate(inner):
+                cut = rows // len(inner)
+                start = pl.multiple_of(places_ref[i] * rows + to * cut, cut)
+                copies.append(
+                    pltpu.make_async_copy(
+                        parts[i].at[pl.ds(j * cut, cut), :],
+                        whole.at[pl.ds(start, cut), :],
+                        sems.at[i * len(inner) + j],
+                    )
+                )
         for copy in copies:
             copy.start()
         for copy in copies:
@@ -300,7 +308,7 @@
         in_specs=[pl.BlockSpec(memory_space=pltpu.SMEM)]
         + [pl.BlockSpec(memory_space=pl.ANY)] * count,
         out_specs=pl.BlockSpec(memory_space=pltpu.VMEM),
-        scratch_shapes=[pltpu.SemaphoreType.DMA((count,))],
+        scratch_shapes=[pltpu.SemaphoreType.DMA((count * len(inner),))],
         compiler_params=pltpu.CompilerParams(vmem_limit_bytes=32 * 1024 * 1024),
         cost_estimate=pl.CostEstimate(flops=0, bytes_accessed=4 * rows * width * count, transcendentals=0),
     )(jnp.stack(places).astype(jnp.int32), *pieces)
@@ -406,16 +414,6 @@
         scratch_shapes=[pltpu.SemaphoreType.DMA((count,))],
         compiler_params=pltpu.CompilerParams(vmem_limit_bytes=32 * 1024 * 1024),
     )(stack)
-
-
-def whole_ring():
-    n = lax.axis_size("ctx")
-    depth = n // 2
-    chips = []
-    for far, side, upward in ((0, 0, True), (0, 1, False), (1, 1, True), (1, 0, False)):
-        levels = range(depth) if upward else range(depth - 1, -1, -1)
-        chips += [(far, 2 * level + side) for level in levels]
-    return [(2 * far + core) * n + ctx for far, ctx in chips for core in range(2)]
 
 
 def core_swap(block):
@@ -496,9 +494,7 @@
         (w_out, w_gate, w_up, qkv_mine, down_far.value)
     )
     qkv_steps = gather_seq(x, qkv_mine)
-    out_stack = lax.all_gather(
-        late_out, ("seq", "ctx"), axis=0, tiled=True, axis_index_groups=[whole_ring()]
-    )
+    out_ring = gather_ring(late_out)
     blocks = cut_columns((late_gate, late_up), seqs, None)
     gate_up = lax.all_to_all(blocks, "ctx", 0, 0, tiled=True).reshape(n * weight_rows, -1)
     qkv_sub = from_devices(qkv_steps)
@@ -530,9 +526,20 @@
     cut = gate_up.shape[0] // 2
     parts = [gate_up[:cut], gate_up[cut:]]
     far = [x.swap(parts[0], 2)]
-    att_low, out_stack, far[0].value = lax.optimization_barrier((att_low, out_stack, far[0].value))
+    att_low, out_ring, far[0].value = lax.optimization_barrier((att_low, out_ring, far[0].value))
     att_stack = gather_ring(att_low)
+    out_steps = gather_seq(x, out_ring)
     far.append(x.swap(parts[1], 2))
+    full_out = place([part for _, part in out_steps], [seq_here ^ o for o, _ in out_steps], ring())
+    late_grad, att_stack = lax.optimization_barrier((out_grad[0], att_stack))
+    grad_all = gather_ring(late_grad)
+    att_stack, full_out, down_sub = lax.optimization_barrier((att_stack, full_out, down_sub))
+    att_low = rearranged(att_stack, ring(), columns=True)
+
+    middle = x_all + dot(att_low, full_out)
+    mlp_scale = rms_scale(middle)
+    normed_mid = (middle * mlp_scale * gain2).astype(bf16)
+    normed_mid, far[1].value = lax.optimization_barrier((normed_mid, far[1].value))
     held = []
     for part, other in zip(parts, far):
         held += [(0, part), (1, core_swap(part)), (2, other), (3, core_swap(other))]
@@ -540,16 +547,6 @@
         [part for _, part in held],
         [(seq_here ^ o) * 2 + i // 4 for i, (o, _) in enumerate(held)],
     )
-    full_out = rearranged(out_stack, whole_ring())
-    late_grad, att_stack, full_out, gate_up, down_sub = lax.optimization_barrier(
-        (out_grad[0], att_stack, full_out, gate_up, down_sub)
-    )
-    grad_all = gather_ring(late_grad)
-    att_low = rearranged(att_stack, ring(), columns=True)
-
-    middle = x_all + dot(att_low, full_out)
-    mlp_scale = rms_scale(middle)
-    normed_mid = (middle * mlp_scale * gain2).astype(bf16)
     gate_up_act = dot(normed_mid, gate_up)
     units = gate_up.shape[1] // 2
     gate_act, up_act = gate_up_act[:, :units], gate_up_act[:, units:]
@@ -589,7 +586,10 @@
 
     gate_up_sum = (gate_up_near + gate_up_far.value.astype(f32)).astype(bf16)
     att_grad, gate_up_sum = lax.optimization_barrier((att_grad, gate_up_sum))
-    w_gate_up = lax.all_to_all(gate_up_sum.reshape(n, weight_rows, -1), "ctx", 0, 0, tiled=True)
+    gate_sum, up_sum = (
+        lax.all_to_all(part.reshape(n, weight_rows, -1), "ctx", 0, 0, tiled=True)
+        for part in (gate_up_sum[:, :units], gate_up_sum[:, units:])
+    )
     grads = [
         attention_back(
             *(m[:, halves[0]] for m in (query, key, value)), pos_all, att_first, lse_first, att_grad[:, halves[0]]
@@ -619,10 +619,7 @@
     )
     w_out_near, w_out_far = scatter_seq_near(dot_rows(att_sub, middle_low_all), seq_here)
     hidden_out = (middle_own + down_own).astype(bf16)
-    w_down_grad = down_weight_near + down_weight_far.value.astype(f32)
-    qkv_grad, w_gate_up, w_down_grad, w_out_far = lax.optimization_barrier(
-        (qkv_grad, w_gate_up, w_down_grad, w_out_far)
-    )
+    qkv_grad, gate_sum = lax.optimization_barrier((qkv_grad, gate_sum))
     normed_grad_part = dot_cols(qkv_grad, qkv_sub)
     attn_gain_part = jnp.sum(normed_grad_part * (x_all * attn_scale), axis=0)
     beside = jnp.stack([attn_gain_part, mlp_gain_part], axis=1)
@@ -631,12 +628,17 @@
     qkv_near, qkv_far = scatter_seq_near(qkv_part, seq_here)
     normed_grad = scatter_ring(normed_grad_part.astype(bf16))
     qkv_far = Link("seq", 1).swap(qkv_far, 2)
+    qkv_far.value, up_sum, w_out_far = lax.optimization_barrier((qkv_far.value, up_sum, w_out_far))
     qkv_sum = (qkv_near + qkv_far.value.astype(f32)).astype(bf16)
     w_query_grad, w_key_grad, w_value_grad, gain_grads = to_owners(qkv_sum, 3, 1, 128)
     gain_grads = gain_grads.astype(f32).reshape(weight_rows, n, 128).sum(axis=1)
     w_out_grad = w_out_near + Link("seq", 1).swap(w_out_far, 2).value.astype(f32)
-    w_out_grad, normed_grad = lax.optimization_barrier((w_out_grad, normed_grad))
-    w_gate_grad, w_up_grad = paste_columns(w_gate_up, 2, seqs)
+    w_down_grad = down_weight_near + down_weight_far.value.astype(f32)
+    w_out_grad, w_down_grad, normed_grad = lax.optimization_barrier(
+        (w_out_grad, w_down_grad, normed_grad)
+    )
+    (w_gate_grad,) = paste_columns(gate_sum, 1, seqs)
+    (w_up_grad,) = paste_columns(up_sum, 1, seqs)
 
     own_scale = own_rows(attn_scale)
     own_unit = hidden_in[0].astype(f32) * own_scale

time: 613 us -> 586 us (0.956)
  waiting for transfers between devices: 258 us -> 226 us
  other arithmetic: 64.2 us -> 73.5 us
  matrix products: 150 us -> 142 us
    all_gather x1 -> x0, waiting for transfers between devices: 20.1 us -> none  [tuned(): lax.all_gather(late_out, ('seq', 'ctx'), axis=0, tiled=True, axis_index_g...]
    all_to_all x1 -> x2, waiting for transfers between devices: 6.05 us -> 25.7 us  [tuned(): lax.all_to_all(part.reshape(n, weight_rows, -1), 'ctx', 0, 0, tiled=True)]
    all_gather x4 -> x5, waiting for transfers between devices: 28.2 us -> 9.81 us  [gather_ring(): lax.all_gather(block, 'ctx', axis=0, tiled=True, axis_index_groups=[ring()])]
    ppermute x8 -> x9, waiting for transfers between devices: 107 us -> 91 us  [swap(): lax.ppermute(value_of(block), self.axis, [(i, i ^ mask) for i in range(n)])]
    dot_general x4, matrix products: 39.6 us -> 33.1 us  [dot(): return jnp.dot(left, right, preferred_element_type=f32)]
    all_to_all x1, waiting for transfers between devices: 17.8 us -> 11.6 us  [to_owners(): lax.all_to_all(part.reshape(n, -1, part.shape[1]), 'ctx', 0, 0, tiled=True)]
    ppermute x12 -> x14, waiting for transfers between devices: 12.4 us -> 17.2 us  [core_swap(): lax.ppermute(value_of(block), 'seq', [(i, i ^ 1) for i in range(n)])]
    unnamed x149 -> x135, local copies, waits for them, and re-layouts: 38.1 us -> 41.6 us
  transfers between devices with their start and end apart: 33 -> 37, of which waited for: 22 -> 17; matrix products, arithmetic and copies ran while one was open for 36% -> 39% of each run, Pallas kernels for 3% -> 3%
where the time goes in v6:
time: 586 us; the launch traced here: 581 us
  waiting for transfers between devices  226 us (39%)
  matrix products  142 us (24%)
  other arithmetic  73.5 us (13%)
  local copies, waits for them, and re-layouts  66.2 us (11%)
  starting transfers between devices  41.2 us (7%)
  Pallas kernels  16.5 us (3%)
  between operations  15.6 us (3%)
    ppermute x9, waiting for transfers between devices, swap(): lax.ppermute(value_of(block), self.axis, [(i, i ^ mask) for i in range(n)])  91 us
    unnamed x135, local copies, waits for them, and re-layouts  41.6 us
    dot_general x4, matrix products, dot_cols(): lax.dot_general(left, right, (((1,), (1,)), ((), ())), preferred_element_...  37.1 us
    dot_general x4, matrix products, dot(): return jnp.dot(left, right, preferred_element_type=f32)  33.1 us
    dot_general x4, matrix products, dot_rows(): lax.dot_general(left, right, (((0,), (0,)), ((), ())), preferred_element_...  31.2 us
    all_to_all x2, waiting for transfers between devices, tuned(): lax.all_to_all(blocks, 'ctx', 0, 0, tiled=True).reshape(n * weight_rows, -1)  30.9 us
    all_to_all x2, waiting for transfers between devices, tuned(): lax.all_to_all(part.reshape(n, weight_rows, -1), 'ctx', 0, 0, tiled=True)  25.7 us
    reduce_scatter x3, waiting for transfers between devices, scatter_ring(): lax.psum_scatter(total, 'ctx', scatter_dimension=0, tiled=True, axis_inde...  25.3 us
  transfers between devices with their start and end apart: 37, of which 17 were waited for; matrix products, arithmetic and copies ran while one was open for 39% of the time, Pallas kernels for 3%

profile of v6, /device:TPU:0, one launch (start us, length us, event | category | flops | bytes accessed | tf_op | source)
XLA Modules:
  0.0 581.2 jit_solution(256945182446178496)
XLA Ops:
  14.8 7.3 %all-to-all-start = ((bf16[8,64,896]{2,1,0:T(8,128)(2,1)}), bf16[8,64,896]{2,1,0:T(8,128)(2,1)S(1)}, u32[]{:S(2)}, u32[]{:S(2)}) async-start(bf16[8,64,896]{2,1,0:T(8,128)(2,1)} %shard_map.203), calls=%async_computation | async-start | bytes 1835008 | tf_op jit(solution)/shard_map/all_to_all | solution.py:491
  23.7 23.0 %collective-permute-done.refs_2_ = bf16[256,2048]{1,0:T(8,128)(2,1)S(1)} collective-permute-done((bf16[256,2048]{1,0:T(8,128)(2,1)S(1)}, bf16[256,2048]{1,0:T(8,128)(2,1)S(1)}, u32[]{:S(2)}, u32[]{:S(2)}) %collective-permute-start) | collective-permute-done | bytes 1048608 | tf_op jit(solution)/shard_map/ppermute | solution.py:275
  46.7 8.5 %all-to-all-done = bf16[8,64,896]{2,1,0:T(8,128)(2,1)S(1)} async-done(((bf16[8,64,896]{2,1,0:T(8,128)(2,1)}), bf16[8,64,896]{2,1,0:T(8,128)(2,1)S(1)}, u32[]{:S(2)}, u32[]{:S(2)}) %all-to-all-start) | async-done | bytes 917536 | tf_op jit(solution)/shard_map/all_to_all | solution.py:491
  66.6 8.3 %collective-permute-done.2.refs_2_ = bf16[512,896]{1,0:T(8,128)(2,1)} collective-permute-done((bf16[512,896]{1,0:T(8,128)(2,1)S(1)}, bf16[512,896]{1,0:T(8,128)(2,1)}, u32[]{:S(2)}, u32[]{:S(2)}) %collective-permute-start.2) | collective-permute-done | bytes 917536 | tf_op jit(solution)/shard_map/ppermute | solution.py:275
  82.9 9.8 %all-gather.15.cloned.1.call-done = bf16[1,1024,2048]{2,1,0:T(8,128)(2,1)} async-done(((bf16[1,128,2048]{2,1,0:T(8,128)(2,1)}), bf16[1,1024,2048]{2,1,0:T(8,128)(2,1)}) %all-gather.15.cloned.1.call-update) | async-done | bytes 4194320 | tf_op jit(solution)/shard_map/all_gather | solution.py:381
  105.5 22.4 %all-to-all-done.1 = bf16[8,64,2048]{2,1,0:T(8,128)(2,1)} async-done(((bf16[8,64,2048]{2,1,0:T(8,128)(2,1)}), bf16[8,64,2048]{2,1,0:T(8,128)(2,1)}, u32[]{:S(2)}, u32[]{:S(2)}) %all-to-all-start.1) | async-done | bytes 2097184 | tf_op jit(solution)/shard_map/all_to_all | solution.py:499
  159.8 46.5 %collective-permute-done.6.refs_2_ = bf16[512,2048]{1,0:T(8,128)(2,1)S(1)} collective-permute-done((bf16[512,2048]{1,0:T(8,128)(2,1)}, bf16[512,2048]{1,0:T(8,128)(2,1)S(1)}, u32[]{:S(2)}, u32[]{:S(2)}) %collective-permute-start.6) | collective-permute-done | bytes 2097184 | tf_op jit(solution)/shard_map/ppermute | solution.py:275
  206.9 6.6 %collective-permute-done.8.refs_1_ = bf16[256,2048]{1,0:T(8,128)(2,1)S(1)} collective-permute-done((bf16[256,2048]{1,0:T(8,128)(2,1)S(1)}, bf16[256,2048]{1,0:T(8,128)(2,1)S(1)}, u32[]{:S(2)}, u32[]{:S(2)}) %collective-permute-start.8) | collective-permute-done | bytes 1048608 | tf_op jit(solution)/shard_map/ppermute | solution.py:421
  229.7 12.4 %multiply_reduce_fusion = (f32[1024]{0:T(1024)S(1)}, f32[1024,2048]{1,0:T(8,128)S(1)}) fusion(bf16[1024,2048]{1,0:T(8,128)(2,1)S(1)} %shard_map.208, bf16[2048,2048]{1,0:T(8,128)(2,1)S(1)} %copy-done.1, bf16[1,1024,2048]{2,1,0:T(8,128)(2,1)} %all-gather.15.cloned.1.call-done), kind=kOutput, calls=%fused_computation.17 | convolution fusion | flops 8598322176 | bytes 25169920 | tf_op jit(solution)/shard_map/dot_general | solution.py:65
  256.5 8.8 %fusion.100 = f32[1024,2048]{1,0:T(8,128)S(1)} fusion(bf16[1024,2048]{1,0:T(8,128)(2,1)S(1)} %copy-done.30, bf16[2048,2048]{1,0:T(8,128)(2,1)S(1)} %shard_map.209), kind=kOutput, calls=%fused_computation.201 | convolution fusion | flops 8589934592 | bytes 20971520 | tf_op jit(solution)/shard_map/dot_general | solution.py:65
  270.5 6.1 %convolution_convert_fusion.1 = bf16[1024,2048]{1,0:T(8,128)(2,1)} fusion(bf16[1024,1024]{1,0:T(8,128)(2,1)S(1)} %multiply_convert_fusion.5, bf16[1024,2048]{1,0:T(8,128)(2,1)S(1)} %copy-done.7), kind=kOutput, calls=%fused_computation.51 | convolution fusion | flops 4297064448 | bytes 10485760 | tf_op jit(solution)/shard_map/dot_general | solution.py:65
  276.7 8.0 %fusion.101 = f32[1024,1024]{1,0:T(8,128)S(1)} fusion(bf16[1024,2048]{1,0:T(8,128)(2,1)} %all-gather.11.cloned.1.call-done, bf16[1024,2048]{1,0:T(8,128)(2,1)} %copy-done.6), kind=kOutput, calls=%fused_computation.202 | convolution fusion | flops 4294967296 | bytes 12582912 | tf_op jit(solution)/shard_map/dot_general | solution.py:73
  289.9 12.6 %convolution_convert_fusion = bf16[1024,2048]{1,0:T(8,128)(2,1)} fusion(bf16[1024,2048]{1,0:T(8,128)(2,1)S(1)} %pad_maximum_fusion, bf16[2048,2048]{1,0:T(8,128)(2,1)} %copy-done.2), kind=kOutput, calls=%fused_computation.50 | convolution fusion | flops 8592031744 | bytes 16777216 | tf_op jit(solution)/shard_map/dot_general | solution.py:73
  302.6 12.5 %fusion.103 = f32[2048,2048]{1,0:T(8,128)S(1)} fusion(bf16[1024,2048]{1,0:T(8,128)(2,1)} %multiply_convert_fusion.2, bf16[1024,2048]{1,0:T(8,128)(2,1)} %copy-done.35), kind=kOutput, calls=%fused_computation.204 | convolution fusion | flops 8589934592 | bytes 25165824 | tf_op jit(solution)/shard_map/dot_general | solution.py:69
  324.4 7.4 %collective-permute-done.15 = bf16[1024,2048]{1,0:T(8,128)(2,1)} collective-permute-done((bf16[1024,2048]{1,0:T(8,128)(2,1)}, bf16[1024,2048]{1,0:T(8,128)(2,1)}, u32[]{:S(2)}, u32[]{:S(2)}) %collective-permute-start.15) | collective-permute-done | bytes 4194336 | tf_op jit(solution)/shard_map/ppermute | solution.py:421
  338.6 9.0 %fusion.102 = f32[1024,2048]{1,0:T(8,128)} fusion(bf16[1024,1024]{1,0:T(8,128)(2,1)S(1)} %multiply_convert_fusion.5, bf16[1024,2048]{1,0:T(8,128)(2,1)} %all-gather.11.cloned.1.call-done), kind=kOutput, calls=%fused_computation.203 | convolution fusion | flops 4294967296 | bytes 14680064 | tf_op jit(solution)/shard_map/dot_general | solution.py:69
  349.7 25.3 %reduce-scatter.4.cloned.1.call-done = bf16[128,2048]{1,0:T(8,128)(2,1)} async-done(((bf16[1024,2048]{1,0:T(8,128)(2,1)}), bf16[128,2048]{1,0:T(8,128)(2,1)}) %reduce-scatter.4.cloned.1.call-update) | async-done | bytes 524304 | tf_op jit(solution)/shard_map/reduce_scatter | solution.py:385
  376.2 8.8 %collective-permute-done.16 = bf16[512,2048]{1,0:T(8,128)(2,1)} collective-permute-done((bf16[512,2048]{1,0:T(8,128)(2,1)}, bf16[512,2048]{1,0:T(8,128)(2,1)}, u32[]{:S(2)}, u32[]{:S(2)}) %collective-permute-start.16) | collective-permute-done | bytes 2097184 | tf_op jit(solution)/shard_map/ppermute | solution.py:275
  388.2 6.4 %convolution_convert_fusion.2.refs_0_ = bf16[128,2048]{1,0:T(8,128)(2,1)S(1)} fusion(bf16[128,2048]{1,0:T(8,128)(2,1)S(1)} %fusion.88, bf16[2048,2048]{1,0:T(8,128)(2,1)} %copy-done), kind=kOutput, calls=%fused_computation.56 | convolution fusion | flops 1074003968 | bytes 9437184 | tf_op jit(solution)/shard_map/dot_general | solution.py:73
  408.6 13.9 %all-to-all-done.2 = bf16[8,128,256]{2,1,0:T(8,128)(2,1)} async-done(((bf16[8,128,256]{2,1,0:T(8,128)(2,1)}), bf16[8,128,256]{2,1,0:T(8,128)(2,1)}, u32[]{:S(2)}, u32[]{:S(2)}) %all-to-all-start.2) | async-done | bytes 524320 | tf_op jit(solution)/shard_map/all_to_all | solution.py:583
  438.4 6.3 %fusion.13 = bf16[2,64,1024]{2,1,0:T(8,128)(2,1)} fusion(bf16[1024,2,64]{0,2,1:T(8,128)(2,1)S(1)} %bitcast.163, f32[2,1024,1024]{1,2,0:T(8,128)} %copy-done.60, f32[2,1024]{1,0:T(2,128)S(1)} %log_add_fusion.1, pred[1024,1024]{0,1:T(8,128)(4,1)S(1)} %copy-done.33), kind=kOutput, calls=%fused_computation.43 | convolution fusion | flops 276824064 | bytes 9969664 | tf_op jit(solution)/shard_map/hqk,qhd->khd/dot_general | solution.py:121
  464.9 10.0 %fusion.89 = (bf16[1024,2048]{1,0:T(8,128)(2,1)}, f32[2048]{0:T(1024)S(1)}) fusion(f32[1024]{0:T(1024)S(1)} %copy-done.58, bf16[1,1024,2048]{2,1,0:T(8,128)(2,1)} %all-gather.15.cloned.1.call-done, bf16[1024,768]{0,1:T(8,128)(2,1)} %pad_maximum_fusion.4, bf16[2048,896]{1,0:T(8,128)(2,1)} %copy-done.4), kind=kOutput, calls=%fused_computation.190 | convolution fusion | flops 3231709184 | bytes 13119488 | tf_op jit(solution)/shard_map/dot_general | solution.py:73
  505.9 24.3 %all-to-all-done.4.ref = bf16[8,64,1024]{2,1,0:T(8,128)(2,1)S(1)} async-done(((bf16[8,64,1024]{2,1,0:T(8,128)(2,1)}), bf16[8,64,1024]{2,1,0:T(8,128)(2,1)S(1)}, u32[]{:S(2)}, u32[]{:S(2)}) %all-to-all-start.4) | async-done | bytes 1048608 | tf_op jit(solution)/shard_map/all_to_all | solution.py:590
  555.4 11.6 %all-to-all-done.5.ref = bf16[8,64,896]{2,1,0:T(8,128)(2,1)S(1)} async-done(((bf16[8,64,896]{2,1,0:T(8,128)(2,1)}), bf16[8,64,896]{2,1,0:T(8,128)(2,1)S(1)}, u32[]{:S(2)}, u32[]{:S(2)}) %all-to-all-start.5) | async-done | bytes 917536 | tf_op jit(solution)/shard_map/all_to_all | solution.py:443
  (324 shorter events, 249.8 us)
Async XLA Ops:
  7.2 85.5 %all-gather.15.cloned.1.call-start = ((), (), s32[]{:S(2)}) async-start(), calls=%async_computation.16 | async-start | bytes 4718592 | tf_op jit(solution)/shard_map/all_gather | solution.py:381
  14.8 40.5 %all-to-all-start = ((bf16[8,64,896]{2,1,0:T(8,128)(2,1)}), bf16[8,64,896]{2,1,0:T(8,128)(2,1)S(1)}, u32[]{:S(2)}, u32[]{:S(2)}) async-start(bf16[8,64,896]{2,1,0:T(8,128)(2,1)} %shard_map.203), calls=%async_computation | async-start | bytes 1835008 | tf_op jit(solution)/shard_map/all_to_all | solution.py:491
  62.1 65.8 %all-to-all-start.1 = ((bf16[8,64,2048]{2,1,0:T(8,128)(2,1)}), bf16[8,64,2048]{2,1,0:T(8,128)(2,1)}, u32[]{:S(2)}, u32[]{:S(2)}) async-start(bf16[8,64,2048]{2,1,0:T(8,128)(2,1)} %shard_map.205), calls=%async_computation.1 | async-start | bytes 4194304 | tf_op jit(solution)/shard_map/all_to_all | solution.py:499
  66.5 92.6 %all-gather.7.cloned.1.call-start = ((), (), s32[]{:S(2)}) async-start(), calls=%async_computation.9 | async-start | bytes 2359296 | tf_op jit(solution)/shard_map/all_gather | solution.py:381
  75.0 149.0 %all-gather.9.cloned.1.call-start = ((), (), s32[]{:S(2)}) async-start(), calls=%async_computation.10 | async-start | bytes 4718592 | tf_op jit(solution)/shard_map/all_gather | solution.py:381
  129.7 29.4 %collective-permute-start.4 = (bf16[256,2048]{1,0:T(8,128)(2,1)S(1)}, bf16[256,2048]{1,0:T(8,128)(2,1)}, u32[]{:S(2)}, u32[]{:S(2)}) collective-permute-start(bf16[256,2048]{1,0:T(8,128)(2,1)S(1)} %get-tuple-element.66.refs_0_), channel_id=1, source_target_pairs={{0,16},{8,24},{16,0},{24,8},{1,17},{9,25},{17,1},{25,9},{2,18},{10... | collective-permute-start | bytes 3145736 | tf_op jit(solution)/shard_map/ppermute | solution.py:275
  159.1 117.5 %all-gather.11.cloned.1.call-start = ((), (), s32[]{:S(2)}) async-start(), calls=%async_computation.11 | async-start | bytes 4718592 | tf_op jit(solution)/shard_map/all_gather | solution.py:381
  159.2 47.2 %collective-permute-start.6 = (bf16[512,2048]{1,0:T(8,128)(2,1)}, bf16[512,2048]{1,0:T(8,128)(2,1)S(1)}, u32[]{:S(2)}, u32[]{:S(2)}) collective-permute-start(bf16[512,2048]{1,0:T(8,128)(2,1)} %all-gather.7.cloned.1.call-done.refs_0_), channel_id=1, source_target_pairs={{0,16},{8,24},{16,0},{24,8},{1,17},{9,25},{17,1},{25,9},{2,18},{10... | collective-permute-start | bytes 6291464 | tf_op jit(solution)/shard_map/ppermute | solution.py:275
  159.8 58.7 %collective-permute-start.5 = (bf16[512,2048]{1,0:T(8,128)(2,1)}, bf16[512,2048]{1,0:T(8,128)(2,1)S(1)}, u32[]{:S(2)}, u32[]{:S(2)}) collective-permute-start(bf16[512,2048]{1,0:T(8,128)(2,1)} %all-gather.7.cloned.1.call-done.refs_0_), channel_id=1, source_target_pairs={{0,8},{8,0},{16,24},{24,16},{1,9},{9,1},{17,25},{25,17},{2,10},{10... | collective-permute-start | bytes 6291464 | tf_op jit(solution)/shard_map/ppermute | solution.py:421
  217.9 28.9 %collective-permute-start.11 = (bf16[256,2048]{1,0:T(8,128)(2,1)S(1)}, bf16[256,2048]{1,0:T(8,128)(2,1)S(1)}, u32[]{:S(2)}, u32[]{:S(2)}) collective-permute-start(bf16[256,2048]{1,0:T(8,128)(2,1)S(1)} %get-tuple-element.66.refs_0_), channel_id=1, source_target_pairs={{0,8},{8,0},{16,24},{24,16},{1,9},{9,1},{17,25},{25,17},{2,10},{10... | collective-permute-start | bytes 3145736 | tf_op jit(solution)/shard_map/ppermute | solution.py:421
  218.1 28.8 %collective-permute-start.13 = (bf16[256,2048]{1,0:T(8,128)(2,1)S(1)}, bf16[256,2048]{1,0:T(8,128)(2,1)}, u32[]{:S(2)}, u32[]{:S(2)}) collective-permute-start(bf16[256,2048]{1,0:T(8,128)(2,1)S(1)} %get-tuple-element.77.refs_4_), channel_id=1, source_target_pairs={{0,8},{8,0},{16,24},{24,16},{1,9},{9,1},{17,25},{25,17},{2,10},{10... | collective-permute-start | bytes 3145736 | tf_op jit(solution)/shard_map/ppermute | solution.py:421
  218.4 28.4 %collective-permute-start.12 = (bf16[256,2048]{1,0:T(8,128)(2,1)}, bf16[256,2048]{1,0:T(8,128)(2,1)}, u32[]{:S(2)}, u32[]{:S(2)}) collective-permute-start(bf16[256,2048]{1,0:T(8,128)(2,1)} %collective-permute-done.4.refs_2_), channel_id=1, source_target_pairs={{0,8},{8,0},{16,24},{24,16},{1,9},{9,1},{17,25},{25,17},{2,10},{10... | collective-permute-start | bytes 3145736 | tf_op jit(solution)/shard_map/ppermute | solution.py:421
  218.6 28.2 %collective-permute-start.10 = (bf16[256,2048]{1,0:T(8,128)(2,1)S(1)}, bf16[256,2048]{1,0:T(8,128)(2,1)}, u32[]{:S(2)}, u32[]{:S(2)}) collective-permute-start(bf16[256,2048]{1,0:T(8,128)(2,1)S(1)} %get-tuple-element.77.refs_4_), channel_id=1, source_target_pairs={{0,16},{8,24},{16,0},{24,8},{1,17},{9,25},{17,1},{25,9},{2,18},{10... | collective-permute-start | bytes 3145736 | tf_op jit(solution)/shard_map/ppermute | solution.py:275
  224.0 123.5 %reduce-scatter.6.cloned.1.call-start = ((), (), s32[]{:S(2)}) async-start(), calls=%async_computation.13 | async-start | bytes 4718592 | tf_op jit(solution)/shard_map/reduce_scatter | solution.py:385
  276.6 98.4 %reduce-scatter.4.cloned.1.call-start = ((), (), s32[]{:S(2)}) async-start(), calls=%async_computation.12 | async-start | bytes 4718592 | tf_op jit(solution)/shard_map/reduce_scatter | solution.py:385
  302.5 190.3 %all-gather.13.cloned.1.call-start = ((), (), s32[]{:S(2)}) async-start(), calls=%async_computation.14 | async-start | bytes 4718592 | tf_op jit(solution)/shard_map/all_gather | solution.py:381
  337.0 48.0 %collective-permute-start.16 = (bf16[512,2048]{1,0:T(8,128)(2,1)}, bf16[512,2048]{1,0:T(8,128)(2,1)}, u32[]{:S(2)}, u32[]{:S(2)}) collective-permute-start(bf16[512,2048]{1,0:T(8,128)(2,1)} %add_convert_fusion.1), channel_id=1, source_target_pairs={{0,16},{8,24},{16,0},{24,8},{1,17},{9,25},{17,1},{25,9},{2,18},{10... | collective-permute-start | bytes 6291464 | tf_op jit(solution)/shard_map/ppermute | solution.py:275
  404.0 40.8 %collective-permute-start.18 = (bf16[512,2048]{1,0:T(8,128)(2,1)}, bf16[512,2048]{1,0:T(8,128)(2,1)}, u32[]{:S(2)}, u32[]{:S(2)}) collective-permute-start(bf16[512,2048]{1,0:T(8,128)(2,1)} %pad_maximum_fusion.2), channel_id=1, source_target_pairs={{0,8},{8,0},{16,24},{24,16},{1,9},{9,1},{17,25},{25,17},{2,10},{10... | collective-permute-start | bytes 6291464 | tf_op jit(solution)/shard_map/ppermute | solution.py:421
  424.1 40.9 %all-to-all-start.3 = ((bf16[8,64,1024]{2,1,0:T(8,128)(2,1)}), bf16[8,64,1024]{2,1,0:T(8,128)(2,1)S(1)}, u32[]{:S(2)}, u32[]{:S(2)}) async-start(bf16[8,64,1024]{2,1,0:T(8,128)(2,1)} %bitcast.147), calls=%async_computation.5 | async-start | bytes 2097152 | tf_op jit(solution)/shard_map/all_to_all | solution.py:590
  427.6 141.4 %reduce-scatter.8.cloned.1.call-start = ((), (), s32[]{:S(2)}) async-start(), calls=%async_computation.15 | async-start | bytes 4718592 | tf_op jit(solution)/shard_map/reduce_scatter | solution.py:385
  488.1 42.1 %all-to-all-start.4 = ((bf16[8,64,1024]{2,1,0:T(8,128)(2,1)}), bf16[8,64,1024]{2,1,0:T(8,128)(2,1)S(1)}, u32[]{:S(2)}, u32[]{:S(2)}) async-start(bf16[8,64,1024]{2,1,0:T(8,128)(2,1)} %bitcast.146), calls=%async_computation.6 | async-start | bytes 2097152 | tf_op jit(solution)/shard_map/all_to_all | solution.py:590
  502.0 28.2 %collective-permute-start.20 = (bf16[512,896]{0,1:T(8,128)(2,1)}, bf16[512,896]{0,1:T(8,128)(2,1)}, u32[]{:S(2)}, u32[]{:S(2)}) collective-permute-start(bf16[512,896]{0,1:T(8,128)(2,1)} %fusion.33), channel_id=1, source_target_pairs={{0,16},{8,24},{16,0},{24,8},{1,17},{9,25},{17,1},{25,9},{2,18},{10... | collective-permute-start | bytes 2752520 | tf_op jit(solution)/shard_map/ppermute | solution.py:275
  503.4 44.5 %collective-permute-start.22 = (bf16[256,2048]{1,0:T(8,128)(2,1)}, bf16[256,2048]{1,0:T(8,128)(2,1)}, u32[]{:S(2)}, u32[]{:S(2)}) collective-permute-start(bf16[256,2048]{1,0:T(8,128)(2,1)} %add_convert_fusion.2), channel_id=1, source_target_pairs={{0,16},{8,24},{16,0},{24,8},{1,17},{9,25},{17,1},{25,9},{2,18},{10... | collective-permute-start | bytes 3145736 | tf_op jit(solution)/shard_map/ppermute | solution.py:275
  535.7 31.3 %all-to-all-start.5 = ((bf16[8,64,896]{2,1,0:T(8,128)(2,1)}), bf16[8,64,896]{2,1,0:T(8,128)(2,1)S(1)}, u32[]{:S(2)}, u32[]{:S(2)}) async-start(bf16[8,64,896]{2,1,0:T(8,128)(2,1)} %bitcast.150), calls=%async_computation.8 | async-start | bytes 1835008 | tf_op jit(solution)/shard_map/all_to_all | solution.py:443
  (76 other events, 713.0 us)
Sparse Core Ops, SparseCore 0:
  9.6 83.0 all-gather.14
  94.2 55.1 all-gather.6
  159.2 45.9 all-gather.8
  224.2 47.0 all-gather.10
  276.7 47.6 reduce-scatter.5
  326.5 48.4 reduce-scatter.3
  394.9 78.8 all-gather.12
  476.1 75.8 reduce-scatter.7

commit v7 on v6

--- a/solution.py
+++ b/solution.py
@@ -312,6 +312,40 @@
         compiler_params=pltpu.CompilerParams(vmem_limit_bytes=32 * 1024 * 1024),
         cost_estimate=pl.CostEstimate(flops=0, bytes_accessed=4 * rows * width * count, transcendentals=0),
     )(jnp.stack(places).astype(jnp.int32), *pieces)
+
+
+def place_pairs(stacks, places, inner):
+    count = len(inner)
+    rows, width = stacks[0].shape[0] // (2 * count), stacks[0].shape[1]
+
+    def kernel(places_ref, *refs):
+        parts, whole, sems = refs[: len(stacks)], refs[len(stacks)], refs[len(stacks) + 1]
+        copies = []
+        for p, part in enumerate(parts):
+            for i, to in enumerate(inner):
+                for e in range(2):
+                    start = places_ref[2 * p + e] * (count * rows) + to * rows
+                    copies.append(
+                        pltpu.make_async_copy(
+                            part.at[pl.ds((2 * i + e) * rows, rows), :],
+                            whole.at[pl.ds(pl.multiple_of(start, rows), rows), :],
+                            sems.at[len(copies)],
+                        )
+                    )
+        for copy in copies:
+            copy.start()
+        for copy in copies:
+            copy.wait()
+
+    return pl.pallas_call(
+        kernel,
+        out_shape=jax.ShapeDtypeStruct((2 * len(stacks) * count * rows, width), stacks[0].dtype),
+        in_specs=[pl.BlockSpec(memory_space=pltpu.SMEM)]
+        + [pl.BlockSpec(memory_space=pl.ANY)] * len(stacks),
+        out_specs=pl.BlockSpec(memory_space=pltpu.VMEM),
+        scratch_shapes=[pltpu.SemaphoreType.DMA((2 * len(stacks) * count,))],
+        compiler_params=pltpu.CompilerParams(vmem_limit_bytes=32 * 1024 * 1024),
+    )(jnp.stack(places).astype(jnp.int32), *stacks)
 
 
 def cut_columns(weights, groups, beside, devices=None):
@@ -486,15 +520,16 @@
     )
     beside = jnp.pad(beside, ((0, 0), (0, 128 - beside.shape[1])))
     x_low = gather_ring(hidden_in[0])
+    out_pair = jnp.concatenate([w_out, Link("seq", 1).swap(w_out, 2).value], axis=0)
     down_steps = gather_seq(Link("seq", 1), w_down)
     blocks = cut_columns((w_query, w_key, w_value), 1, beside)
     qkv_mine = lax.all_to_all(blocks, "ctx", 0, 0, tiled=True).reshape(n * weight_rows, -1)
     down_far = down_steps[2][1]
-    late_out, late_gate, late_up, qkv_mine, down_far.value = lax.optimization_barrier(
-        (w_out, w_gate, w_up, qkv_mine, down_far.value)
+    out_pair, late_gate, late_up, qkv_mine, down_far.value = lax.optimization_barrier(
+        (out_pair, w_gate, w_up, qkv_mine, down_far.value)
     )
     qkv_steps = gather_seq(x, qkv_mine)
-    out_ring = gather_ring(late_out)
+    out_ring = gather_ring(out_pair)
     blocks = cut_columns((late_gate, late_up), seqs, None)
     gate_up = lax.all_to_all(blocks, "ctx", 0, 0, tiled=True).reshape(n * weight_rows, -1)
     qkv_sub = from_devices(qkv_steps)
@@ -528,9 +563,11 @@
     far = [x.swap(parts[0], 2)]
     att_low, out_ring, far[0].value = lax.optimization_barrier((att_low, out_ring, far[0].value))
     att_stack = gather_ring(att_low)
-    out_steps = gather_seq(x, out_ring)
+    out_other = core_swap(out_ring)
     far.append(x.swap(parts[1], 2))
-    full_out = place([part for _, part in out_steps], [seq_here ^ o for o, _ in out_steps], ring())
+    full_out = place_pairs(
+        [out_ring, out_other.value], [seq_here ^ o for o in (0, 2, 1, 3)], ring()
+    )
     late_grad, att_stack = lax.optimization_barrier((out_grad[0], att_stack))
     grad_all = gather_ring(late_grad)
     att_stack, full_out, down_sub = lax.optimization_barrier((att_stack, full_out, down_sub))

time: 586 us -> 576 us (0.983)
  waiting for transfers between devices: 226 us -> 212 us
    ppermute x9, waiting for transfers between devices: 91 us -> 48.9 us  [swap(): lax.ppermute(value_of(block), self.axis, [(i, i ^ mask) for i in range(n)])]
    all_gather x5, waiting for transfers between devices: 9.81 us -> 45.1 us  [gather_ring(): lax.all_gather(block, 'ctx', axis=0, tiled=True, axis_index_groups=[ring()])]
    all_to_all x2, waiting for transfers between devices: 30.9 us -> 20.8 us  [tuned(): lax.all_to_all(blocks, 'ctx', 0, 0, tiled=True).reshape(n * weight_rows, -1)]
    ppermute x14 -> x13, waiting for transfers between devices: 17.2 us -> 20 us  [core_swap(): lax.ppermute(value_of(block), 'seq', [(i, i ^ 1) for i in range(n)])]
    unnamed x135 -> x137, local copies, waits for them, and re-layouts: 41.6 us -> 42.3 us
  transfers between devices with their start and end apart: 37 -> 36, of which waited for: 17 -> 18; matrix products, arithmetic and copies ran while one was open for 39% -> 40% of each run, Pallas kernels for 3% -> 3%
where the time goes in v7:
time: 576 us; the launch traced here: 572 us
  waiting for transfers between devices  212 us (37%)
  matrix products  143 us (25%)
  other arithmetic  75.1 us (13%)
  local copies, waits for them, and re-layouts  66.1 us (11%)
  starting transfers between devices  43.4 us (8%)
  Pallas kernels  16.2 us (3%)
  between operations  15.6 us (3%)
    ppermute x9, waiting for transfers between devices, swap(): lax.ppermute(value_of(block), self.axis, [(i, i ^ mask) for i in range(n)])  48.9 us
    all_gather x5, waiting for transfers between devices, gather_ring(): lax.all_gather(block, 'ctx', axis=0, tiled=True, axis_index_groups=[ring()])  45.1 us
    unnamed x137, local copies, waits for them, and re-layouts  42.3 us
    dot_general x4, matrix products, dot_cols(): lax.dot_general(left, right, (((1,), (1,)), ((), ())), preferred_element_...  37.1 us
    dot_general x4, matrix products, dot(): return jnp.dot(left, right, preferred_element_type=f32)  34.8 us
    dot_general x4, matrix products, dot_rows(): lax.dot_general(left, right, (((0,), (0,)), ((), ())), preferred_element_...  31.2 us
    reduce_scatter x3, waiting for transfers between devices, scatter_ring(): lax.psum_scatter(total, 'ctx', scatter_dimension=0, tiled=True, axis_inde...  26.1 us
    all_to_all x2, waiting for transfers between devices, tuned(): lax.all_to_all(part.reshape(n, weight_rows, -1), 'ctx', 0, 0, tiled=True)  25.3 us
  transfers between devices with their start and end apart: 36, of which 18 were waited for; matrix products, arithmetic and copies ran while one was open for 40% of the time, Pallas kernels for 3%

profile of v7, /device:TPU:0, one launch (start us, length us, event | category | flops | bytes accessed | tf_op | source)
XLA Modules:
  0.0 571.9 jit_solution(12443015072689252749)
XLA Ops:
  14.8 7.3 %all-to-all-start = ((bf16[8,64,896]{2,1,0:T(8,128)(2,1)}), bf16[8,64,896]{2,1,0:T(8,128)(2,1)S(1)}, u32[]{:S(2)}, u32[]{:S(2)}) async-start(bf16[8,64,896]{2,1,0:T(8,128)(2,1)} %shard_map.203), calls=%async_computation | async-start | bytes 1835008 | tf_op jit(solution)/shard_map/all_to_all | solution.py:526
  24.2 28.1 %collective-permute-done = bf16[64,2048]{1,0:T(8,128)(2,1)S(1)} collective-permute-done((bf16[64,2048]{1,0:T(8,128)(2,1)}, bf16[64,2048]{1,0:T(8,128)(2,1)S(1)}, u32[]{:S(2)}, u32[]{:S(2)}) %collective-permute-start) | collective-permute-done | bytes 262176 | tf_op jit(solution)/shard_map/ppermute | solution.py:275
  66.9 8.5 %collective-permute-done.3.refs_2_ = bf16[512,896]{1,0:T(8,128)(2,1)} collective-permute-done((bf16[512,896]{1,0:T(8,128)(2,1)S(1)}, bf16[512,896]{1,0:T(8,128)(2,1)}, u32[]{:S(2)}, u32[]{:S(2)}) %collective-permute-start.3) | collective-permute-done | bytes 917536 | tf_op jit(solution)/shard_map/ppermute | solution.py:275
  83.3 10.9 %all-gather.15.cloned.1.call-done = bf16[1,1024,2048]{2,1,0:T(8,128)(2,1)} async-done(((bf16[1,128,2048]{2,1,0:T(8,128)(2,1)}), bf16[1,1024,2048]{2,1,0:T(8,128)(2,1)}) %all-gather.15.cloned.1.call-update) | async-done | bytes 4194320 | tf_op jit(solution)/shard_map/all_gather | solution.py:415
  97.4 7.5 %fusion.97 = (bf16[1024,768]{0,1:T(8,128)(2,1)S(1)}, f32[1024,768]{0,1:T(8,128)}) fusion(bf16[2048,896]{1,0:T(8,128)(2,1)S(1)} %copy-done.5, bf16[1,1024,2048]{2,1,0:T(8,128)(2,1)} %all-gather.15.cloned.1.call-done, f32[2048]{0:T(1024)S(1)} %get-tuple-element.108, f32[1024]{0:T(1024)S(1)} %add_rsqrt_fusion.1), kind=kOutput, calls=%fused_computation.200 | convolution fusion | flops 3230400512 | bytes 12070912 | tf_op jit(solution)/shard_map/dot_general | solution.py:65
  106.5 19.7 %all-to-all-done.1 = bf16[8,64,2048]{2,1,0:T(8,128)(2,1)} async-done(((bf16[8,64,2048]{2,1,0:T(8,128)(2,1)}), bf16[8,64,2048]{2,1,0:T(8,128)(2,1)}, u32[]{:S(2)}, u32[]{:S(2)}) %all-to-all-start.1) | async-done | bytes 2097184 | tf_op jit(solution)/shard_map/all_to_all | solution.py:534
  133.0 6.4 %fusion.5 = (f32[2,1024]{1,0:T(2,128)S(1)}, f32[2,1024]{1,0:T(2,128)S(1)}, f32[2,1024,1024]{1,2,0:T(8,128)}) fusion(f32[2,1024,1024]{1,2,0:T(8,128)S(1)} %get-tuple-element.171, f32[2,1024]{1,0:T(2,128)S(1)} %get-tuple-element.170, pred[1024,1024]{0,1:T(8,128)(4,1)S(1)} %copy-done.31, bf16[1024,2,64]{0,2,1:T(8,128)(2,1)S(1)} %bitcast.164, ...), kind=kOutput, calls=%fused_computation.26 | convolution fusion | flops 283111424 | bytes 18374656 | tf_op jit(solution)/shard_map/qhd,khd->hqk/dot_general | solution.py:100
  158.3 6.7 %all-gather.7.cloned.1.call-done.refs_0_ = bf16[1024,2048]{1,0:T(8,128)(2,1)} async-done(((bf16[128,2048]{1,0:T(8,128)(2,1)}), bf16[1024,2048]{1,0:T(8,128)(2,1)}) %all-gather.7.cloned.1.call-update) | async-done | bytes 4194320 | tf_op jit(solution)/shard_map/all_gather | solution.py:415
  165.8 7.7 %collective-permute-done.7.refs_1_ = bf16[256,2048]{1,0:T(8,128)(2,1)S(1)} collective-permute-done((bf16[256,2048]{1,0:T(8,128)(2,1)S(1)}, bf16[256,2048]{1,0:T(8,128)(2,1)S(1)}, u32[]{:S(2)}, u32[]{:S(2)}) %collective-permute-start.7) | collective-permute-done | bytes 1048608 | tf_op jit(solution)/shard_map/ppermute | solution.py:455
  186.6 27.5 %all-gather.9.cloned.1.call-done.stack_ref = bf16[8192,256]{1,0:T(8,128)(2,1)} async-done(((bf16[1024,256]{1,0:T(8,128)(2,1)}), bf16[8192,256]{1,0:T(8,128)(2,1)}) %all-gather.9.cloned.1.call-update) | async-done | bytes 4194320 | tf_op jit(solution)/shard_map/all_gather | solution.py:415
  219.7 12.4 %multiply_reduce_fusion = (f32[1024]{0:T(1024)S(1)}, f32[1024,2048]{1,0:T(8,128)S(1)}) fusion(bf16[1024,2048]{1,0:T(8,128)(2,1)S(1)} %shard_map.208, bf16[2048,2048]{1,0:T(8,128)(2,1)S(1)} %copy-done.1, bf16[1,1024,2048]{2,1,0:T(8,128)(2,1)} %all-gather.15.cloned.1.call-done), kind=kOutput, calls=%fused_computation.17 | convolution fusion | flops 8598322176 | bytes 25169920 | tf_op jit(solution)/shard_map/dot_general | solution.py:65
  246.5 8.8 %fusion.100 = f32[1024,2048]{1,0:T(8,128)S(1)} fusion(bf16[1024,2048]{1,0:T(8,128)(2,1)S(1)} %copy-done.30, bf16[2048,2048]{1,0:T(8,128)(2,1)S(1)} %shard_map.209), kind=kOutput, calls=%fused_computation.203 | convolution fusion | flops 8589934592 | bytes 20971520 | tf_op jit(solution)/shard_map/dot_general | solution.py:65
  266.7 8.0 %fusion.101 = f32[1024,1024]{1,0:T(8,128)S(1)} fusion(bf16[1024,2048]{1,0:T(8,128)(2,1)} %all-gather.11.cloned.1.call-done, bf16[1024,2048]{1,0:T(8,128)(2,1)} %copy-done.7), kind=kOutput, calls=%fused_computation.204 | convolution fusion | flops 4294967296 | bytes 12582912 | tf_op jit(solution)/shard_map/dot_general | solution.py:73
  279.9 12.6 %convolution_convert_fusion = bf16[1024,2048]{1,0:T(8,128)(2,1)} fusion(bf16[1024,2048]{1,0:T(8,128)(2,1)S(1)} %pad_maximum_fusion, bf16[2048,2048]{1,0:T(8,128)(2,1)} %copy-done.2), kind=kOutput, calls=%fused_computation.50 | convolution fusion | flops 8592031744 | bytes 16777216 | tf_op jit(solution)/shard_map/dot_general | solution.py:73
  292.6 12.5 %fusion.103 = f32[2048,2048]{1,0:T(8,128)S(1)} fusion(bf16[1024,2048]{1,0:T(8,128)(2,1)} %multiply_convert_fusion.2, bf16[1024,2048]{1,0:T(8,128)(2,1)} %copy-done.35), kind=kOutput, calls=%fused_computation.206 | convolution fusion | flops 8589934592 | bytes 25165824 | tf_op jit(solution)/shard_map/dot_general | solution.py:69
  314.4 7.4 %collective-permute-done.14 = bf16[1024,2048]{1,0:T(8,128)(2,1)} collective-permute-done((bf16[1024,2048]{1,0:T(8,128)(2,1)}, bf16[1024,2048]{1,0:T(8,128)(2,1)}, u32[]{:S(2)}, u32[]{:S(2)}) %collective-permute-start.14) | collective-permute-done | bytes 4194336 | tf_op jit(solution)/shard_map/ppermute | solution.py:455
  328.6 9.0 %fusion.102 = f32[1024,2048]{1,0:T(8,128)} fusion(bf16[1024,1024]{1,0:T(8,128)(2,1)S(1)} %multiply_convert_fusion.5, bf16[1024,2048]{1,0:T(8,128)(2,1)} %all-gather.11.cloned.1.call-done), kind=kOutput, calls=%fused_computation.205 | convolution fusion | flops 4294967296 | bytes 14680064 | tf_op jit(solution)/shard_map/dot_general | solution.py:69
  339.8 26.1 %reduce-scatter.4.cloned.1.call-done = bf16[128,2048]{1,0:T(8,128)(2,1)} async-done(((bf16[1024,2048]{1,0:T(8,128)(2,1)}), bf16[128,2048]{1,0:T(8,128)(2,1)}) %reduce-scatter.4.cloned.1.call-update) | async-done | bytes 524304 | tf_op jit(solution)/shard_map/reduce_scatter | solution.py:419
  367.1 8.0 %collective-permute-done.15 = bf16[512,2048]{1,0:T(8,128)(2,1)} collective-permute-done((bf16[512,2048]{1,0:T(8,128)(2,1)}, bf16[512,2048]{1,0:T(8,128)(2,1)}, u32[]{:S(2)}, u32[]{:S(2)}) %collective-permute-start.15) | collective-permute-done | bytes 2097184 | tf_op jit(solution)/shard_map/ppermute | solution.py:275
  378.3 6.5 %convolution_convert_fusion.2.refs_0_ = bf16[128,2048]{1,0:T(8,128)(2,1)S(1)} fusion(bf16[128,2048]{1,0:T(8,128)(2,1)S(1)} %fusion.88, bf16[2048,2048]{1,0:T(8,128)(2,1)} %copy-done), kind=kOutput, calls=%fused_computation.56 | convolution fusion | flops 1074003968 | bytes 9437184 | tf_op jit(solution)/shard_map/dot_general | solution.py:73
  399.3 13.2 %all-to-all-done.2 = bf16[8,128,256]{2,1,0:T(8,128)(2,1)} async-done(((bf16[8,128,256]{2,1,0:T(8,128)(2,1)}), bf16[8,128,256]{2,1,0:T(8,128)(2,1)}, u32[]{:S(2)}, u32[]{:S(2)}) %all-to-all-start.2) | async-done | bytes 524320 | tf_op jit(solution)/shard_map/all_to_all | solution.py:620
  454.5 10.1 %fusion.89 = (bf16[1024,2048]{1,0:T(8,128)(2,1)}, f32[2048]{0:T(1024)S(1)}) fusion(f32[1024]{0:T(1024)S(1)} %copy-done.59, bf16[1,1024,2048]{2,1,0:T(8,128)(2,1)} %all-gather.15.cloned.1.call-done, bf16[1024,768]{0,1:T(8,128)(2,1)} %pad_maximum_fusion.4, bf16[2048,896]{1,0:T(8,128)(2,1)} %copy-done.4), kind=kOutput, calls=%fused_computation.192 | convolution fusion | flops 3231709184 | bytes 13119488 | tf_op jit(solution)/shard_map/dot_general | solution.py:73
  495.9 24.3 %all-to-all-done.4.ref = bf16[8,64,1024]{2,1,0:T(8,128)(2,1)S(1)} async-done(((bf16[8,64,1024]{2,1,0:T(8,128)(2,1)}), bf16[8,64,1024]{2,1,0:T(8,128)(2,1)S(1)}, u32[]{:S(2)}, u32[]{:S(2)}) %all-to-all-start.4) | async-done | bytes 1048608 | tf_op jit(solution)/shard_map/all_to_all | solution.py:627
  545.4 12.2 %all-to-all-done.5.ref = bf16[8,64,896]{2,1,0:T(8,128)(2,1)S(1)} async-done(((bf16[8,64,896]{2,1,0:T(8,128)(2,1)}), bf16[8,64,896]{2,1,0:T(8,128)(2,1)S(1)}, u32[]{:S(2)}, u32[]{:S(2)}) %all-to-all-start.5) | async-done | bytes 917536 | tf_op jit(solution)/shard_map/all_to_all | solution.py:477
  (326 shorter events, 255.1 us)
Async XLA Ops:
  7.2 86.9 %all-gather.15.cloned.1.call-start = ((), (), s32[]{:S(2)}) async-start(), calls=%async_computation.16 | async-start | bytes 4718592 | tf_op jit(solution)/shard_map/all_gather | solution.py:415
  14.8 40.5 %all-to-all-start = ((bf16[8,64,896]{2,1,0:T(8,128)(2,1)}), bf16[8,64,896]{2,1,0:T(8,128)(2,1)S(1)}, u32[]{:S(2)}, u32[]{:S(2)}) async-start(bf16[8,64,896]{2,1,0:T(8,128)(2,1)} %shard_map.203), calls=%async_computation | async-start | bytes 1835008 | tf_op jit(solution)/shard_map/all_to_all | solution.py:526
  22.1 32.1 %collective-permute-start.1 = (bf16[256,2048]{1,0:T(8,128)(2,1)S(1)}, bf16[256,2048]{1,0:T(8,128)(2,1)S(1)}, u32[]{:S(2)}, u32[]{:S(2)}) collective-permute-start(bf16[256,2048]{1,0:T(8,128)(2,1)S(1)} %copy-done.10), channel_id=1, source_target_pairs={{0,16},{8,24},{16,0},{24,8},{1,17},{9,25},{17,1},{25,9},{2,18},{10... | collective-permute-start | bytes 3145736 | tf_op jit(solution)/shard_map/ppermute | solution.py:275
  23.6 28.7 %collective-permute-start = (bf16[64,2048]{1,0:T(8,128)(2,1)}, bf16[64,2048]{1,0:T(8,128)(2,1)S(1)}, u32[]{:S(2)}, u32[]{:S(2)}) collective-permute-start(bf16[64,2048]{1,0:T(8,128)(2,1)} %param.18), channel_id=1, source_target_pairs={{0,16},{8,24},{16,0},{24,8},{1,17},{9,25},{17,1},{25,9},{2,18},{10... | collective-permute-start | bytes 786440 | tf_op jit(solution)/shard_map/ppermute | solution.py:275
  60.8 65.4 %all-to-all-start.1 = ((bf16[8,64,2048]{2,1,0:T(8,128)(2,1)}), bf16[8,64,2048]{2,1,0:T(8,128)(2,1)}, u32[]{:S(2)}, u32[]{:S(2)}) async-start(bf16[8,64,2048]{2,1,0:T(8,128)(2,1)} %shard_map.205), calls=%async_computation.1 | async-start | bytes 4194304 | tf_op jit(solution)/shard_map/all_to_all | solution.py:534
  65.4 99.6 %all-gather.7.cloned.1.call-start = ((), (), s32[]{:S(2)}) async-start(), calls=%async_computation.9 | async-start | bytes 4718592 | tf_op jit(solution)/shard_map/all_gather | solution.py:415
  75.4 138.7 %all-gather.9.cloned.1.call-start = ((), (), s32[]{:S(2)}) async-start(), calls=%async_computation.10 | async-start | bytes 4718592 | tf_op jit(solution)/shard_map/all_gather | solution.py:415
  128.0 30.3 %collective-permute-start.5 = (bf16[256,2048]{1,0:T(8,128)(2,1)S(1)}, bf16[256,2048]{1,0:T(8,128)(2,1)}, u32[]{:S(2)}, u32[]{:S(2)}) collective-permute-start(bf16[256,2048]{1,0:T(8,128)(2,1)S(1)} %get-tuple-element.64.refs_0_), channel_id=1, source_target_pairs={{0,16},{8,24},{16,0},{24,8},{1,17},{9,25},{17,1},{25,9},{2,18},{10... | collective-permute-start | bytes 3145736 | tf_op jit(solution)/shard_map/ppermute | solution.py:275
  165.0 101.6 %all-gather.11.cloned.1.call-start = ((), (), s32[]{:S(2)}) async-start(), calls=%async_computation.11 | async-start | bytes 4718592 | tf_op jit(solution)/shard_map/all_gather | solution.py:415
  179.7 57.2 %collective-permute-start.10 = (bf16[256,2048]{1,0:T(8,128)(2,1)S(1)}, bf16[256,2048]{1,0:T(8,128)(2,1)S(1)}, u32[]{:S(2)}, u32[]{:S(2)}) collective-permute-start(bf16[256,2048]{1,0:T(8,128)(2,1)S(1)} %get-tuple-element.64.refs_0_), channel_id=1, source_target_pairs={{0,8},{8,0},{16,24},{24,16},{1,9},{9,1},{17,25},{25,17},{2,10},{10... | collective-permute-start | bytes 3145736 | tf_op jit(solution)/shard_map/ppermute | solution.py:455
  179.9 57.0 %collective-permute-start.12 = (bf16[256,2048]{1,0:T(8,128)(2,1)S(1)}, bf16[256,2048]{1,0:T(8,128)(2,1)}, u32[]{:S(2)}, u32[]{:S(2)}) collective-permute-start(bf16[256,2048]{1,0:T(8,128)(2,1)S(1)} %get-tuple-element.73.refs_4_), channel_id=1, source_target_pairs={{0,8},{8,0},{16,24},{24,16},{1,9},{9,1},{17,25},{25,17},{2,10},{10... | collective-permute-start | bytes 3145736 | tf_op jit(solution)/shard_map/ppermute | solution.py:455
  180.2 56.6 %collective-permute-start.9 = (bf16[256,2048]{1,0:T(8,128)(2,1)S(1)}, bf16[256,2048]{1,0:T(8,128)(2,1)}, u32[]{:S(2)}, u32[]{:S(2)}) collective-permute-start(bf16[256,2048]{1,0:T(8,128)(2,1)S(1)} %get-tuple-element.73.refs_4_), channel_id=1, source_target_pairs={{0,16},{8,24},{16,0},{24,8},{1,17},{9,25},{17,1},{25,9},{2,18},{10... | collective-permute-start | bytes 3145736 | tf_op jit(solution)/shard_map/ppermute | solution.py:275
  181.7 55.2 %collective-permute-start.11 = (bf16[256,2048]{1,0:T(8,128)(2,1)}, bf16[256,2048]{1,0:T(8,128)(2,1)}, u32[]{:S(2)}, u32[]{:S(2)}) collective-permute-start(bf16[256,2048]{1,0:T(8,128)(2,1)} %collective-permute-done.5.refs_2_), channel_id=1, source_target_pairs={{0,8},{8,0},{16,24},{24,16},{1,9},{9,1},{17,25},{25,17},{2,10},{10... | collective-permute-start | bytes 3145736 | tf_op jit(solution)/shard_map/ppermute | solution.py:455
  214.1 123.5 %reduce-scatter.6.cloned.1.call-start = ((), (), s32[]{:S(2)}) async-start(), calls=%async_computation.13 | async-start | bytes 4718592 | tf_op jit(solution)/shard_map/reduce_scatter | solution.py:419
  266.7 99.3 %reduce-scatter.4.cloned.1.call-start = ((), (), s32[]{:S(2)}) async-start(), calls=%async_computation.12 | async-start | bytes 4718592 | tf_op jit(solution)/shard_map/reduce_scatter | solution.py:419
  292.6 190.2 %all-gather.13.cloned.1.call-start = ((), (), s32[]{:S(2)}) async-start(), calls=%async_computation.14 | async-start | bytes 4718592 | tf_op jit(solution)/shard_map/all_gather | solution.py:415
  327.1 48.0 %collective-permute-start.15 = (bf16[512,2048]{1,0:T(8,128)(2,1)}, bf16[512,2048]{1,0:T(8,128)(2,1)}, u32[]{:S(2)}, u32[]{:S(2)}) collective-permute-start(bf16[512,2048]{1,0:T(8,128)(2,1)} %add_convert_fusion.1), channel_id=1, source_target_pairs={{0,16},{8,24},{16,0},{24,8},{1,17},{9,25},{17,1},{25,9},{2,18},{10... | collective-permute-start | bytes 6291464 | tf_op jit(solution)/shard_map/ppermute | solution.py:275
  394.7 40.1 %collective-permute-start.17 = (bf16[512,2048]{1,0:T(8,128)(2,1)}, bf16[512,2048]{1,0:T(8,128)(2,1)}, u32[]{:S(2)}, u32[]{:S(2)}) collective-permute-start(bf16[512,2048]{1,0:T(8,128)(2,1)} %pad_maximum_fusion.2), channel_id=1, source_target_pairs={{0,8},{8,0},{16,24},{24,16},{1,9},{9,1},{17,25},{25,17},{2,10},{10... | collective-permute-start | bytes 6291464 | tf_op jit(solution)/shard_map/ppermute | solution.py:455
  414.0 40.5 %all-to-all-start.3 = ((bf16[8,64,1024]{2,1,0:T(8,128)(2,1)}), bf16[8,64,1024]{2,1,0:T(8,128)(2,1)S(1)}, u32[]{:S(2)}, u32[]{:S(2)}) async-start(bf16[8,64,1024]{2,1,0:T(8,128)(2,1)} %bitcast.147), calls=%async_computation.5 | async-start | bytes 2097152 | tf_op jit(solution)/shard_map/all_to_all | solution.py:627
  417.6 142.1 %reduce-scatter.8.cloned.1.call-start = ((), (), s32[]{:S(2)}) async-start(), calls=%async_computation.15 | async-start | bytes 4718592 | tf_op jit(solution)/shard_map/reduce_scatter | solution.py:419
  477.7 42.5 %all-to-all-start.4 = ((bf16[8,64,1024]{2,1,0:T(8,128)(2,1)}), bf16[8,64,1024]{2,1,0:T(8,128)(2,1)S(1)}, u32[]{:S(2)}, u32[]{:S(2)}) async-start(bf16[8,64,1024]{2,1,0:T(8,128)(2,1)} %bitcast.146), calls=%async_computation.6 | async-start | bytes 2097152 | tf_op jit(solution)/shard_map/all_to_all | solution.py:627
  492.0 28.2 %collective-permute-start.19 = (bf16[512,896]{0,1:T(8,128)(2,1)}, bf16[512,896]{0,1:T(8,128)(2,1)}, u32[]{:S(2)}, u32[]{:S(2)}) collective-permute-start(bf16[512,896]{0,1:T(8,128)(2,1)} %fusion.33), channel_id=1, source_target_pairs={{0,16},{8,24},{16,0},{24,8},{1,17},{9,25},{17,1},{25,9},{2,18},{10... | collective-permute-start | bytes 2752520 | tf_op jit(solution)/shard_map/ppermute | solution.py:275
  493.5 44.5 %collective-permute-start.21 = (bf16[256,2048]{1,0:T(8,128)(2,1)}, bf16[256,2048]{1,0:T(8,128)(2,1)}, u32[]{:S(2)}, u32[]{:S(2)}) collective-permute-start(bf16[256,2048]{1,0:T(8,128)(2,1)} %add_convert_fusion.2), channel_id=1, source_target_pairs={{0,16},{8,24},{16,0},{24,8},{1,17},{9,25},{17,1},{25,9},{2,18},{10... | collective-permute-start | bytes 3145736 | tf_op jit(solution)/shard_map/ppermute | solution.py:275
  525.7 32.0 %all-to-all-start.5 = ((bf16[8,64,896]{2,1,0:T(8,128)(2,1)}), bf16[8,64,896]{2,1,0:T(8,128)(2,1)S(1)}, u32[]{:S(2)}, u32[]{:S(2)}) async-start(bf16[8,64,896]{2,1,0:T(8,128)(2,1)} %bitcast.150), calls=%async_computation.8 | async-start | bytes 1835008 | tf_op jit(solution)/shard_map/all_to_all | solution.py:477
  (76 other events, 646.8 us)
Sparse Core Ops, SparseCore 0:
  9.6 84.5 all-gather.14
  96.2 68.7 all-gather.6
  167.1 46.9 all-gather.8
  215.5 47.8 all-gather.10
  266.8 48.4 reduce-scatter.5
  317.4 48.4 reduce-scatter.3
  384.9 79.4 all-gather.12
  466.7 77.4 reduce-scatter.7
